TPU v7x, 32 devices: a whole 2x2x4 slice. The times are simulated.
32 devices in a mesh: seq: 8 (over z, x), head: 4 (over y, core).
Axes of the slice: x: 2, y: 2, z: 4, core: 2. Of those that a mesh axis runs over, the one named last changes fastest.
Arguments:
- queries: bfloat16 [8192, 4096], P(('seq', 'head'))
- keys: bfloat16 [8192, 2048], P(('seq', 'head'))
- values: bfloat16 [8192, 2048], P(('seq', 'head')), may hold values from -6 to 6
- dout: bfloat16 [8192, 4096], P(('seq', 'head')), may hold values from -6 to 6
- doc_starts: int32 [8], replicated, may hold values from 0 to 8191, as said below
Outputs:
- dquery: bfloat16 [8192, 4096], P(('seq', 'head'))
- dkey: bfloat16 [8192, 2048], P(('seq', 'head'))
- dvalue: bfloat16 [8192, 2048], P(('seq', 'head'))
Inputs may be any that keep to these rules, and one draw needn't show every extreme that they name: doc_starts[0] = 0, strictly increasing.
All inputs are finite; a program needn't handle non-finite values.
Results may differ from a plain program's by a relative error of at most 0.03.
Values may be sent and summed in bfloat16 or wider, within the bound.
No kernel may reach another device: no remote copies, remote signals or barrier semaphores. Data moves between devices by JAX's collectives and lax.ppermute only.
A program may use at most 128 MiB of HBM per device.

v0:
```python
import jax
import jax.numpy as jnp
from jax import lax
from jax.sharding import PartitionSpec as P

HEAD_SIZE = 128
WINDOW_LENGTH = 512


scale_factor = 168.0 ** (-0.5)
negative = -1e30


def passed_along(x, axis, by):
    length = lax.axis_size(axis)
    pairs = [(i, i + by) for i in range(length) if 0 <= i + by < length]
    return lax.ppermute(x, axis, pairs)


def doc_ids(positions, doc_starts):
    return jnp.sum((doc_starts[None, :] <= positions[:, None]).astype(jnp.int32), axis=1) - 1


def allowed_pairs(query_pos, key_pos, doc_starts, limit, window):
    query_doc = doc_ids(query_pos, doc_starts)
    key_doc = doc_ids(key_pos, doc_starts)
    return (
        (key_pos[None, :] >= 0)
        & (key_pos[None, :] <= query_pos[:, None])
        & (query_pos[:, None] - key_pos[None, :] < window)
        & (query_doc[:, None] == key_doc[None, :])
        & (query_pos[:, None] < limit)
    )


def dot_rows(left, right):
    return lax.dot_general(
        left, right, (((1,), (1,)), ((), ())), preferred_element_type=jnp.float32
    )


def dot_cols(left, right):
    return lax.dot_general(
        left, right, (((0,), (0,)), ((), ())), preferred_element_type=jnp.float32
    )


def head_tile(q_blk, g_blk, key_win, value_win, allowed):
    masked = jnp.where(allowed, dot_rows(q_blk, key_win) * scale_factor, negative)
    peak = jnp.max(masked, axis=1, keepdims=True)
    total = jnp.sum(jnp.exp(masked - peak), axis=1, keepdims=True)
    log_sum = peak + jnp.log(total)
    probs = jnp.exp(masked - log_sum)
    probs_low = probs.astype(jnp.bfloat16)
    output = jnp.dot(probs_low, value_win, preferred_element_type=jnp.float32).astype(jnp.bfloat16)
    output = lax.optimization_barrier(output)
    delta = jnp.sum(g_blk.astype(jnp.float32) * output.astype(jnp.float32), axis=1, keepdims=True)
    dprobs = dot_rows(g_blk, value_win)
    dscores = (probs * (dprobs - delta) * scale_factor).astype(jnp.bfloat16)
    dq_blk = jnp.dot(dscores, key_win, preferred_element_type=jnp.float32)
    return (dq_blk, dscores, probs_low, log_sum, delta)


def shards(queries, keys, values, dout, doc_starts):
    q_local, k_local, v_local, g_local = (
        lax.all_to_all(queries, "head", split_axis=1, concat_axis=0, tiled=True),
        lax.all_to_all(keys, "head", split_axis=1, concat_axis=0, tiled=True),
        lax.all_to_all(values, "head", split_axis=1, concat_axis=0, tiled=True),
        lax.all_to_all(dout, "head", split_axis=1, concat_axis=0, tiled=True),
    )
    rows = q_local.shape[0]
    width = k_local.shape[1]
    kv_heads = width // HEAD_SIZE
    query_group = q_local.shape[1] // width
    span = WINDOW_LENGTH
    blocks = rows // span
    halo_keys, halo_values = passed_along(
        (k_local[rows - span :], v_local[rows - span :]), "seq", 1
    )
    extended_keys = jnp.concatenate([halo_keys, k_local], axis=0)
    extended_values = jnp.concatenate([halo_values, v_local], axis=0)
    base = lax.axis_index("seq") * rows
    limit = lax.axis_size("seq") * rows
    spread = jnp.arange(span, dtype=jnp.int32)
    double = jnp.arange(2 * span, dtype=jnp.int32)
    skipped = 0
    key_grad = jnp.zeros((rows + span, width), jnp.float32)
    value_grad = jnp.zeros((rows + span, width), jnp.float32)
    dq_rows = []
    first_lse = []
    first_delta = []
    for blk in range(blocks):
        lower = skipped if blk == 0 else 0
        allowed = allowed_pairs(
            base + blk * span + spread, base + (blk - 1) * span + double, doc_starts, limit, span
        )
        row_parts = []
        for head in range(kv_heads):
            key_win = extended_keys[
                blk * span : (blk + 2) * span, head * HEAD_SIZE : (head + 1) * HEAD_SIZE
            ]
            value_win = extended_values[
                blk * span : (blk + 2) * span, head * HEAD_SIZE : (head + 1) * HEAD_SIZE
            ]
            key_sum = jnp.zeros((2 * span - lower, HEAD_SIZE), jnp.float32)
            value_sum = jnp.zeros((2 * span - lower, HEAD_SIZE), jnp.float32)
            for member in range(query_group):
                column = (head * query_group + member) * HEAD_SIZE
                q_blk = q_local[blk * span : (blk + 1) * span, column : column + HEAD_SIZE]
                g_blk = g_local[blk * span : (blk + 1) * span, column : column + HEAD_SIZE]
                dq_blk, dscores, probs_low, log_sum, delta = head_tile(
                    q_blk, g_blk, key_win, value_win, allowed
                )
                row_parts.append(dq_blk.astype(jnp.bfloat16))
                if blk == 0:
                    first_lse.append(log_sum[:, 0])
                    first_delta.append(delta[:, 0])
                key_sum = key_sum + dot_cols(dscores, q_blk)
                value_sum = value_sum + dot_cols(probs_low, g_blk)
            key_grad = key_grad.at[
                blk * span + lower : (blk + 2) * span, head * HEAD_SIZE : (head + 1) * HEAD_SIZE
            ].add(key_sum)
            value_grad = value_grad.at[
                blk * span + lower : (blk + 2) * span, head * HEAD_SIZE : (head + 1) * HEAD_SIZE
            ].add(value_sum)
        dq_rows.append(jnp.concatenate(row_parts, axis=1))
    dquery_local = jnp.concatenate(dq_rows, axis=0)
    back_keys, back_values = passed_along((key_grad[:span], value_grad[:span]), "seq", -1)
    dkey_local = jnp.concatenate([key_grad[span:rows], key_grad[rows:] + back_keys], axis=0).astype(
        jnp.bfloat16
    )
    dvalue_local = jnp.concatenate(
        [value_grad[span:rows], value_grad[rows:] + back_values], axis=0
    ).astype(jnp.bfloat16)
    dquery, dkey, dvalue = (
        lax.all_to_all(dquery_local, "head", split_axis=0, concat_axis=1, tiled=True),
        lax.all_to_all(dkey_local, "head", split_axis=0, concat_axis=1, tiled=True),
        lax.all_to_all(dvalue_local, "head", split_axis=0, concat_axis=1, tiled=True),
    )
    return (dquery, dkey, dvalue)


def solution(mesh):
    return jax.shard_map(
        shards,
        mesh=mesh,
        in_specs=(
            P(("seq", "head"), None),
            P(("seq", "head"), None),
            P(("seq", "head"), None),
            P(("seq", "head"), None),
            P(),
        ),
        out_specs=(P(("seq", "head"), None), P(("seq", "head"), None), P(("seq", "head"), None)),
        check_vma=False,
    )
```

profile of v0, /device:TPU:26, one launch (start us, length us, event | category | flops | bytes accessed | tf_op | source)
XLA Modules:
  0.0 368.3 jit_solution(4483929283789763976)
XLA Ops:
  0.6 2.4 copy.105
  3.1 3.5 all-to-all-start
  6.6 2.5 copy.108
  9.1 2.3 copy.110
  11.4 9.6 %all-to-all-done = bf16[256,4,512]{0,2,1:T(8,128)(2,1)S(1)} async-done(((bf16[256,4,512]{0,2,1:T(8,128)(2,1)}), bf16[256,4,512]{0,2,1:T(8,128)(2,1)S(1)}, u32[]{:S(2)}, u32[]{:S(2)}) %all-to-all-start) | async-done | bytes 1048608 | tf_op jit(solution)/shard_map/all_to_all | solution.py:67
  21.0 3.5 all-to-all-start.2
  26.6 12.4 %all-to-all-done.2 = bf16[256,4,512]{0,2,1:T(8,128)(2,1)S(1)} async-done(((bf16[256,4,512]{0,2,1:T(8,128)(2,1)}), bf16[256,4,512]{0,2,1:T(8,128)(2,1)S(1)}, u32[]{:S(2)}, u32[]{:S(2)}) %all-to-all-start.2) | async-done | bytes 1048608 | tf_op jit(solution)/shard_map/all_to_all | solution.py:68
  39.9 3.6 all-to-all-start.1
  49.6 2.1 copy.111
  53.0 3.2 copy.157
  59.7 3.7 collective-permute-done
  63.4 2.3 pad_maximum_fusion.6
  65.7 8.5 %collective-permute-done.1 = bf16[512,512]{1,0:T(8,128)(2,1)} collective-permute-done((bf16[512,512]{1,0:T(8,128)(2,1)}, bf16[512,512]{1,0:T(8,128)(2,1)}, u32[]{:S(2)}, u32[]{:S(2)}) %collective-permute-start.1) | collective-permute-done | bytes 524320 | tf_op jit(solution)/shard_map/ppermute | solution.py:17
  77.5 3.8 %all-to-all-start.3 = ((bf16[256,4,1024]{2,0,1:T(8,128)(2,1)}), bf16[256,4,1024]{2,0,1:T(8,128)(2,1)S(1)}, u32[]{:S(2)}, u32[]{:S(2)}) async-start(bf16[256,4,1024]{2,0,1:T(8,128)(2,1)} %bitcast.218), calls=%async_computation.3 | async-start | bytes 4194304 | tf_op jit(solution)/shard_map/all_to_all | solution.py:69
  81.3 4.0 %copy.109 = bf16[4,256,1024]{2,1,0:T(8,128)(2,1)} copy(bf16[4,256,1024]{1,2,0:T(8,128)(2,1)} %bitcast.219) | data formatting | bytes 4194304 | tf_op jit(solution)/shard_map/all_to_all | solution.py:66
  85.3 4.2 %fusion.232 = (f32[512]{0:T(512)}, f32[512,1024]{0,1:T(8,128)}) fusion(bf16[1024,128]{1,0:T(8,128)(2,1)} %get-tuple-element.226, bf16[1024,1024]{1,0:T(8,128)(2,1)} %bitcast.222, pred[512]{0:T(512)(128)(4,1)S(1)} %broadcast_compare_fusion.3, s32[1024]{0:T(1024)S(1)} %broadcast_add_fusion.1, s32[512]{0:T(512)S(1)} %broadcast_add_fusion.3, ...), kind=kOutput, calls=%fused_computation.387 | convolution fusion | flops 139984384 | bytes 2506240 | tf_op jit(solution)/shard_map/dot_general | solution.py:37
  89.6 3.4 fusion.233
  93.0 3.3 fusion.234
  96.3 3.3 fusion.235
  99.7 3.4 fusion.236
  103.0 2.8 fusion.237
  105.8 3.3 fusion.238
  109.2 2.8 fusion.231
  113.1 2.9 fusion.241
  116.0 2.8 fusion.242
  120.3 3.3 fusion.243
  123.7 3.4 fusion.244
  127.0 3.3 fusion.245
  130.4 3.3 fusion.246
  133.7 3.6 fusion.240
  137.2 3.0 fusion.101
  164.5 2.3 fusion.193
  168.3 2.1 fusion.173
  174.9 3.1 fusion.53
  178.0 6.0 %scatter-add.69 = f32[1536,512]{1,0:T(8,128)} dynamic-update-slice(f32[1536,512]{1,0:T(8,128)} %scatter-add.66, f32[1024,128]{1,0:T(8,128)} %fusion.53, s32[]{:T(128)} %bitcast.32, s32[]{:T(128)} %bitcast.33) | dynamic-update-slice | bytes 1048580 | tf_op jit(solution)/shard_map/scatter-add | solution.py:125
  184.0 5.4 %fusion.55 = f32[1024,128]{1,0:T(8,128)} fusion(f32[1024,128]{1,0:T(8,128)} %fusion.111, f32[1536,512]{1,0:T(8,128)} %scatter-add.69, s32[]{:T(128)} %bitcast.34, s32[]{:T(128)} %bitcast.35, f32[512,1024]{0,1:T(8,128)} %get-tuple-element.251, f32[512]{0:T(512)S(1)} %log_add_fusion.10, pred[]{:T(512)} %get-tuple-element.218, ...), kind=kOutput, calls=%fused_computation.140 | convolution fusion | flops 135659520 | bytes 3803145 | tf_op jit(solution)/shard_map/dot_general | solution.py:43
  189.4 6.4 %scatter-add.70 = f32[1536,512]{1,0:T(8,128)} dynamic-update-slice(f32[1536,512]{1,0:T(8,128)} %scatter-add.69, f32[1024,128]{1,0:T(8,128)} %fusion.55, s32[]{:T(128)} %bitcast.34, s32[]{:T(128)} %bitcast.35) | dynamic-update-slice | bytes 1048580 | tf_op jit(solution)/shard_map/scatter-add | solution.py:125
  195.8 5.0 %fusion.57 = f32[1024,128]{1,0:T(8,128)} fusion(f32[1024,128]{1,0:T(8,128)} %fusion.106, f32[1536,512]{1,0:T(8,128)} %scatter-add.70, s32[]{:T(128)} %bitcast.36, s32[]{:T(128)} %bitcast.37, f32[512,1024]{0,1:T(8,128)} %get-tuple-element.239, f32[512]{0:T(512)S(1)} %log_add_fusion.8, pred[]{:T(512)} %get-tuple-element.217, bf16[1024,1024]{1,0:T(8,128)(2,1)S(1)} %bitcast.198), kind=kOutput, calls=%fused_computation.142 | convolution fusion | flops 135659520 | bytes 3803145 | tf_op jit(solution)/shard_map/dot_general | solution.py:43
  200.8 5.7 %scatter-add.71 = f32[1536,512]{1,0:T(8,128)} dynamic-update-slice(f32[1536,512]{1,0:T(8,128)} %scatter-add.70, f32[1024,128]{1,0:T(8,128)} %fusion.57, s32[]{:T(128)} %bitcast.36, s32[]{:T(128)} %bitcast.37) | dynamic-update-slice | bytes 1048580 | tf_op jit(solution)/shard_map/scatter-add | solution.py:125
  206.5 2.1 exponential_reduce_fusion.6
  221.0 4.6 %collective-permute-start.3 = (f32[512,512]{1,0:T(8,128)}, f32[512,512]{1,0:T(8,128)}, u32[]{:S(2)}, u32[]{:S(2)}) collective-permute-start(f32[512,512]{1,0:T(8,128)} %slice.673), channel_id=1, source_target_pairs={{4,0},{8,4},{12,8},{16,12},{20,16},{24,20},{28,24},{5,1},{9,5},{13... | collective-permute-start | bytes 3145736 | tf_op jit(solution)/shard_map/ppermute | solution.py:17
  226.9 2.1 fusion.188
  231.5 2.1 scatter-add.54
  234.2 2.4 fusion.183
  238.3 4.0 %fusion.39 = f32[1024,128]{1,0:T(8,128)} fusion(f32[1024,128]{1,0:T(8,128)S(1)} %fusion.188, bf16[512,1024]{0,1:T(8,128)(2,1)S(1)} %fusion.9, s32[]{:T(128)} %bitcast.32, s32[]{:T(128)} %bitcast.33, f32[1024,128]{1,0:T(8,128)S(1)} %convolution_add_fusion.15, pred[]{:T(512)} %get-tuple-element.219, bf16[1024,1024]{1,0:T(8,128)(2,1)} %bitcast.228), kind=kOutput, calls=%fused_computation.124 | convolution fusion | flops 134610944 | bytes 2754048 | tf_op jit(solution)/shard_map/dot_general | solution.py:43
  242.2 6.3 %scatter-add.55 = f32[1536,512]{1,0:T(8,128)} dynamic-update-slice(f32[1536,512]{1,0:T(8,128)} %scatter-add.54, f32[1024,128]{1,0:T(8,128)} %fusion.39, s32[]{:T(128)} %bitcast.32, s32[]{:T(128)} %bitcast.33) | dynamic-update-slice | bytes 1048580 | tf_op jit(solution)/shard_map/scatter-add | solution.py:122
  248.5 5.1 %fusion.41 = f32[1024,128]{1,0:T(8,128)} fusion(f32[1024,128]{1,0:T(8,128)} %fusion.183, bf16[512,1024]{0,1:T(8,128)(2,1)} %fusion.5, f32[1536,512]{1,0:T(8,128)} %scatter-add.55, s32[]{:T(128)} %bitcast.34, s32[]{:T(128)} %bitcast.35, pred[]{:T(512)} %get-tuple-element.218, bf16[1024,1024]{1,0:T(8,128)(2,1)} %bitcast.229), kind=kOutput, calls=%fused_computation.126 | convolution fusion | flops 134610944 | bytes 2754048 | tf_op jit(solution)/shard_map/dot_general | solution.py:43
  253.6 6.4 %scatter-add.56 = f32[1536,512]{1,0:T(8,128)} dynamic-update-slice(f32[1536,512]{1,0:T(8,128)} %scatter-add.55, f32[1024,128]{1,0:T(8,128)} %fusion.41, s32[]{:T(128)} %bitcast.34, s32[]{:T(128)} %bitcast.35) | dynamic-update-slice | bytes 1048580 | tf_op jit(solution)/shard_map/scatter-add | solution.py:122
  260.0 2.3 fusion.3
  265.4 4.2 %fusion.43 = f32[1024,128]{1,0:T(8,128)} fusion(f32[1024,128]{1,0:T(8,128)S(1)} %fusion.178, bf16[512,1024]{0,1:T(8,128)(2,1)S(1)} %fusion.1, f32[1536,512]{1,0:T(8,128)} %scatter-add.56, s32[]{:T(128)} %bitcast.36, s32[]{:T(128)} %bitcast.37, pred[]{:T(512)} %get-tuple-element.217, bf16[1024,1024]{1,0:T(8,128)(2,1)} %bitcast.231), kind=kOutput, calls=%fused_computation.128 | convolution fusion | flops 134610944 | bytes 2754048 | tf_op jit(solution)/shard_map/dot_general | solution.py:43
  269.7 5.5 %scatter-add.59 = f32[1536,512]{1,0:T(8,128)} dynamic-update-slice(f32[1536,512]{1,0:T(8,128)} %scatter-add.56, f32[1024,128]{1,0:T(8,128)} %fusion.43, s32[]{:T(128)} %bitcast.36, s32[]{:T(128)} %bitcast.37) | dynamic-update-slice | bytes 1048580 | tf_op jit(solution)/shard_map/scatter-add | solution.py:122
  276.8 2.3 multiply_convert_fusion.6
  279.8 2.6 fusion.168
  284.6 2.2 fusion.163
  299.5 5.0 %all-to-all-start.4 = ((bf16[4,256,1024]{1,2,0:T(8,128)(2,1)}), bf16[4,256,1024]{1,2,0:T(8,128)(2,1)}, u32[]{:S(2)}, u32[]{:S(2)}) async-start(bf16[4,256,1024]{1,2,0:T(8,128)(2,1)} %bitcast.220), calls=%async_computation.4 | async-start | bytes 4194304 | tf_op jit(solution)/shard_map/all_to_all | solution.py:136
  313.5 2.4 collective-permute-start.2
  318.5 11.8 %all-to-all-done.4 = bf16[4,256,1024]{1,2,0:T(8,128)(2,1)} async-done(((bf16[4,256,1024]{1,2,0:T(8,128)(2,1)}), bf16[4,256,1024]{1,2,0:T(8,128)(2,1)}, u32[]{:S(2)}, u32[]{:S(2)}) %all-to-all-start.4) | async-done | bytes 2097184 | tf_op jit(solution)/shard_map/all_to_all | solution.py:136
  330.2 4.2 %all-to-all-start.6 = ((bf16[4,256,512]{2,1,0:T(8,128)(2,1)}), bf16[4,256,512]{2,1,0:T(8,128)(2,1)}, u32[]{:S(2)}, u32[]{:S(2)}) async-start(bf16[4,256,512]{2,1,0:T(8,128)(2,1)} %bitcast.275), calls=%async_computation.6 | async-start | bytes 2097152 | tf_op jit(solution)/shard_map/all_to_all | solution.py:138
  334.6 3.9 %collective-permute-done.2 = f32[512,512]{1,0:T(8,128)} collective-permute-done((f32[512,512]{1,0:T(8,128)}, f32[512,512]{1,0:T(8,128)}, u32[]{:S(2)}, u32[]{:S(2)}) %collective-permute-start.2) | collective-permute-done | bytes 1048608 | tf_op jit(solution)/shard_map/ppermute | solution.py:17
  340.8 8.2 %all-to-all-done.6 = bf16[4,256,512]{2,1,0:T(8,128)(2,1)} async-done(((bf16[4,256,512]{2,1,0:T(8,128)(2,1)}), bf16[4,256,512]{2,1,0:T(8,128)(2,1)}, u32[]{:S(2)}, u32[]{:S(2)}) %all-to-all-start.6) | async-done | bytes 1048608 | tf_op jit(solution)/shard_map/all_to_all | solution.py:138
  349.0 3.5 all-to-all-start.5
  352.5 4.1 %copy.133 = bf16[256,4096]{1,0:T(8,128)(2,1)} copy(bf16[256,4096]{0,1:T(8,128)(2,1)} %bitcast.31) | data formatting | bytes 4194304
  356.6 2.3 copy.153
  358.9 8.0 %all-to-all-done.5 = bf16[4,256,512]{2,1,0:T(8,128)(2,1)S(1)} async-done(((bf16[4,256,512]{2,1,0:T(8,128)(2,1)}), bf16[4,256,512]{2,1,0:T(8,128)(2,1)S(1)}, u32[]{:S(2)}, u32[]{:S(2)}) %all-to-all-start.5) | async-done | bytes 1048608 | tf_op jit(solution)/shard_map/all_to_all | solution.py:137
  (401 shorter events, 103.0 us)
Async XLA Ops:
  0.6 6.0 %copy-start.67 = (bf16[256,4096]{1,0:T(8,128)(2,1)S(1)}, bf16[256,4096]{1,0:T(8,128)(2,1)}, u32[]{:S(2)}) copy-start(bf16[256,4096]{1,0:T(8,128)(2,1)} %param.37) | copy-start | bytes 6291460
  3.1 18.0 %all-to-all-start = ((bf16[256,4,512]{0,2,1:T(8,128)(2,1)}), bf16[256,4,512]{0,2,1:T(8,128)(2,1)S(1)}, u32[]{:S(2)}, u32[]{:S(2)}) async-start(bf16[256,4,512]{0,2,1:T(8,128)(2,1)} %bitcast), calls=%async_computation | async-start | bytes 2097152 | tf_op jit(solution)/shard_map/all_to_all | solution.py:67
  9.0 17.3 %copy-start.127 = (s32[8]{0:T(128)S(1)}, s32[8]{0:T(128)}, u32[]{:S(2)}) copy-start(s32[8]{0:T(128)} %param.41) | copy-start | bytes 100
  21.0 18.0 %all-to-all-start.2 = ((bf16[256,4,512]{0,2,1:T(8,128)(2,1)}), bf16[256,4,512]{0,2,1:T(8,128)(2,1)S(1)}, u32[]{:S(2)}, u32[]{:S(2)}) async-start(bf16[256,4,512]{0,2,1:T(8,128)(2,1)} %bitcast.8), calls=%async_computation.2 | async-start | bytes 2097152 | tf_op jit(solution)/shard_map/all_to_all | solution.py:68
  39.9 36.3 %all-to-all-start.1 = ((bf16[256,4,1024]{0,2,1:T(8,128)(2,1)}), bf16[256,4,1024]{0,2,1:T(8,128)(2,1)S(1)}, u32[]{:S(2)}, u32[]{:S(2)}) async-start(bf16[256,4,1024]{0,2,1:T(8,128)(2,1)} %bitcast.4), calls=%async_computation.1 | async-start | bytes 4194304 | tf_op jit(solution)/shard_map/all_to_all | solution.py:66
  46.5 16.9 %collective-permute-start = (bf16[512,512]{1,0:T(8,128)(2,1)}, bf16[512,512]{1,0:T(8,128)(2,1)}, u32[]{:S(2)}, u32[]{:S(2)}) collective-permute-start(bf16[512,512]{1,0:T(8,128)(2,1)} %bitcast.281), channel_id=1, source_target_pairs={{0,4},{4,8},{8,12},{12,16},{16,20},{20,24},{24,28},{1,5},{5,9},{9,... | collective-permute-start | bytes 1572872 | tf_op jit(solution)/shard_map/ppermute | solution.py:17
  51.7 22.5 %collective-permute-start.1 = (bf16[512,512]{1,0:T(8,128)(2,1)}, bf16[512,512]{1,0:T(8,128)(2,1)}, u32[]{:S(2)}, u32[]{:S(2)}) collective-permute-start(bf16[512,512]{1,0:T(8,128)(2,1)} %bitcast.280), channel_id=1, source_target_pairs={{0,4},{4,8},{8,12},{12,16},{16,20},{20,24},{24,28},{1,5},{5,9},{9,... | collective-permute-start | bytes 1572872 | tf_op jit(solution)/shard_map/ppermute | solution.py:17
  53.0 3.2 copy-start.128
  77.5 59.7 %all-to-all-start.3 = ((bf16[256,4,1024]{2,0,1:T(8,128)(2,1)}), bf16[256,4,1024]{2,0,1:T(8,128)(2,1)S(1)}, u32[]{:S(2)}, u32[]{:S(2)}) async-start(bf16[256,4,1024]{2,0,1:T(8,128)(2,1)} %bitcast.218), calls=%async_computation.3 | async-start | bytes 4194304 | tf_op jit(solution)/shard_map/all_to_all | solution.py:69
  85.3 4.3 %copy-start.34 = (bf16[4,256,1024]{2,1,0:T(8,128)(2,1)S(1)}, bf16[4,256,1024]{2,1,0:T(8,128)(2,1)}, u32[]{:S(2)}) copy-start(bf16[4,256,1024]{2,1,0:T(8,128)(2,1)} %copy.109) | copy-start | bytes 6291460
  85.3 4.3 %copy-start.85 = (bf16[1024,128]{1,0:T(8,128)(2,1)S(1)}, bf16[1024,128]{1,0:T(8,128)(2,1)}, u32[]{:S(2)}) copy-start(bf16[1024,128]{1,0:T(8,128)(2,1)} %get-tuple-element.226) | copy-start | bytes 786436
  89.6 3.4 copy-start.83
  96.3 3.3 copy-start.81
  105.8 48.6 %copy-start.119 = (f32[512]{0:T(512)}, f32[512]{0:T(512)S(1)}, u32[]{:S(2)}) copy-start(f32[512]{0:T(512)S(1)} %get-tuple-element.250) | copy-start | bytes 6148
  112.0 45.1 %copy-start.117 = (f32[512]{0:T(512)}, f32[512]{0:T(512)S(1)}, u32[]{:S(2)}) copy-start(f32[512]{0:T(512)S(1)} %get-tuple-element.238) | copy-start | bytes 6148
  113.1 6.1 %copy-start.27 = (f32[512,1024]{0,1:T(8,128)}, f32[512,1024]{0,1:T(8,128)S(1)}, u32[]{:S(2)}) copy-start(f32[512,1024]{0,1:T(8,128)S(1)} %get-tuple-element.255) | copy-start | bytes 6291460
  116.0 90.4 %copy-start.113 = (f32[512]{0:T(512)}, f32[512]{0:T(512)S(1)}, u32[]{:S(2)}) copy-start(f32[512]{0:T(512)S(1)} %get-tuple-element.258) | copy-start | bytes 6148
  137.2 3.0 copy-start.7
  150.0 22.4 %copy-start.105 = (f32[512]{0:T(512)}, f32[512]{0:T(512)S(1)}, u32[]{:S(2)}) copy-start(f32[512]{0:T(512)S(1)} %log_add_fusion.14) | copy-start | bytes 6148
  150.8 8.9 %copy-start.101 = (f32[512]{0:T(512)}, f32[512]{0:T(512)S(1)}, u32[]{:S(2)}) copy-start(f32[512]{0:T(512)S(1)} %log_add_fusion.13) | copy-start | bytes 6148
  152.4 22.5 %copy-start.103 = (f32[512]{0:T(512)}, f32[512]{0:T(512)S(1)}, u32[]{:S(2)}) copy-start(f32[512]{0:T(512)S(1)} %log_add_fusion.12) | copy-start | bytes 6148
  153.1 5.5 %copy-start.97 = (f32[512]{0:T(512)}, f32[512]{0:T(512)S(1)}, u32[]{:S(2)}) copy-start(f32[512]{0:T(512)S(1)} %log_add_fusion.11) | copy-start | bytes 6148
  155.4 28.6 %copy-start.99 = (f32[512]{0:T(512)}, f32[512]{0:T(512)S(1)}, u32[]{:S(2)}) copy-start(f32[512]{0:T(512)S(1)} %log_add_fusion.10) | copy-start | bytes 6148
  158.1 37.6 %copy-start.94 = (f32[512]{0:T(512)}, f32[512]{0:T(512)S(1)}, u32[]{:S(2)}) copy-start(f32[512]{0:T(512)S(1)} %log_add_fusion.8) | copy-start | bytes 6148
  164.5 3.3 copy-start.28
  200.8 8.5 %copy-start.114 = (f32[512]{0:T(512)S(1)}, f32[512]{0:T(512)}, u32[]{:S(2)}) copy-start(f32[512]{0:T(512)} %get-tuple-element.262) | copy-start | bytes 6148
  206.5 3.2 copy-start.3
  206.5 3.2 copy-start.115
  219.4 6.2 %copy-start.25 = (f32[512,1024]{0,1:T(8,128)S(1)}, f32[512,1024]{0,1:T(8,128)}, u32[]{:S(2)}) copy-start(f32[512,1024]{0,1:T(8,128)} %get-tuple-element.243) | copy-start | bytes 6291460
  219.4 6.2 %copy-start.41 = (bf16[1024,128]{1,0:T(8,128)(2,1)S(1)}, bf16[1024,128]{1,0:T(8,128)(2,1)}, u32[]{:S(2)}) copy-start(bf16[1024,128]{1,0:T(8,128)(2,1)} %get-tuple-element.230) | copy-start | bytes 786436
  219.4 6.2 %copy-start.106 = (f32[512]{0:T(512)S(1)}, f32[512]{0:T(512)}, u32[]{:S(2)}) copy-start(f32[512]{0:T(512)} %copy-done.105) | copy-start | bytes 6148
  219.4 6.2 %copy-start.112 = (f32[512]{0:T(512)S(1)}, f32[512]{0:T(512)}, u32[]{:S(2)}) copy-start(f32[512]{0:T(512)} %get-tuple-element.203) | copy-start | bytes 6148
  219.9 6.3 %copy-start.31 = (f32[1536,512]{1,0:T(8,128)}, f32[1536,512]{1,0:T(8,128)S(1)}, u32[]{:S(2)}) copy-start(f32[1536,512]{1,0:T(8,128)S(1)} %fusion.65) | copy-start | bytes 9437188
  221.0 5.2 %copy-start.23 = (f32[512,1024]{0,1:T(8,128)S(1)}, f32[512,1024]{0,1:T(8,128)}, u32[]{:S(2)}) copy-start(f32[512,1024]{0,1:T(8,128)} %get-tuple-element.245) | copy-start | bytes 6291460
  221.0 5.2 %copy-start.39 = (bf16[1024,128]{1,0:T(8,128)(2,1)S(1)}, bf16[1024,128]{1,0:T(8,128)(2,1)}, u32[]{:S(2)}) copy-start(bf16[1024,128]{1,0:T(8,128)(2,1)} %get-tuple-element.229) | copy-start | bytes 786436
  221.0 5.2 %copy-start.102 = (f32[512]{0:T(512)S(1)}, f32[512]{0:T(512)}, u32[]{:S(2)}) copy-start(f32[512]{0:T(512)} %copy-done.101) | copy-start | bytes 6148
  221.0 5.2 %copy-start.111 = (f32[512]{0:T(512)S(1)}, f32[512]{0:T(512)}, u32[]{:S(2)}) copy-start(f32[512]{0:T(512)} %get-tuple-element.204) | copy-start | bytes 6148
  221.0 95.0 %collective-permute-start.3 = (f32[512,512]{1,0:T(8,128)}, f32[512,512]{1,0:T(8,128)}, u32[]{:S(2)}, u32[]{:S(2)}) collective-permute-start(f32[512,512]{1,0:T(8,128)} %slice.673), channel_id=1, source_target_pairs={{4,0},{8,4},{12,8},{16,12},{20,16},{24,20},{28,24},{5,1},{9,5},{13... | collective-permute-start | bytes 3145736 | tf_op jit(solution)/shard_map/ppermute | solution.py:17
  226.2 3.4 copy-start.44
  230.0 8.3 %copy-start.46 = (bf16[512,1024]{0,1:T(8,128)(2,1)}, bf16[512,1024]{0,1:T(8,128)(2,1)S(1)}, u32[]{:S(2)}) copy-start(bf16[512,1024]{0,1:T(8,128)(2,1)S(1)} %fusion.9) | copy-start | bytes 3145732
  233.6 3.0 copy-start.17
  233.7 3.0 copy-start.100
  233.7 3.0 copy-start.108
  234.2 4.0 %copy-start.60 = (bf16[512,1024]{0,1:T(8,128)(2,1)}, bf16[512,1024]{0,1:T(8,128)(2,1)S(1)}, u32[]{:S(2)}) copy-start(bf16[512,1024]{0,1:T(8,128)(2,1)S(1)} %fusion.7) | copy-start | bytes 3145732
  260.0 3.8 %copy-start.14 = (f32[512,1024]{0,1:T(8,128)S(1)}, f32[512,1024]{0,1:T(8,128)}, u32[]{:S(2)}) copy-start(f32[512,1024]{0,1:T(8,128)} %get-tuple-element.239) | copy-start | bytes 6291460
  260.0 3.8 %copy-start.95 = (f32[512]{0:T(512)S(1)}, f32[512]{0:T(512)}, u32[]{:S(2)}) copy-start(f32[512]{0:T(512)} %copy-done.94) | copy-start | bytes 6148
  260.0 3.8 %copy-start.107 = (f32[512]{0:T(512)S(1)}, f32[512]{0:T(512)}, u32[]{:S(2)}) copy-start(f32[512]{0:T(512)} %get-tuple-element.201) | copy-start | bytes 6148
  265.4 9.7 %copy-start.76 = (bf16[512,128]{1,0:T(8,128)(2,1)S(1)}, bf16[512,128]{1,0:T(8,128)(2,1)}, u32[]{:S(2)}) copy-start(bf16[512,128]{1,0:T(8,128)(2,1)} %convolution_convert_fusion.7) | copy-start | bytes 393220
  265.4 9.7 %copy-start.77 = (bf16[512,128]{1,0:T(8,128)(2,1)S(1)}, bf16[512,128]{1,0:T(8,128)(2,1)}, u32[]{:S(2)}) copy-start(bf16[512,128]{1,0:T(8,128)(2,1)} %convolution_convert_fusion.3) | copy-start | bytes 393220
  279.1 15.8 %copy-start.49 = (bf16[512,1024]{0,1:T(8,128)(2,1)}, bf16[512,1024]{0,1:T(8,128)(2,1)S(1)}, u32[]{:S(2)}) copy-start(bf16[512,1024]{0,1:T(8,128)(2,1)S(1)} %multiply_convert_fusion.6) | copy-start | bytes 3145732
  279.2 3.1 copy-start.6
  282.9 13.0 %copy-start.52 = (bf16[512,1024]{0,1:T(8,128)(2,1)}, bf16[512,1024]{0,1:T(8,128)(2,1)S(1)}, u32[]{:S(2)}) copy-start(bf16[512,1024]{0,1:T(8,128)(2,1)S(1)} %multiply_convert_fusion.4) | copy-start | bytes 3145732
  287.3 9.3 %copy-start.54 = (bf16[512,1024]{0,1:T(8,128)(2,1)}, bf16[512,1024]{0,1:T(8,128)(2,1)S(1)}, u32[]{:S(2)}) copy-start(bf16[512,1024]{0,1:T(8,128)(2,1)S(1)} %multiply_convert_fusion.2) | copy-start | bytes 3145732
  289.0 8.0 %copy-start.64 = (bf16[512,1024]{0,1:T(8,128)(2,1)}, bf16[512,1024]{0,1:T(8,128)(2,1)S(1)}, u32[]{:S(2)}) copy-start(bf16[512,1024]{0,1:T(8,128)(2,1)S(1)} %multiply_convert_fusion.1) | copy-start | bytes 3145732
  291.1 6.3 %copy-start.56 = (bf16[512,1024]{0,1:T(8,128)(2,1)}, bf16[512,1024]{0,1:T(8,128)(2,1)S(1)}, u32[]{:S(2)}) copy-start(bf16[512,1024]{0,1:T(8,128)(2,1)S(1)} %multiply_convert_fusion) | copy-start | bytes 3145732
  299.5 5.0 %copy-start.29 = (f32[1536,512]{1,0:T(8,128)S(1)}, f32[1536,512]{1,0:T(8,128)}, u32[]{:S(2)}) copy-start(f32[1536,512]{1,0:T(8,128)} %scatter-add.59) | copy-start | bytes 9437188
  299.5 30.8 %all-to-all-start.4 = ((bf16[4,256,1024]{1,2,0:T(8,128)(2,1)}), bf16[4,256,1024]{1,2,0:T(8,128)(2,1)}, u32[]{:S(2)}, u32[]{:S(2)}) async-start(bf16[4,256,1024]{1,2,0:T(8,128)(2,1)} %bitcast.220), calls=%async_computation.4 | async-start | bytes 4194304 | tf_op jit(solution)/shard_map/all_to_all | solution.py:136
  304.5 3.6 copy-start.65
  306.6 2.9 copy-start.55
  306.6 2.9 copy-start.73
  310.9 5.0 %copy-start.32 = (f32[1536,512]{1,0:T(8,128)S(1)}, f32[1536,512]{1,0:T(8,128)}, u32[]{:S(2)}) copy-start(f32[1536,512]{1,0:T(8,128)} %copy-done.31) | copy-start | bytes 9437188
  313.5 24.9 %collective-permute-start.2 = (f32[512,512]{1,0:T(8,128)}, f32[512,512]{1,0:T(8,128)}, u32[]{:S(2)}, u32[]{:S(2)}) collective-permute-start(f32[512,512]{1,0:T(8,128)} %slice.666), channel_id=1, source_target_pairs={{4,0},{8,4},{12,8},{16,12},{20,16},{24,20},{28,24},{5,1},{9,5},{13... | collective-permute-start | bytes 3145736 | tf_op jit(solution)/shard_map/ppermute | solution.py:17
  330.2 18.8 %all-to-all-start.6 = ((bf16[4,256,512]{2,1,0:T(8,128)(2,1)}), bf16[4,256,512]{2,1,0:T(8,128)(2,1)}, u32[]{:S(2)}, u32[]{:S(2)}) async-start(bf16[4,256,512]{2,1,0:T(8,128)(2,1)} %bitcast.275), calls=%async_computation.6 | async-start | bytes 2097152 | tf_op jit(solution)/shard_map/all_to_all | solution.py:138
  349.0 18.0 %all-to-all-start.5 = ((bf16[4,256,512]{2,1,0:T(8,128)(2,1)}), bf16[4,256,512]{2,1,0:T(8,128)(2,1)S(1)}, u32[]{:S(2)}, u32[]{:S(2)}) async-start(bf16[4,256,512]{2,1,0:T(8,128)(2,1)} %bitcast.38), calls=%async_computation.5 | async-start | bytes 2097152 | tf_op jit(solution)/shard_map/all_to_all | solution.py:137
  (76 other events, 146.6 us)
where the time goes:
time: 374 us; the launch traced here: 368 us
  matrix products  148 us (40%)
  local copies, waits for them, and re-layouts  91.8 us (25%)
  waiting for transfers between devices  66 us (18%)
  starting transfers between devices  36.7 us (10%)
  other arithmetic  23 us (6%)
    dot_general x32, matrix products, dot_rows(): lax.dot_general(left, right, (((1,), (1,)), ((), ())), preferred_element_...  63.8 us
    dot_general x32, matrix products, dot_cols(): lax.dot_general(left, right, (((0,), (0,)), ((), ())), preferred_element_...  63.8 us
    unnamed x262, local copies, waits for them, and re-layouts  25.6 us
    scatter-add x4, local copies, waits for them, and re-layouts, shards(): key_grad = key_grad.at[blk * span + lower:(blk + 2) * span, head * HEAD_S...  20.3 us
    scatter-add x4, local copies, waits for them, and re-layouts, shards(): value_grad = value_grad.at[blk * span + lower:(blk + 2) * span, head * HE...  20.1 us
    ppermute x4, waiting for transfers between devices, passed_along(): return lax.ppermute(x, axis, pairs)  16 us
    dot_general x16, matrix products, head_tile(): jnp.dot(probs_low, value_win, preferred_element_type=jnp.float32)  13 us
    all_to_all x1, waiting for transfers between devices, shards(): lax.all_to_all(values, 'head', split_axis=1, concat_axis=0, tiled=True)  12.4 us
  transfers between devices with their start and end apart: 11, of which 8 were waited for; matrix products, arithmetic and copies ran while one was open for 45% of the time, Pallas kernels for 0%

commit v1 on v0

v1 whole, which is shorter than its diff:
```python
import functools
import math

import jax
import jax.numpy as jnp
from jax import lax
from jax.experimental import pallas as pl
from jax.experimental.pallas import tpu as pltpu
from jax.sharding import PartitionSpec as P

HEAD_SIZE = 128
WINDOW_LENGTH = 512
AXES = ("seq", "head")
GROUPS = (6, 6, 4)
STEP = 2
UNIT = 128
STRIP = 32
VMEM_LIMIT = 16 * 1024 * 1024


scale_factor = 168.0 ** (-0.5)
log2_scale = scale_factor * math.log2(math.e)
negative = -1e30


def shifted(x, by, devices):
    pairs = [(i, i + by) for i in range(devices) if 0 <= i + by < devices]
    return lax.ppermute(x, AXES, pairs)


def swapped(x, devices):
    return lax.ppermute(x, AXES, [(i, i ^ 1) for i in range(devices)])


def to_odd(x, devices):
    return lax.ppermute(x, AXES, [(i, i + 1) for i in range(0, devices, 2)])


def to_even(x, devices):
    return lax.ppermute(x, AXES, [(i + 1, i) for i in range(0, devices, 2)])


def after(x, *others):
    return lax.optimization_barrier((x, *others))[0]


def dot_rows(left, right):
    return lax.dot_general(
        left, right, (((1,), (1,)), ((), ())), preferred_element_type=jnp.float32
    )


def dot_cols(left, right):
    return lax.dot_general(
        left, right, (((0,), (0,)), ((), ())), preferred_element_type=jnp.float32
    )


def dot(left, right):
    return jnp.dot(left, right, preferred_element_type=jnp.float32)


def merged(x, unit, pick_ref, at):
    if at >= unit:
        return x[at : at + STRIP]
    last = x.shape[0] - unit + at
    own = pick_ref[at : at + STRIP] > 0.5
    return jnp.where(own, x[last : last + STRIP], x[at : at + STRIP])


def spread(strips, unit, tri):
    edge = jnp.concatenate(strips[: unit // STRIP], axis=0)
    own = edge * tri
    return jnp.concatenate([edge - own] + strips[unit // STRIP :] + [own], axis=0)


def weigh(scores, dprobs, unit, bounds, pick_ref, tri):
    strips = range(0, scores.shape[0] - unit, STRIP)
    kept, peak = [], None
    for at in strips:
        s = jnp.minimum(merged(scores, unit, pick_ref, at), bounds[at : at + STRIP])
        kept.append(s)
        peak = s if peak is None else jnp.maximum(peak, s)
    peak = jnp.max(peak, axis=0, keepdims=True)
    low, dps = [], []
    total, weighted = 0.0, 0.0
    for at, s in zip(strips, kept):
        e = jnp.exp2((s - peak) * log2_scale)
        dp = merged(dprobs, unit, pick_ref, at)
        total = total + e
        weighted = weighted + e * dp
        low.append(e.astype(jnp.bfloat16))
        dps.append(dp)
    inverse = 1.0 / jnp.sum(total, axis=0, keepdims=True)
    delta = jnp.sum(weighted, axis=0, keepdims=True) * inverse
    ds = [e * (dp - delta).astype(jnp.bfloat16) for e, dp in zip(low, dps)]
    return spread(low, unit, tri), spread(ds, unit, tri), inverse


def products(q, g, k, low, ds, inverse):
    by_row = jnp.transpose(jnp.broadcast_to(inverse, (HEAD_SIZE, q.shape[0])))
    g_scaled = (g.astype(jnp.float32) * by_row).astype(jnp.bfloat16)
    q_scaled = (q.astype(jnp.float32) * (by_row * scale_factor)).astype(jnp.bfloat16)
    dv = dot(low, g_scaled)
    dk = dot(ds, q_scaled)
    dq = jnp.transpose(dot_cols(k, ds) * (inverse * scale_factor)).astype(jnp.bfloat16)
    return dq, dk, dv


def kernel(rows, back, group, split, pieces, base_ref, starts_ref, q_ref, g_ref, k_ref, v_ref, *refs):
    pairs = [refs[2 * j : 2 * j + 2] for j in range(back + split)]
    outs = refs[len(refs) - (back + 1 + pieces) - 3 : len(refs) - 3]
    bound_ref, pick_ref, tri_ref = refs[-3:]
    dq_ref, own_ref, near_refs, far_refs = outs[0], outs[1], outs[2 : 2 + pieces], outs[2 + pieces :]
    unit = min(UNIT, rows)
    units = rows // unit
    columns = group * unit
    span = back * rows

    @pl.when(pl.program_id(0) == 0)
    def _():
        col = lax.broadcasted_iota(jnp.int32, (unit, columns), 1) % unit
        row = lax.broadcasted_iota(jnp.int32, (unit, columns), 0)
        own = row <= col
        pick_ref[...] = own.astype(jnp.float32)
        tri_ref[...] = pick_ref[...].astype(jnp.bfloat16)
        for u in range(units):
            base = base_ref[0] + u * unit
            pos = base + col[:1]
            start = jnp.zeros_like(pos)
            for doc in range(starts_ref.shape[0]):
                at = starts_ref[doc]
                start = jnp.where(pos >= at, at, start)
            start = jnp.broadcast_to(start, (unit, columns))
            for at in range(0, span, unit):
                key_pos = base - span + at + row
                if at == 0:
                    key_pos = jnp.where(own, key_pos + span, key_pos)
                bound_ref[u, at : at + unit] = jnp.where(key_pos >= start, jnp.inf, negative)

    tri = tri_ref[...]
    heads = range(k_ref.shape[1] // HEAD_SIZE)
    works = []
    for h in heads:
        at = slice(h * HEAD_SIZE, (h + 1) * HEAD_SIZE)

        def gathered(own, half):
            blocks = [pair[half][:, at] for pair in pairs]
            if split:
                blocks[:2] = [blocks[0] + blocks[1]]
            return jnp.concatenate(blocks[::-1] + [own[:, at]], axis=0)

        k_all = gathered(k_ref, 0)
        v_all = gathered(v_ref, 1)
        for u in range(units):
            of_rows = slice(u * unit, (u + 1) * unit)
            wide = [
                slice((h * group + m) * HEAD_SIZE, (h * group + m + 1) * HEAD_SIZE)
                for m in range(group)
            ]
            q = jnp.concatenate([q_ref[of_rows, w] for w in wide], axis=0)
            g = jnp.concatenate([g_ref[of_rows, w] for w in wide], axis=0)
            seen = slice(u * unit, u * unit + span + unit)
            works.append((h, u, of_rows, wide, q, g, k_all[seen], v_all[seen]))

    def begin(work):
        h, u, of_rows, wide, q, g, k, v = work
        return dot_rows(k, q), dot_rows(v, g)

    sums = {}
    ahead = begin(works[0])
    for i, work in enumerate(works):
        h, u, of_rows, wide, q, g, k, v = work
        scores, dprobs = ahead
        if i + 1 < len(works):
            ahead = begin(works[i + 1])
        low, ds, inverse = weigh(scores, dprobs, unit, bound_ref.at[u], pick_ref, tri)
        dq, dk, dv = products(q, g, k, low, ds, inverse)
        for m, w in enumerate(wide):
            dq_ref[of_rows, w] = dq[m * unit : (m + 1) * unit]
        for name, term in (("k", dk), ("v", dv)):
            for j in range((span + unit) // unit):
                key = (name, u + j)
                piece = term[j * unit : (j + 1) * unit]
                sums[key] = piece if key not in sums else sums[key] + piece
        if u + 1 < units:
            continue
        at = slice(h * HEAD_SIZE, (h + 1) * HEAD_SIZE)
        order = [[x] for x in far_refs[::-1]] + [near_refs, [own_ref]]
        for j, arrays in enumerate(order):
            height = 2 * rows // len(arrays)
            for name, below in (("k", 0), ("v", rows)):
                for of_unit in range(units):
                    piece, to = divmod(below + of_unit * unit, height)
                    total = sums[(name, j * units + of_unit)].astype(jnp.bfloat16)
                    arrays[piece][to : to + unit, at] = total
        sums = {}


def attend(
    base, doc_starts, queries, dout, keys, values, near, others, first, heads, buffer, pieces
):
    rows, width = keys.shape
    back = 1 + len(others)
    group = queries.shape[1] // width
    step = STEP * HEAD_SIZE
    unit = min(UNIT, rows)

    def part(height, wide, offset, row=0):
        return pl.BlockSpec((height, wide), lambda i: (row, offset // STEP + i))

    wide = part(rows, group * step, first)
    narrow = part(rows, step, first)
    smem = pl.BlockSpec(memory_space=pltpu.SMEM)
    operands = [base, doc_starts, queries, dout, keys, values]
    in_specs = [smem, smem, wide, wide, narrow, narrow]
    for pair in near + others:
        operands += [pair[0], pair[-1]]
        in_specs += [part(rows, step, 0), part(rows, step, 0, 2 - len(pair))]
    if len(near) == 2:
        operands[6:] = [pltpu.with_memory_space_constraint(x, pltpu.VMEM) for x in operands[6:]]
    aliases = {}
    if buffer is not None:
        aliases = {len(operands): 0}
        operands.append(buffer)
        in_specs.append(pl.BlockSpec(memory_space=pl.ANY))
    whole = (2 * rows, heads * HEAD_SIZE)
    outs = [whole] + [(2 * rows // pieces, heads * HEAD_SIZE)] * pieces + [whole] * (back - 1)
    outs = [queries.shape] + outs
    return pl.pallas_call(
        functools.partial(kernel, rows, back, group, len(near) == 2, pieces),
        grid=(heads // STEP,),
        in_specs=in_specs,
        out_specs=[wide] + [part(shape[0], step, 0) for shape in outs[1:]],
        out_shape=[jax.ShapeDtypeStruct(outs[0], jnp.bfloat16)]
        + [pltpu.VMEM(shape, jnp.bfloat16) for shape in outs[1:]],
        scratch_shapes=[
            pltpu.VMEM((rows // unit, back * rows, group * unit), jnp.float32),
            pltpu.VMEM((unit, group * unit), jnp.float32),
            pltpu.VMEM((unit, group * unit), jnp.bfloat16),
        ],
        input_output_aliases=aliases,
        compiler_params=pltpu.CompilerParams(vmem_limit_bytes=VMEM_LIMIT),
        cost_estimate=pl.CostEstimate(flops=1, bytes_accessed=1, transcendentals=0),
        name="attend",
    )(*operands)


def pack_kernel(first, k_ref, v_ref, *refs):
    outs, sems = refs[:-1], refs[-1]
    rows, wide = k_ref.shape[0], outs[0].shape[1]
    columns = pl.ds(first * HEAD_SIZE, wide)
    copies = []
    for i, ref in enumerate((k_ref, v_ref)):
        place = outs[i] if len(outs) == 2 else outs[0].at[pl.ds(i * rows, rows)]
        copies.append(pltpu.make_async_copy(ref.at[:, columns], place, sems.at[i]))
        copies[-1].start()
    for copy in copies:
        copy.wait()


def pack(keys, values, first, heads, arrays):
    rows, wide = keys.shape[0], heads * HEAD_SIZE
    keys, values = (pltpu.with_memory_space_constraint(x, pltpu.HBM) for x in (keys, values))
    shape = (2 * rows // arrays, wide)
    return pl.pallas_call(
        functools.partial(pack_kernel, first),
        in_specs=[pl.BlockSpec(memory_space=pl.ANY)] * 2,
        out_specs=[pl.BlockSpec(memory_space=pltpu.VMEM)] * arrays,
        out_shape=[pltpu.VMEM(shape, keys.dtype)] * arrays,
        scratch_shapes=[pltpu.SemaphoreType.DMA((2,))],
        compiler_params=pltpu.CompilerParams(vmem_limit_bytes=4 * 1024 * 1024),
        name="pack",
    )(keys, values)


def finish_kernel(odd_ref, own_ref, back_ref, home_ref, *refs):
    dk_ref, dv_ref = refs[-2:]
    rows = dk_ref.shape[0]
    back = back_ref[...].astype(jnp.float32)
    total = own_ref[...].astype(jnp.float32) + jnp.where(odd_ref[0] == 1, 0.0, back)
    total = total + home_ref[...].astype(jnp.float32)
    dk_ref[...] = total[:rows].astype(dk_ref.dtype)
    dv_ref[...] = total[rows:].astype(dv_ref.dtype)


def finish(odd, own, back, home, start, heads, width, buffers):
    rows, wide = own.shape[0] // 2, STEP * HEAD_SIZE
    operands = [odd] + [
        pltpu.with_memory_space_constraint(x, pltpu.VMEM) for x in (own, back, home)
    ]
    in_specs = [pl.BlockSpec(memory_space=pltpu.SMEM)]
    in_specs += [pl.BlockSpec((2 * rows, wide), lambda i: (0, i))] * 3
    aliases = {}
    if buffers is not None:
        aliases = {len(operands): 0, len(operands) + 1: 1}
        operands += buffers
        in_specs += [pl.BlockSpec(memory_space=pl.ANY)] * 2
    return pl.pallas_call(
        finish_kernel,
        grid=(heads // STEP,),
        in_specs=in_specs,
        out_specs=[pl.BlockSpec((rows, wide), lambda i: (0, start // STEP + i))] * 2,
        out_shape=[pltpu.HBM((rows, width), jnp.bfloat16)] * 2,
        input_output_aliases=aliases,
        compiler_params=pltpu.CompilerParams(vmem_limit_bytes=4 * 1024 * 1024),
        cost_estimate=pl.CostEstimate(flops=1, bytes_accessed=1, transcendentals=0),
        name="finish",
    )(*operands)


def shards(queries, keys, values, dout, doc_starts):
    rows, width = keys.shape
    kv_heads = width // HEAD_SIZE
    back = WINDOW_LENGTH // rows
    devices = lax.axis_size("seq") * lax.axis_size("head")
    index = lax.axis_index("seq") * lax.axis_size("head") + lax.axis_index("head")
    base = (index * rows).astype(jnp.int32).reshape(1)
    if back != 2 or lax.axis_size("head") % 2 != 0:
        both = jnp.concatenate([keys, values], axis=0)
        halos = [shifted(both, j, devices) for j in range(1, back + 1)]
        dquery, own, *sent = attend(
            base, doc_starts, queries, dout, keys, values, [[halos[0]]], [[x] for x in halos[1:]], 0,
            kv_heads, None, 1,
        )
        total = own.astype(jnp.float32)
        for j in range(back):
            total = total + shifted(sent[j], -(j + 1), devices).astype(jnp.float32)
        total = total.astype(jnp.bfloat16)
        return (dquery, total[:rows], total[rows:])

    odd = (index % 2).astype(jnp.int32).reshape(1)
    keys, values, base, odd = lax.optimization_barrier((keys, values, base, odd))
    starts = [sum(GROUPS[:c]) for c in range(len(GROUPS))]
    packed = [pack(keys, values, start, heads, 1)[0] for start, heads in zip(starts, GROUPS)]
    far = [shifted(x, 2, devices) for x in packed]
    early = [to_odd(x, devices) for x in packed]

    def work(start, heads, received, own_near, dquery):
        near = to_even(received, devices)
        dquery, own, to_near, to_far = attend(
            base, doc_starts, queries, dout, keys, values, [[near], [own_near]], [[received]],
            start, heads, dquery, 1,
        )
        returned = swapped(to_near, devices)
        extra = jnp.where(odd[0] == 1, returned.astype(jnp.float32), 0.0)
        send = (to_far.astype(jnp.float32) + extra).astype(jnp.bfloat16)
        return dquery, own, returned, send

    always = (doc_starts[0] | 1) != 0
    dquery, homes, kept = None, [], []
    for start, heads, received, own_near in zip(starts, GROUPS, far, early):
        def skip(received, own_near, dquery):
            zeros = jnp.zeros_like(received)
            return jnp.zeros_like(queries) if dquery is None else dquery, zeros, zeros, zeros

        dquery, own, returned, send = lax.cond(
            always, functools.partial(work, start, heads), skip, received, own_near, dquery
        )
        homes.append(shifted(send, -2, devices))
        kept.append((own, returned))
    grads = None
    for start, heads, home, (own, returned) in zip(starts, GROUPS, homes, kept):
        grads = finish(odd, own, returned, home, start, heads, width, grads)
    dkey, dvalue = grads
    return (dquery, dkey, dvalue)


def solution(mesh):
    spec = P(AXES, None)
    return jax.shard_map(
        shards,
        mesh=mesh,
        in_specs=(spec, spec, spec, spec, P()),
        out_specs=(spec, spec, spec),
        check_vma=False,
    )
```

time: 374 us -> 103 us (0.28)
  the two profiles are of different devices: /device:TPU:26 before, /device:TPU:14 now
where the time goes in v1:
time: 103 us; the launch traced here: 102 us
  Pallas kernels  37.5 us (36%)
  starting transfers between devices  30.2 us (29%)
  waiting for transfers between devices  27.4 us (27%)
  other arithmetic  5.69 us (6%)
    pallas_call x3, Pallas kernels, attend(): pl.pallas_call(functools.partial(kernel, rows, back, group, len(near) ==...  24.1 us
    ppermute x6, starting transfers between devices, shifted(): return lax.ppermute(x, AXES, pairs)  19.9 us
    ppermute x6, waiting for transfers between devices, shifted(): return lax.ppermute(x, AXES, pairs)  12.4 us
    ppermute x3, waiting for transfers between devices, to_even(): return lax.ppermute(x, AXES, [(i + 1, i) for i in range(0, devices, 2)])  8.47 us
    pallas_call x3, Pallas kernels, finish(): pl.pallas_call(finish_kernel, grid=(heads // STEP,), in_specs=in_specs, o...  8.17 us
    ppermute x3, waiting for transfers between devices, swapped(): return lax.ppermute(x, AXES, [(i, i ^ 1) for i in range(devices)])  6.46 us
    ppermute x3, starting transfers between devices, to_odd(): return lax.ppermute(x, AXES, [(i, i + 1) for i in range(0, devices, 2)])  5.83 us
    convert_element_type x3, other arithmetic, work(): send = (to_far.astype(jnp.float32) + extra).astype(jnp.bfloat16)  5.69 us
  transfers between devices with their start and end apart: 15, of which 10 were waited for; matrix products, arithmetic and copies ran while one was open for 6% of the time, Pallas kernels for 34%

profile of v1, /device:TPU:14, one launch (start us, length us, event | category | flops | bytes accessed | tf_op | source)
XLA Modules:
  0.0 101.8 jit_solution(3273092457156528168)
XLA Ops:
  0.6 0.0 copy-start.4
  0.7 1.3 %pack.3 = bf16[512,768]{1,0:T(8,128)(2,1)S(1)} custom-call(bf16[256,2048]{1,0:T(8,128)(2,1)} %k_ref.2, bf16[256,2048]{1,0:T(8,128)(2,1)} %v_ref.2), custom_call_target="tpu_custom_call" | custom-call | tf_op jit(solution)/shard_map/pack/pallas_call | solution.py:266
  1.9 3.4 %collective-permute-start.6 = (bf16[512,768]{1,0:T(8,128)(2,1)S(1)}, bf16[512,768]{1,0:T(8,128)(2,1)S(1)}, u32[]{:S(2)}, u32[]{:S(2)}) collective-permute-start(bf16[512,768]{1,0:T(8,128)(2,1)S(1)} %pack.3), channel_id=1, source_target_pairs={{0,2},{1,3},{2,4},{3,5},{4,6},{5,7},{6,8},{7,9},{8,10},{9,11},{10,... | collective-permute-start | bytes 2359304 | tf_op jit(solution)/shard_map/ppermute | solution.py:28
  5.4 1.5 %collective-permute-start.7 = (bf16[512,768]{1,0:T(8,128)(2,1)S(1)}, bf16[512,768]{1,0:T(8,128)(2,1)S(1)}, u32[]{:S(2)}, u32[]{:S(2)}) collective-permute-start(bf16[512,768]{1,0:T(8,128)(2,1)S(1)} %pack.3), channel_id=1, source_target_pairs={{0,1},{2,3},{4,5},{6,7},{8,9},{10,11},{12,13},{14,15},{16,17},{18,... | collective-permute-start | bytes 2359304 | tf_op jit(solution)/shard_map/ppermute | solution.py:36
  6.9 0.0 copy-start.3
  6.9 2.2 %pack.4 = bf16[512,768]{1,0:T(8,128)(2,1)} custom-call(bf16[256,2048]{1,0:T(8,128)(2,1)} %k_ref.2, bf16[256,2048]{1,0:T(8,128)(2,1)} %v_ref.2), custom_call_target="tpu_custom_call" | custom-call | tf_op jit(solution)/shard_map/pack/pallas_call | solution.py:266
  9.1 0.0 copy-start.5
  9.1 0.0 copy-start
  9.1 0.0 copy-start.1
  9.1 3.6 %collective-permute-start.8 = (bf16[512,768]{1,0:T(8,128)(2,1)}, bf16[512,768]{1,0:T(8,128)(2,1)S(1)}, u32[]{:S(2)}, u32[]{:S(2)}) collective-permute-start(bf16[512,768]{1,0:T(8,128)(2,1)} %pack.4), channel_id=1, source_target_pairs={{0,2},{1,3},{2,4},{3,5},{4,6},{5,7},{6,8},{7,9},{8,10},{9,11},{10,... | collective-permute-start | bytes 2359304 | tf_op jit(solution)/shard_map/ppermute | solution.py:28
  12.7 2.2 %collective-permute-start.9 = (bf16[512,768]{1,0:T(8,128)(2,1)}, bf16[512,768]{1,0:T(8,128)(2,1)}, u32[]{:S(2)}, u32[]{:S(2)}) collective-permute-start(bf16[512,768]{1,0:T(8,128)(2,1)} %pack.4), channel_id=1, source_target_pairs={{0,1},{2,3},{4,5},{6,7},{8,9},{10,11},{12,13},{14,15},{16,17},{18,... | collective-permute-start | bytes 2359304 | tf_op jit(solution)/shard_map/ppermute | solution.py:36
  14.9 1.8 %pack.5 = bf16[512,512]{1,0:T(8,128)(2,1)} custom-call(bf16[256,2048]{1,0:T(8,128)(2,1)} %k_ref.2, bf16[256,2048]{1,0:T(8,128)(2,1)} %v_ref.2), custom_call_target="tpu_custom_call" | custom-call | tf_op jit(solution)/shard_map/pack/pallas_call | solution.py:266
  16.7 3.3 %collective-permute-start.10 = (bf16[512,512]{1,0:T(8,128)(2,1)}, bf16[512,512]{1,0:T(8,128)(2,1)}, u32[]{:S(2)}, u32[]{:S(2)}) collective-permute-start(bf16[512,512]{1,0:T(8,128)(2,1)} %pack.5), channel_id=1, source_target_pairs={{0,2},{1,3},{2,4},{3,5},{4,6},{5,7},{6,8},{7,9},{8,10},{9,11},{10,... | collective-permute-start | bytes 1572872 | tf_op jit(solution)/shard_map/ppermute | solution.py:28
  20.1 4.2 %collective-permute-done.6 = bf16[512,768]{1,0:T(8,128)(2,1)S(1)} collective-permute-done((bf16[512,768]{1,0:T(8,128)(2,1)S(1)}, bf16[512,768]{1,0:T(8,128)(2,1)S(1)}, u32[]{:S(2)}, u32[]{:S(2)}) %collective-permute-start.6) | collective-permute-done | bytes 786464 | tf_op jit(solution)/shard_map/ppermute | solution.py:28
  24.3 2.1 %collective-permute-start.11 = (bf16[512,512]{1,0:T(8,128)(2,1)}, bf16[512,512]{1,0:T(8,128)(2,1)}, u32[]{:S(2)}, u32[]{:S(2)}) collective-permute-start(bf16[512,512]{1,0:T(8,128)(2,1)} %pack.5), channel_id=1, source_target_pairs={{0,1},{2,3},{4,5},{6,7},{8,9},{10,11},{12,13},{14,15},{16,17},{18,... | collective-permute-start | bytes 1572872 | tf_op jit(solution)/shard_map/ppermute | solution.py:36
  26.4 0.0 copy-done.5
  26.4 0.0 collective-permute-done.7
  26.4 0.0 copy-done.4
  26.4 0.0 copy-done.3
  26.4 0.0 copy-done
  26.4 0.0 copy-done.1
  26.5 17.5 %conditional.3 = (bf16[256,4096]{1,0:T(8,128)(2,1)S(1)}, bf16[512,768]{1,0:T(8,128)(2,1)S(1)}, bf16[512,768]{1,0:T(8,128)(2,1)}, bf16[512,768]{1,0:T(8,128)(2,1)}) conditional(s32[]{:T(128)} %bitcast.3, () %tuple.33, (bf16[512,768]{1,0:T(8,128)(2,1)S(1)}, s32[1]{0:T(128)}, s32[8]{0:T(128)S(1)}, bf16[256,4096]{1,0:T(8,128)(2,1)S(1)}, ...), branch_computations={%region_0.1_spmd, %region_1.2_spmd} | conditional | flops 1966082 | bytes 8650875 | solution.py:357
  26.5 1.3 %collective-permute-start = (bf16[512,768]{1,0:T(8,128)(2,1)S(1)}, bf16[512,768]{1,0:T(8,128)(2,1)S(1)}, u32[]{:S(2)}, u32[]{:S(2)}) collective-permute-start(bf16[512,768]{1,0:T(8,128)(2,1)S(1)} %get-tuple-element.66.refs_4_.refs_5_), channel_id=1, source_target_pairs={{1,0},{3,2},{5,4},{7,6},{9,8},{11,10},{13,12},{15,14},{17,16},{19,... | collective-permute-start | bytes 2359304 | tf_op jit(solution)/shard_map/cond/branch_1_fun/ppermute | solution.py:40
  27.8 2.9 %collective-permute-done.refs_0_.refs_1_ = bf16[512,768]{1,0:T(8,128)(2,1)S(1)} collective-permute-done((bf16[512,768]{1,0:T(8,128)(2,1)S(1)}, bf16[512,768]{1,0:T(8,128)(2,1)S(1)}, u32[]{:S(2)}, u32[]{:S(2)}) %collective-permute-start) | collective-permute-done | bytes 786464 | tf_op jit(solution)/shard_map/cond/branch_1_fun/ppermute | solution.py:40
  30.7 8.6 %attend.3 = (bf16[256,4096]{1,0:T(8,128)(2,1)S(1)}, bf16[512,768]{1,0:T(8,128)(2,1)S(1)}, bf16[512,768]{1,0:T(8,128)(2,1)S(1)}, bf16[512,768]{1,0:T(8,128)(2,1)S(1)}) custom-call(s32[1]{0:T(128)} %get-tuple-element.60.base_ref, s32[8]{0:T(128)S(1)} %get-tuple-element.61.starts_ref, bf16[256,4096]{1,0:T(8,128)(2,1)S(1)} %get-tuple-element.62.q_ref, ...), custom_call_target="tpu_custom_call" | custom-call | flops 1 | bytes 1 | tf_op jit(solution)/shard_map/cond/branch_1_fun/attend/pallas_call | solution.py:230
  39.3 0.2 collective-permute-start.1
  39.5 2.3 %collective-permute-done.1 = bf16[512,768]{1,0:T(8,128)(2,1)} collective-permute-done((bf16[512,768]{1,0:T(8,128)(2,1)S(1)}, bf16[512,768]{1,0:T(8,128)(2,1)}, u32[]{:S(2)}, u32[]{:S(2)}) %collective-permute-start.1) | collective-permute-done | bytes 786464 | tf_op jit(solution)/shard_map/cond/branch_1_fun/ppermute | solution.py:32
  41.7 2.2 %add_convert_fusion = bf16[512,768]{1,0:T(8,128)(2,1)} fusion(bf16[512,768]{1,0:T(8,128)(2,1)} %collective-permute-done.1, bf16[512,768]{1,0:T(8,128)(2,1)S(1)} %get-tuple-element.71, pred[]{:T(512)} %bitcast), kind=kLoop, calls=%fused_computation | loop fusion | flops 1966080 | bytes 2359297 | tf_op jit(solution)/shard_map/cond/branch_1_fun/convert_element_type | solution.py:347
  44.0 3.3 %collective-permute-start.14 = (bf16[512,768]{1,0:T(8,128)(2,1)}, bf16[512,768]{1,0:T(8,128)(2,1)}, u32[]{:S(2)}, u32[]{:S(2)}) collective-permute-start(bf16[512,768]{1,0:T(8,128)(2,1)} %get-tuple-element.141), channel_id=1, source_target_pairs={{2,0},{3,1},{4,2},{5,3},{6,4},{7,5},{8,6},{9,7},{10,8},{11,9},{12,... | collective-permute-start | bytes 2359304 | tf_op jit(solution)/shard_map/ppermute | solution.py:28
  47.3 0.0 collective-permute-done.8
  47.3 0.0 collective-permute-done.9
  47.3 17.9 %conditional.4 = (bf16[256,4096]{1,0:T(8,128)(2,1)S(1)}, bf16[512,768]{1,0:T(8,128)(2,1)S(1)}, bf16[512,768]{1,0:T(8,128)(2,1)}, bf16[512,768]{1,0:T(8,128)(2,1)}) conditional(s32[]{:T(128)} %bitcast.3, bf16[256,4096]{1,0:T(8,128)(2,1)S(1)} %get-tuple-element.130, (bf16[512,768]{1,0:T(8,128)(2,1)S(1)}, s32[1]{0:T(128)}, s32[8]{0:T(128)S(1)}, ...), branch_computations={%region_2.3_spmd, %region_3.4_spmd} | conditional | flops 1966082 | bytes 8650875 | solution.py:357
  47.3 1.3 %collective-permute-start.2 = (bf16[512,768]{1,0:T(8,128)(2,1)S(1)}, bf16[512,768]{1,0:T(8,128)(2,1)S(1)}, u32[]{:S(2)}, u32[]{:S(2)}) collective-permute-start(bf16[512,768]{1,0:T(8,128)(2,1)S(1)} %get-tuple-element.79.refs_4_.refs_5_), channel_id=1, source_target_pairs={{1,0},{3,2},{5,4},{7,6},{9,8},{11,10},{13,12},{15,14},{17,16},{19,... | collective-permute-start | bytes 2359304 | tf_op jit(solution)/shard_map/cond/branch_1_fun/ppermute | solution.py:40
  48.6 2.9 %collective-permute-done.2.refs_0_.refs_1_ = bf16[512,768]{1,0:T(8,128)(2,1)S(1)} collective-permute-done((bf16[512,768]{1,0:T(8,128)(2,1)S(1)}, bf16[512,768]{1,0:T(8,128)(2,1)S(1)}, u32[]{:S(2)}, u32[]{:S(2)}) %collective-permute-start.2) | collective-permute-done | bytes 786464 | tf_op jit(solution)/shard_map/cond/branch_1_fun/ppermute | solution.py:40
  51.5 9.0 %attend.4 = (bf16[256,4096]{1,0:T(8,128)(2,1)S(1)}, bf16[512,768]{1,0:T(8,128)(2,1)S(1)}, bf16[512,768]{1,0:T(8,128)(2,1)S(1)}, bf16[512,768]{1,0:T(8,128)(2,1)S(1)}) custom-call(s32[1]{0:T(128)} %get-tuple-element.73.base_ref, s32[8]{0:T(128)S(1)} %get-tuple-element.74.starts_ref, ...), custom_call_target="tpu_custom_call", output_to_operand_aliasing={{0}: (12, {})} | custom-call | flops 1 | bytes 1 | tf_op jit(solution)/shard_map/cond/branch_1_fun/attend/pallas_call | solution.py:230
  60.5 0.2 collective-permute-start.3
  60.7 2.3 %collective-permute-done.3 = bf16[512,768]{1,0:T(8,128)(2,1)} collective-permute-done((bf16[512,768]{1,0:T(8,128)(2,1)S(1)}, bf16[512,768]{1,0:T(8,128)(2,1)}, u32[]{:S(2)}, u32[]{:S(2)}) %collective-permute-start.3) | collective-permute-done | bytes 786464 | tf_op jit(solution)/shard_map/cond/branch_1_fun/ppermute | solution.py:32
  63.0 2.2 %add_convert_fusion.1 = bf16[512,768]{1,0:T(8,128)(2,1)} fusion(bf16[512,768]{1,0:T(8,128)(2,1)} %collective-permute-done.3, bf16[512,768]{1,0:T(8,128)(2,1)S(1)} %get-tuple-element.85, pred[]{:T(512)} %bitcast.1), kind=kLoop, calls=%fused_computation.1 | loop fusion | flops 1966080 | bytes 2359297 | tf_op jit(solution)/shard_map/cond/branch_1_fun/convert_element_type | solution.py:347
  65.3 2.5 %collective-permute-start.13 = (bf16[512,768]{1,0:T(8,128)(2,1)}, bf16[512,768]{1,0:T(8,128)(2,1)}, u32[]{:S(2)}, u32[]{:S(2)}) collective-permute-start(bf16[512,768]{1,0:T(8,128)(2,1)} %get-tuple-element.138), channel_id=1, source_target_pairs={{2,0},{3,1},{4,2},{5,3},{6,4},{7,5},{8,6},{9,7},{10,8},{11,9},{12,... | collective-permute-start | bytes 2359304 | tf_op jit(solution)/shard_map/ppermute | solution.py:28
  67.7 0.4 collective-permute-done.10
  68.2 0.0 collective-permute-done.11
  68.2 13.8 %conditional.5 = (bf16[256,4096]{1,0:T(8,128)(2,1)S(1)}, bf16[512,512]{1,0:T(8,128)(2,1)S(1)}, bf16[512,512]{1,0:T(8,128)(2,1)}, bf16[512,512]{1,0:T(8,128)(2,1)S(1)}) conditional(s32[]{:T(128)} %bitcast.3, bf16[256,4096]{1,0:T(8,128)(2,1)S(1)} %get-tuple-element.131, (bf16[512,512]{1,0:T(8,128)(2,1)}, s32[1]{0:T(128)}, s32[8]{0:T(128)S(1)}, ...), branch_computations={%region_4.5_spmd, %region_5.6_spmd} | conditional | flops 1310722 | bytes 5767291 | solution.py:357
  68.2 1.3 %collective-permute-start.4 = (bf16[512,512]{1,0:T(8,128)(2,1)}, bf16[512,512]{1,0:T(8,128)(2,1)S(1)}, u32[]{:S(2)}, u32[]{:S(2)}) collective-permute-start(bf16[512,512]{1,0:T(8,128)(2,1)} %get-tuple-element.93.refs_4_.refs_5_), channel_id=1, source_target_pairs={{1,0},{3,2},{5,4},{7,6},{9,8},{11,10},{13,12},{15,14},{17,16},{19,... | collective-permute-start | bytes 1572872 | tf_op jit(solution)/shard_map/cond/branch_1_fun/ppermute | solution.py:40
  69.5 2.7 %collective-permute-done.4.refs_0_.refs_1_ = bf16[512,512]{1,0:T(8,128)(2,1)S(1)} collective-permute-done((bf16[512,512]{1,0:T(8,128)(2,1)}, bf16[512,512]{1,0:T(8,128)(2,1)S(1)}, u32[]{:S(2)}, u32[]{:S(2)}) %collective-permute-start.4) | collective-permute-done | bytes 524320 | tf_op jit(solution)/shard_map/cond/branch_1_fun/ppermute | solution.py:40
  72.2 6.5 %attend.5 = (bf16[256,4096]{1,0:T(8,128)(2,1)S(1)}, bf16[512,512]{1,0:T(8,128)(2,1)S(1)}, bf16[512,512]{1,0:T(8,128)(2,1)S(1)}, bf16[512,512]{1,0:T(8,128)(2,1)S(1)}) custom-call(s32[1]{0:T(128)} %get-tuple-element.87.base_ref, s32[8]{0:T(128)S(1)} %get-tuple-element.88.starts_ref, ...), custom_call_target="tpu_custom_call", output_to_operand_aliasing={{0}: (12, {})} | custom-call | flops 1 | bytes 1 | tf_op jit(solution)/shard_map/cond/branch_1_fun/attend/pallas_call | solution.py:230
  78.7 0.2 collective-permute-start.5
  78.9 1.9 %collective-permute-done.5 = bf16[512,512]{1,0:T(8,128)(2,1)} collective-permute-done((bf16[512,512]{1,0:T(8,128)(2,1)S(1)}, bf16[512,512]{1,0:T(8,128)(2,1)}, u32[]{:S(2)}, u32[]{:S(2)}) %collective-permute-start.5) | collective-permute-done | bytes 524320 | tf_op jit(solution)/shard_map/cond/branch_1_fun/ppermute | solution.py:32
  80.8 1.2 %add_convert_fusion.2 = bf16[512,512]{1,0:T(8,128)(2,1)S(1)} fusion(bf16[512,512]{1,0:T(8,128)(2,1)} %collective-permute-done.5, bf16[512,512]{1,0:T(8,128)(2,1)S(1)} %get-tuple-element.99, pred[]{:T(512)} %bitcast.2), kind=kLoop, calls=%fused_computation.2 | loop fusion | flops 1310720 | bytes 1572865 | tf_op jit(solution)/shard_map/cond/branch_1_fun/convert_element_type | solution.py:347
  82.0 0.0 copy-start.2
  82.0 3.8 %collective-permute-start.12 = (bf16[512,512]{1,0:T(8,128)(2,1)S(1)}, bf16[512,512]{1,0:T(8,128)(2,1)S(1)}, u32[]{:S(2)}, u32[]{:S(2)}) collective-permute-start(bf16[512,512]{1,0:T(8,128)(2,1)S(1)} %get-tuple-element.135), channel_id=1, source_target_pairs={{2,0},{3,1},{4,2},{5,3},{6,4},{7,5},{8,6},{9,7},{10,8},{11,9},{12,... | collective-permute-start | bytes 1572872 | tf_op jit(solution)/shard_map/ppermute | solution.py:28
  85.8 0.0 collective-permute-done.14.home_ref
  85.8 3.2 %finish.3 = (bf16[256,2048]{1,0:T(8,128)(2,1)}, bf16[256,2048]{1,0:T(8,128)(2,1)}) custom-call(s32[1]{0:T(128)} %bitcast.5.odd_ref, bf16[512,768]{1,0:T(8,128)(2,1)S(1)} %get-tuple-element.139.own_ref, bf16[512,768]{1,0:T(8,128)(2,1)} %get-tuple-element.140.back_ref, bf16[512,768]{1,0:T(8,128)(2,1)} %collective-permute-done.14.home_ref), custom_call_target="tpu_custom_call" | custom-call | flops 1 | bytes 1 | tf_op jit(solution)/shard_map/finish/pallas_call | solution.py:299
  89.0 0.1 collective-permute-done.13.home_ref
  89.1 3.1 %finish.4 = (bf16[256,2048]{1,0:T(8,128)(2,1)}, bf16[256,2048]{1,0:T(8,128)(2,1)}) custom-call(s32[1]{0:T(128)} %bitcast.5.odd_ref, bf16[512,768]{1,0:T(8,128)(2,1)S(1)} %get-tuple-element.136.own_ref, bf16[512,768]{1,0:T(8,128)(2,1)} %get-tuple-element.137.back_ref, ...), custom_call_target="tpu_custom_call", output_to_operand_aliasing={{0}: (4, {}), {1}: (5, {})} | custom-call | flops 1 | bytes 1 | tf_op jit(solution)/shard_map/finish/pallas_call | solution.py:299
  92.2 0.0 copy-done.2
  92.2 7.7 %collective-permute-done.12.home_ref = bf16[512,512]{1,0:T(8,128)(2,1)S(1)} collective-permute-done((bf16[512,512]{1,0:T(8,128)(2,1)S(1)}, bf16[512,512]{1,0:T(8,128)(2,1)S(1)}, u32[]{:S(2)}, u32[]{:S(2)}) %collective-permute-start.12) | collective-permute-done | bytes 524320 | tf_op jit(solution)/shard_map/ppermute | solution.py:28
  100.0 1.9 %finish.5 = (bf16[256,2048]{1,0:T(8,128)(2,1)}, bf16[256,2048]{1,0:T(8,128)(2,1)}) custom-call(s32[1]{0:T(128)} %bitcast.5.odd_ref, bf16[512,512]{1,0:T(8,128)(2,1)S(1)} %get-tuple-element.133.own_ref, bf16[512,512]{1,0:T(8,128)(2,1)} %get-tuple-element.134.back_ref, ...), custom_call_target="tpu_custom_call", output_to_operand_aliasing={{0}: (4, {}), {1}: (5, {})} | custom-call | flops 1 | bytes 1 | tf_op jit(solution)/shard_map/finish/pallas_call | solution.py:299
Async XLA Ops:
  0.6 25.8 %copy-start.4 = (bf16[256,4096]{1,0:T(8,128)(2,1)S(1)}, bf16[256,4096]{1,0:T(8,128)(2,1)}, u32[]{:S(2)}) copy-start(bf16[256,4096]{1,0:T(8,128)(2,1)} %param.14) | copy-start | bytes 6291460
  1.9 22.3 %collective-permute-start.6 = (bf16[512,768]{1,0:T(8,128)(2,1)S(1)}, bf16[512,768]{1,0:T(8,128)(2,1)S(1)}, u32[]{:S(2)}, u32[]{:S(2)}) collective-permute-start(bf16[512,768]{1,0:T(8,128)(2,1)S(1)} %pack.3), channel_id=1, source_target_pairs={{0,2},{1,3},{2,4},{3,5},{4,6},{5,7},{6,8},{7,9},{8,10},{9,11},{10,... | collective-permute-start | bytes 2359304 | tf_op jit(solution)/shard_map/ppermute | solution.py:28
  5.4 21.1 %collective-permute-start.7 = (bf16[512,768]{1,0:T(8,128)(2,1)S(1)}, bf16[512,768]{1,0:T(8,128)(2,1)S(1)}, u32[]{:S(2)}, u32[]{:S(2)}) collective-permute-start(bf16[512,768]{1,0:T(8,128)(2,1)S(1)} %pack.3), channel_id=1, source_target_pairs={{0,1},{2,3},{4,5},{6,7},{8,9},{10,11},{12,13},{14,15},{16,17},{18,... | collective-permute-start | bytes 2359304 | tf_op jit(solution)/shard_map/ppermute | solution.py:36
  6.9 19.6 %copy-start.3 = (bf16[256,4096]{1,0:T(8,128)(2,1)S(1)}, bf16[256,4096]{1,0:T(8,128)(2,1)}, u32[]{:S(2)}) copy-start(bf16[256,4096]{1,0:T(8,128)(2,1)} %param.11) | copy-start | bytes 6291460
  9.1 17.3 %copy-start.5 = (s32[8]{0:T(128)S(1)}, s32[8]{0:T(128)}, u32[]{:S(2)}) copy-start(s32[8]{0:T(128)} %param.15) | copy-start | bytes 100
  9.1 17.4 %copy-start = (bf16[256,2048]{1,0:T(8,128)(2,1)S(1)}, bf16[256,2048]{1,0:T(8,128)(2,1)}, u32[]{:S(2)}) copy-start(bf16[256,2048]{1,0:T(8,128)(2,1)} %k_ref.2) | copy-start | bytes 3145732
  9.1 17.4 %copy-start.1 = (bf16[256,2048]{1,0:T(8,128)(2,1)S(1)}, bf16[256,2048]{1,0:T(8,128)(2,1)}, u32[]{:S(2)}) copy-start(bf16[256,2048]{1,0:T(8,128)(2,1)} %v_ref.2) | copy-start | bytes 3145732
  9.1 38.2 %collective-permute-start.8 = (bf16[512,768]{1,0:T(8,128)(2,1)}, bf16[512,768]{1,0:T(8,128)(2,1)S(1)}, u32[]{:S(2)}, u32[]{:S(2)}) collective-permute-start(bf16[512,768]{1,0:T(8,128)(2,1)} %pack.4), channel_id=1, source_target_pairs={{0,2},{1,3},{2,4},{3,5},{4,6},{5,7},{6,8},{7,9},{8,10},{9,11},{10,... | collective-permute-start | bytes 2359304 | tf_op jit(solution)/shard_map/ppermute | solution.py:28
  12.7 34.6 %collective-permute-start.9 = (bf16[512,768]{1,0:T(8,128)(2,1)}, bf16[512,768]{1,0:T(8,128)(2,1)}, u32[]{:S(2)}, u32[]{:S(2)}) collective-permute-start(bf16[512,768]{1,0:T(8,128)(2,1)} %pack.4), channel_id=1, source_target_pairs={{0,1},{2,3},{4,5},{6,7},{8,9},{10,11},{12,13},{14,15},{16,17},{18,... | collective-permute-start | bytes 2359304 | tf_op jit(solution)/shard_map/ppermute | solution.py:36
  16.7 51.4 %collective-permute-start.10 = (bf16[512,512]{1,0:T(8,128)(2,1)}, bf16[512,512]{1,0:T(8,128)(2,1)}, u32[]{:S(2)}, u32[]{:S(2)}) collective-permute-start(bf16[512,512]{1,0:T(8,128)(2,1)} %pack.5), channel_id=1, source_target_pairs={{0,2},{1,3},{2,4},{3,5},{4,6},{5,7},{6,8},{7,9},{8,10},{9,11},{10,... | collective-permute-start | bytes 1572872 | tf_op jit(solution)/shard_map/ppermute | solution.py:28
  24.3 43.9 %collective-permute-start.11 = (bf16[512,512]{1,0:T(8,128)(2,1)}, bf16[512,512]{1,0:T(8,128)(2,1)}, u32[]{:S(2)}, u32[]{:S(2)}) collective-permute-start(bf16[512,512]{1,0:T(8,128)(2,1)} %pack.5), channel_id=1, source_target_pairs={{0,1},{2,3},{4,5},{6,7},{8,9},{10,11},{12,13},{14,15},{16,17},{18,... | collective-permute-start | bytes 1572872 | tf_op jit(solution)/shard_map/ppermute | solution.py:36
  26.5 4.2 %collective-permute-start = (bf16[512,768]{1,0:T(8,128)(2,1)S(1)}, bf16[512,768]{1,0:T(8,128)(2,1)S(1)}, u32[]{:S(2)}, u32[]{:S(2)}) collective-permute-start(bf16[512,768]{1,0:T(8,128)(2,1)S(1)} %get-tuple-element.66.refs_4_.refs_5_), channel_id=1, source_target_pairs={{1,0},{3,2},{5,4},{7,6},{9,8},{11,10},{13,12},{15,14},{17,16},{19,... | collective-permute-start | bytes 2359304 | tf_op jit(solution)/shard_map/cond/branch_1_fun/ppermute | solution.py:40
  39.3 2.5 %collective-permute-start.1 = (bf16[512,768]{1,0:T(8,128)(2,1)S(1)}, bf16[512,768]{1,0:T(8,128)(2,1)}, u32[]{:S(2)}, u32[]{:S(2)}) collective-permute-start(bf16[512,768]{1,0:T(8,128)(2,1)S(1)} %get-tuple-element.70), channel_id=1, source_target_pairs={{0,1},{1,0},{2,3},{3,2},{4,5},{5,4},{6,7},{7,6},{8,9},{9,8},{10,11... | collective-permute-start | bytes 2359304 | tf_op jit(solution)/shard_map/cond/branch_1_fun/ppermute | solution.py:32
  44.0 41.9 %collective-permute-start.14 = (bf16[512,768]{1,0:T(8,128)(2,1)}, bf16[512,768]{1,0:T(8,128)(2,1)}, u32[]{:S(2)}, u32[]{:S(2)}) collective-permute-start(bf16[512,768]{1,0:T(8,128)(2,1)} %get-tuple-element.141), channel_id=1, source_target_pairs={{2,0},{3,1},{4,2},{5,3},{6,4},{7,5},{8,6},{9,7},{10,8},{11,9},{12,... | collective-permute-start | bytes 2359304 | tf_op jit(solution)/shard_map/ppermute | solution.py:28
  47.3 4.2 %collective-permute-start.2 = (bf16[512,768]{1,0:T(8,128)(2,1)S(1)}, bf16[512,768]{1,0:T(8,128)(2,1)S(1)}, u32[]{:S(2)}, u32[]{:S(2)}) collective-permute-start(bf16[512,768]{1,0:T(8,128)(2,1)S(1)} %get-tuple-element.79.refs_4_.refs_5_), channel_id=1, source_target_pairs={{1,0},{3,2},{5,4},{7,6},{9,8},{11,10},{13,12},{15,14},{17,16},{19,... | collective-permute-start | bytes 2359304 | tf_op jit(solution)/shard_map/cond/branch_1_fun/ppermute | solution.py:40
  60.5 2.5 %collective-permute-start.3 = (bf16[512,768]{1,0:T(8,128)(2,1)S(1)}, bf16[512,768]{1,0:T(8,128)(2,1)}, u32[]{:S(2)}, u32[]{:S(2)}) collective-permute-start(bf16[512,768]{1,0:T(8,128)(2,1)S(1)} %get-tuple-element.84), channel_id=1, source_target_pairs={{0,1},{1,0},{2,3},{3,2},{4,5},{5,4},{6,7},{7,6},{8,9},{9,8},{10,11... | collective-permute-start | bytes 2359304 | tf_op jit(solution)/shard_map/cond/branch_1_fun/ppermute | solution.py:32
  65.3 23.8 %collective-permute-start.13 = (bf16[512,768]{1,0:T(8,128)(2,1)}, bf16[512,768]{1,0:T(8,128)(2,1)}, u32[]{:S(2)}, u32[]{:S(2)}) collective-permute-start(bf16[512,768]{1,0:T(8,128)(2,1)} %get-tuple-element.138), channel_id=1, source_target_pairs={{2,0},{3,1},{4,2},{5,3},{6,4},{7,5},{8,6},{9,7},{10,8},{11,9},{12,... | collective-permute-start | bytes 2359304 | tf_op jit(solution)/shard_map/ppermute | solution.py:28
  68.2 4.0 %collective-permute-start.4 = (bf16[512,512]{1,0:T(8,128)(2,1)}, bf16[512,512]{1,0:T(8,128)(2,1)S(1)}, u32[]{:S(2)}, u32[]{:S(2)}) collective-permute-start(bf16[512,512]{1,0:T(8,128)(2,1)} %get-tuple-element.93.refs_4_.refs_5_), channel_id=1, source_target_pairs={{1,0},{3,2},{5,4},{7,6},{9,8},{11,10},{13,12},{15,14},{17,16},{19,... | collective-permute-start | bytes 1572872 | tf_op jit(solution)/shard_map/cond/branch_1_fun/ppermute | solution.py:40
  78.7 2.1 %collective-permute-start.5 = (bf16[512,512]{1,0:T(8,128)(2,1)S(1)}, bf16[512,512]{1,0:T(8,128)(2,1)}, u32[]{:S(2)}, u32[]{:S(2)}) collective-permute-start(bf16[512,512]{1,0:T(8,128)(2,1)S(1)} %get-tuple-element.98), channel_id=1, source_target_pairs={{0,1},{1,0},{2,3},{3,2},{4,5},{5,4},{6,7},{7,6},{8,9},{9,8},{10,11... | collective-permute-start | bytes 1572872 | tf_op jit(solution)/shard_map/cond/branch_1_fun/ppermute | solution.py:32
  82.0 10.3 %copy-start.2 = (bf16[256,4096]{1,0:T(8,128)(2,1)}, bf16[256,4096]{1,0:T(8,128)(2,1)S(1)}, u32[]{:S(2)}) copy-start(bf16[256,4096]{1,0:T(8,128)(2,1)S(1)} %get-tuple-element.123) | copy-start | bytes 6291460
  82.0 18.0 %collective-permute-start.12 = (bf16[512,512]{1,0:T(8,128)(2,1)S(1)}, bf16[512,512]{1,0:T(8,128)(2,1)S(1)}, u32[]{:S(2)}, u32[]{:S(2)}) collective-permute-start(bf16[512,512]{1,0:T(8,128)(2,1)S(1)} %get-tuple-element.135), channel_id=1, source_target_pairs={{2,0},{3,1},{4,2},{5,3},{6,4},{7,5},{8,6},{9,7},{10,8},{11,9},{12,... | collective-permute-start | bytes 1572872 | tf_op jit(solution)/shard_map/ppermute | solution.py:28

commit v2 on v1

--- a/solution.py
+++ b/solution.py
@@ -11,7 +11,7 @@
 HEAD_SIZE = 128
 WINDOW_LENGTH = 512
 AXES = ("seq", "head")
-GROUPS = (6, 6, 4)
+GROUPS = ((8,), (4, 4))
 STEP = 2
 UNIT = 128
 STRIP = 32
@@ -21,6 +21,10 @@
 scale_factor = 168.0 ** (-0.5)
 log2_scale = scale_factor * math.log2(math.e)
 negative = -1e30
+
+
+def device_index():
+    return lax.axis_index("seq") * lax.axis_size("head") + lax.axis_index("head")
 
 
 def shifted(x, by, devices):
@@ -107,7 +111,7 @@
     return dq, dk, dv
 
 
-def kernel(rows, back, group, split, pieces, base_ref, starts_ref, q_ref, g_ref, k_ref, v_ref, *refs):
+def kernel(rows, back, group, split, pieces, starts_ref, q_ref, g_ref, k_ref, v_ref, *refs):
     pairs = [refs[2 * j : 2 * j + 2] for j in range(back + split)]
     outs = refs[len(refs) - (back + 1 + pieces) - 3 : len(refs) - 3]
     bound_ref, pick_ref, tri_ref = refs[-3:]
@@ -125,7 +129,7 @@
         pick_ref[...] = own.astype(jnp.float32)
         tri_ref[...] = pick_ref[...].astype(jnp.bfloat16)
         for u in range(units):
-            base = base_ref[0] + u * unit
+            base = device_index() * rows + u * unit
             pos = base + col[:1]
             start = jnp.zeros_like(pos)
             for doc in range(starts_ref.shape[0]):
@@ -198,7 +202,7 @@
 
 
 def attend(
-    base, doc_starts, queries, dout, keys, values, near, others, first, heads, buffer, pieces
+    doc_starts, queries, dout, keys, values, near, others, start, first, heads, buffer, pieces
 ):
     rows, width = keys.shape
     back = 1 + len(others)
@@ -212,13 +216,13 @@
     wide = part(rows, group * step, first)
     narrow = part(rows, step, first)
     smem = pl.BlockSpec(memory_space=pltpu.SMEM)
-    operands = [base, doc_starts, queries, dout, keys, values]
-    in_specs = [smem, smem, wide, wide, narrow, narrow]
+    operands = [doc_starts, queries, dout, keys, values]
+    in_specs = [smem, wide, wide, narrow, narrow]
     for pair in near + others:
         operands += [pair[0], pair[-1]]
-        in_specs += [part(rows, step, 0), part(rows, step, 0, 2 - len(pair))]
+        in_specs += [part(rows, step, first - start, row) for row in (0, 2 - len(pair))]
     if len(near) == 2:
-        operands[6:] = [pltpu.with_memory_space_constraint(x, pltpu.VMEM) for x in operands[6:]]
+        operands[5:] = [pltpu.with_memory_space_constraint(x, pltpu.VMEM) for x in operands[5:]]
     aliases = {}
     if buffer is not None:
         aliases = {len(operands): 0}
@@ -274,37 +278,77 @@
     )(keys, values)
 
 
-def finish_kernel(odd_ref, own_ref, back_ref, home_ref, *refs):
-    dk_ref, dv_ref = refs[-2:]
-    rows = dk_ref.shape[0]
-    back = back_ref[...].astype(jnp.float32)
-    total = own_ref[...].astype(jnp.float32) + jnp.where(odd_ref[0] == 1, 0.0, back)
-    total = total + home_ref[...].astype(jnp.float32)
-    dk_ref[...] = total[:rows].astype(dk_ref.dtype)
-    dv_ref[...] = total[rows:].astype(dv_ref.dtype)
-
-
-def finish(odd, own, back, home, start, heads, width, buffers):
-    rows, wide = own.shape[0] // 2, STEP * HEAD_SIZE
-    operands = [odd] + [
-        pltpu.with_memory_space_constraint(x, pltpu.VMEM) for x in (own, back, home)
-    ]
-    in_specs = [pl.BlockSpec(memory_space=pltpu.SMEM)]
-    in_specs += [pl.BlockSpec((2 * rows, wide), lambda i: (0, i))] * 3
+SMALL = pltpu.CompilerParams(vmem_limit_bytes=6 * 1024 * 1024)
+FREE = pl.CostEstimate(flops=1, bytes_accessed=1, transcendentals=0)
+
+
+def in_vmem(*arrays):
+    return [pltpu.with_memory_space_constraint(x, pltpu.VMEM) for x in arrays]
+
+
+def merge_kernel(far_ref, own_ref, back_ref, send_ref, kept_ref):
+    odd = device_index() % 2 == 1
+
+    @pl.when(odd)
+    def _():
+        total = far_ref[...].astype(jnp.float32) + back_ref[...].astype(jnp.float32)
+        send_ref[...] = total.astype(send_ref.dtype)
+        kept_ref[...] = own_ref[...]
+
+    @pl.when(jnp.logical_not(odd))
+    def _():
+        send_ref[...] = far_ref[...]
+        total = own_ref[...].astype(jnp.float32) + back_ref[...].astype(jnp.float32)
+        kept_ref[...] = total.astype(kept_ref.dtype)
+
+
+def merge(far, own, back):
+    whole = pl.BlockSpec(memory_space=pltpu.VMEM)
+    return pl.pallas_call(
+        merge_kernel,
+        in_specs=[whole] * 3,
+        out_specs=[whole] * 2,
+        out_shape=[pltpu.VMEM(far.shape, far.dtype)] * 2,
+        compiler_params=SMALL,
+        cost_estimate=FREE,
+        name="merge",
+    )(*in_vmem(far, own, back))
+
+
+def finish_kernel(first, kept_ref, home_ref, *refs):
+    outs, total_ref, sems = refs[-4:-2], refs[-2], refs[-1]
+    rows, wide = kept_ref.shape[0] // 2, kept_ref.shape[1]
+    copies = []
+    for i, out in enumerate(outs):
+        half = slice(i * rows, (i + 1) * rows)
+        total = kept_ref[half].astype(jnp.float32) + home_ref[half].astype(jnp.float32)
+        total_ref[half] = total.astype(total_ref.dtype)
+        place = out.at[:, pl.ds(first * HEAD_SIZE, wide)]
+        copies.append(pltpu.make_async_copy(total_ref.at[half], place, sems.at[i]))
+        copies[-1].start()
+    for copy in copies:
+        copy.wait()
+
+
+def finish(kept, home, first, width, buffers):
+    whole = pl.BlockSpec(memory_space=pltpu.VMEM)
+    anywhere = pl.BlockSpec(memory_space=pl.ANY)
+    operands = in_vmem(kept, home)
+    in_specs = [whole] * 2
     aliases = {}
     if buffers is not None:
-        aliases = {len(operands): 0, len(operands) + 1: 1}
+        aliases = {2: 0, 3: 1}
         operands += buffers
-        in_specs += [pl.BlockSpec(memory_space=pl.ANY)] * 2
+        in_specs += [anywhere] * 2
     return pl.pallas_call(
-        finish_kernel,
-        grid=(heads // STEP,),
+        functools.partial(finish_kernel, first),
         in_specs=in_specs,
-        out_specs=[pl.BlockSpec((rows, wide), lambda i: (0, start // STEP + i))] * 2,
-        out_shape=[pltpu.HBM((rows, width), jnp.bfloat16)] * 2,
+        out_specs=[anywhere] * 2,
+        out_shape=[pltpu.HBM((kept.shape[0] // 2, width), kept.dtype)] * 2,
+        scratch_shapes=[pltpu.VMEM(kept.shape, kept.dtype), pltpu.SemaphoreType.DMA((2,))],
         input_output_aliases=aliases,
-        compiler_params=pltpu.CompilerParams(vmem_limit_bytes=4 * 1024 * 1024),
-        cost_estimate=pl.CostEstimate(flops=1, bytes_accessed=1, transcendentals=0),
+        compiler_params=SMALL,
+        cost_estimate=FREE,
         name="finish",
     )(*operands)
 
@@ -314,13 +358,11 @@
     kv_heads = width // HEAD_SIZE
     back = WINDOW_LENGTH // rows
     devices = lax.axis_size("seq") * lax.axis_size("head")
-    index = lax.axis_index("seq") * lax.axis_size("head") + lax.axis_index("head")
-    base = (index * rows).astype(jnp.int32).reshape(1)
     if back != 2 or lax.axis_size("head") % 2 != 0:
         both = jnp.concatenate([keys, values], axis=0)
         halos = [shifted(both, j, devices) for j in range(1, back + 1)]
         dquery, own, *sent = attend(
-            base, doc_starts, queries, dout, keys, values, [[halos[0]]], [[x] for x in halos[1:]], 0,
+            doc_starts, queries, dout, keys, values, [[halos[0]]], [[x] for x in halos[1:]], 0, 0,
             kv_heads, None, 1,
         )
         total = own.astype(jnp.float32)
@@ -329,39 +371,46 @@
         total = total.astype(jnp.bfloat16)
         return (dquery, total[:rows], total[rows:])
 
-    odd = (index % 2).astype(jnp.int32).reshape(1)
-    keys, values, base, odd = lax.optimization_barrier((keys, values, base, odd))
-    starts = [sum(GROUPS[:c]) for c in range(len(GROUPS))]
-    packed = [pack(keys, values, start, heads, 1)[0] for start, heads in zip(starts, GROUPS)]
+    starts = [sum(map(sum, GROUPS[:c])) for c in range(len(GROUPS))]
+    packed = [pack(keys, values, start, sum(group), 1)[0] for start, group in zip(starts, GROUPS)]
     far = [shifted(x, 2, devices) for x in packed]
-    early = [to_odd(x, devices) for x in packed]
-
-    def work(start, heads, received, own_near, dquery):
-        near = to_even(received, devices)
+    early = [to_odd(after(x, *packed), devices) for x in packed]
+    far[0] = after(far[0], *early)
+
+    def work(start, first, heads, received, own_near, near, dquery):
+        if near is None:
+            near = to_even(received, devices)
         dquery, own, to_near, to_far = attend(
-            base, doc_starts, queries, dout, keys, values, [[near], [own_near]], [[received]],
-            start, heads, dquery, 1,
+            doc_starts, queries, dout, keys, values, [[near], [own_near]], [[received]],
+            start, first, heads, dquery, 1,
         )
         returned = swapped(to_near, devices)
-        extra = jnp.where(odd[0] == 1, returned.astype(jnp.float32), 0.0)
-        send = (to_far.astype(jnp.float32) + extra).astype(jnp.bfloat16)
-        return dquery, own, returned, send
+        return near, dquery, *merge(to_far, own, returned)
 
     always = (doc_starts[0] | 1) != 0
-    dquery, homes, kept = None, [], []
-    for start, heads, received, own_near in zip(starts, GROUPS, far, early):
-        def skip(received, own_near, dquery):
-            zeros = jnp.zeros_like(received)
-            return jnp.zeros_like(queries) if dquery is None else dquery, zeros, zeros, zeros
-
-        dquery, own, returned, send = lax.cond(
-            always, functools.partial(work, start, heads), skip, received, own_near, dquery
-        )
-        homes.append(shifted(send, -2, devices))
-        kept.append((own, returned))
+    dquery, sums = None, []
+    for start, group, received, own_near in zip(starts, GROUPS, far, early):
+        near, first = None, start
+        for heads in group:
+            def skip(received, own_near, near, dquery):
+                part = jnp.zeros((2 * rows, heads * HEAD_SIZE), received.dtype)
+                near = jnp.zeros_like(received) if near is None else near
+                return near, jnp.zeros_like(queries) if dquery is None else dquery, part, part
+
+            near, dquery, send, kept = lax.cond(
+                always,
+                functools.partial(work, start, first, heads),
+                skip,
+                received,
+                own_near,
+                near,
+                dquery,
+            )
+            sums.append((first, kept, shifted(send, -2, devices)))
+            first += heads
     grads = None
-    for start, heads, home, (own, returned) in zip(starts, GROUPS, homes, kept):
-        grads = finish(odd, own, returned, home, start, heads, width, grads)
+    for first, kept, home in sums:
+        grads = finish(kept, home, first, width, grads)
     dkey, dvalue = grads
     return (dquery, dkey, dvalue)
 

time: 103 us -> 110 us (1.068)
  waiting for transfers between devices: 27.4 us -> 47.4 us
  starting transfers between devices: 30.2 us -> 23.2 us
  other arithmetic: 5.69 us -> 0 us
  Pallas kernels: 37.5 us -> 35.7 us
  local copies, waits for them, and re-layouts: 0.04 us -> 1.81 us
    ppermute x6 -> x5, waiting for transfers between devices: 12.4 us -> 34.6 us  [shifted(): return lax.ppermute(x, AXES, pairs)]
    convert_element_type x3 -> x0, other arithmetic: 5.69 us -> none  [work(): send = (to_far.astype(jnp.float32) + extra).astype(jnp.bfloat16)]
    ppermute x6 -> x5, starting transfers between devices: 19.9 us -> 17 us  [shifted(): return lax.ppermute(x, AXES, pairs)]
    ppermute x3 -> x2, starting transfers between devices: 5.83 us -> 3.16 us  [to_odd(): return lax.ppermute(x, AXES, [(i, i + 1) for i in range(0, devices, 2)])]
    ppermute x3 -> x2, waiting for transfers between devices: 8.47 us -> 6.64 us  [to_even(): return lax.ppermute(x, AXES, [(i + 1, i) for i in range(0, devices, 2)])]
    cond x0 -> x4, local copies, waits for them, and re-layouts: none -> 1.76 us
    pallas_call x3 -> x2, Pallas kernels: 5.28 us -> 3.7 us  [pack(): pl.pallas_call(functools.partial(pack_kernel, first), in_specs=[pl.BlockS...]
    ppermute x3 -> x2, starting transfers between devices: 3.87 us -> 2.58 us  [to_even(): return lax.ppermute(x, AXES, [(i + 1, i) for i in range(0, devices, 2)])]
  transfers between devices with their start and end apart: 15 -> 12, of which waited for: 10 -> 8; matrix products, arithmetic and copies ran while one was open for 6% -> 0% of each run, Pallas kernels for 34% -> 29%
where the time goes in v2:
time: 110 us; the launch traced here: 109 us
  waiting for transfers between devices  47.4 us (43%)
  Pallas kernels  35.7 us (32%)
  starting transfers between devices  23.2 us (21%)
  local copies, waits for them, and re-layouts  1.81 us (2%)
    ppermute x5, waiting for transfers between devices, shifted(): return lax.ppermute(x, AXES, pairs)  34.6 us
    pallas_call x3, Pallas kernels, attend(): pl.pallas_call(functools.partial(kernel, rows, back, group, len(near) ==...  24.5 us
    ppermute x5, starting transfers between devices, shifted(): return lax.ppermute(x, AXES, pairs)  17 us
    ppermute x2, waiting for transfers between devices, to_even(): return lax.ppermute(x, AXES, [(i + 1, i) for i in range(0, devices, 2)])  6.64 us
    ppermute x3, waiting for transfers between devices, swapped(): return lax.ppermute(x, AXES, [(i, i ^ 1) for i in range(devices)])  6.19 us
    pallas_call x3, Pallas kernels, finish(): pl.pallas_call(functools.partial(finish_kernel, first), in_specs=in_specs...  5.1 us
    pallas_call x2, Pallas kernels, pack(): pl.pallas_call(functools.partial(pack_kernel, first), in_specs=[pl.BlockS...  3.7 us
    ppermute x2, starting transfers between devices, to_odd(): return lax.ppermute(x, AXES, [(i, i + 1) for i in range(0, devices, 2)])  3.16 us
  transfers between devices with their start and end apart: 12, of which 8 were waited for; matrix products, arithmetic and copies ran while one was open for 0% of the time, Pallas kernels for 29%

profile of v2, /device:TPU:14, one launch (start us, length us, event | category | flops | bytes accessed | tf_op | source)
XLA Modules:
  0.0 109.2 jit_solution(10370543856060764650)
XLA Ops:
  0.6 0.0 copy-start.6
  0.6 0.0 copy-start.7
  0.7 2.3 %pack.3 = bf16[512,1024]{1,0:T(8,128)(2,1)} custom-call(bf16[256,2048]{1,0:T(8,128)(2,1)} %k_ref.3, bf16[256,2048]{1,0:T(8,128)(2,1)} %v_ref.3), custom_call_target="tpu_custom_call" | custom-call | tf_op jit(solution)/shard_map/pack/pallas_call | solution.py:270
  3.0 0.0 copy-start.9
  3.0 0.0 copy-start.4
  3.0 0.0 copy-start.5
  3.0 1.4 %pack.2 = bf16[512,1024]{1,0:T(8,128)(2,1)S(1)} custom-call(bf16[256,2048]{1,0:T(8,128)(2,1)} %k_ref.3, bf16[256,2048]{1,0:T(8,128)(2,1)} %v_ref.3), custom_call_target="tpu_custom_call" | custom-call | tf_op jit(solution)/shard_map/pack/pallas_call | solution.py:270
  4.4 1.8 %collective-permute-start.6 = (bf16[512,1024]{1,0:T(8,128)(2,1)S(1)}, bf16[512,1024]{1,0:T(8,128)(2,1)S(1)}, u32[]{:S(2)}, u32[]{:S(2)}) collective-permute-start(bf16[512,1024]{1,0:T(8,128)(2,1)S(1)} %pack.2), channel_id=1, source_target_pairs={{0,1},{2,3},{4,5},{6,7},{8,9},{10,11},{12,13},{14,15},{16,17},{18,... | collective-permute-start | bytes 3145736 | tf_op jit(solution)/shard_map/ppermute | solution.py:40
  6.2 1.4 %collective-permute-start.7 = (bf16[512,1024]{1,0:T(8,128)(2,1)}, bf16[512,1024]{1,0:T(8,128)(2,1)S(1)}, u32[]{:S(2)}, u32[]{:S(2)}) collective-permute-start(bf16[512,1024]{1,0:T(8,128)(2,1)} %pack.3), channel_id=1, source_target_pairs={{0,1},{2,3},{4,5},{6,7},{8,9},{10,11},{12,13},{14,15},{16,17},{18,... | collective-permute-start | bytes 3145736 | tf_op jit(solution)/shard_map/ppermute | solution.py:40
  7.6 3.4 %collective-permute-start.5 = (bf16[512,1024]{1,0:T(8,128)(2,1)S(1)}, bf16[512,1024]{1,0:T(8,128)(2,1)S(1)}, u32[]{:S(2)}, u32[]{:S(2)}) collective-permute-start(bf16[512,1024]{1,0:T(8,128)(2,1)S(1)} %pack.2), channel_id=1, source_target_pairs={{0,2},{1,3},{2,4},{3,5},{4,6},{5,7},{6,8},{7,9},{8,10},{9,11},{10,... | collective-permute-start | bytes 3145736 | tf_op jit(solution)/shard_map/ppermute | solution.py:32
  11.0 3.4 %collective-permute-start.8 = (bf16[512,1024]{1,0:T(8,128)(2,1)}, bf16[512,1024]{1,0:T(8,128)(2,1)S(1)}, u32[]{:S(2)}, u32[]{:S(2)}) collective-permute-start(bf16[512,1024]{1,0:T(8,128)(2,1)} %pack.3), channel_id=1, source_target_pairs={{0,2},{1,3},{2,4},{3,5},{4,6},{5,7},{6,8},{7,9},{8,10},{9,11},{10,... | collective-permute-start | bytes 3145736 | tf_op jit(solution)/shard_map/ppermute | solution.py:32
  14.4 0.0 copy-done.9
  14.5 0.0 collective-permute-done.6
  14.5 0.0 collective-permute-done.7
  14.5 21.1 %collective-permute-done.5 = bf16[512,1024]{1,0:T(8,128)(2,1)S(1)} collective-permute-done((bf16[512,1024]{1,0:T(8,128)(2,1)S(1)}, bf16[512,1024]{1,0:T(8,128)(2,1)S(1)}, u32[]{:S(2)}, u32[]{:S(2)}) %collective-permute-start.5) | collective-permute-done | bytes 1048608 | tf_op jit(solution)/shard_map/ppermute | solution.py:32
  35.6 0.0 copy-done.6
  35.6 0.0 copy-done.7
  35.6 0.0 copy-done.4
  35.6 0.0 copy-done.5
  35.6 21.2 %conditional.3 = (bf16[256,4096]{1,0:T(8,128)(2,1)S(1)}, bf16[512,1024]{1,0:T(8,128)(2,1)}, bf16[512,1024]{1,0:T(8,128)(2,1)}) conditional(s32[]{:T(128)} %bitcast, () %tuple.35, (bf16[512,1024]{1,0:T(8,128)(2,1)S(1)}, s32[8]{0:T(128)S(1)}, bf16[256,4096]{1,0:T(8,128)(2,1)S(1)}, bf16[256,4096]{1,0:T(8,128)(2,1)S(1)}, bf16[256,2048]{1,0:T(8,128)(2,1)S(1)}, ...), branch_computations={%region_0.0_spmd, %region_1.0_spmd} | conditional | flops 2 | bytes 12583046 | solution.py:400
  35.6 1.3 %collective-permute-start = (bf16[512,1024]{1,0:T(8,128)(2,1)S(1)}, bf16[512,1024]{1,0:T(8,128)(2,1)S(1)}, u32[]{:S(2)}, u32[]{:S(2)}) collective-permute-start(bf16[512,1024]{1,0:T(8,128)(2,1)S(1)} %get-tuple-element.55.refs_4_.refs_5_), channel_id=1, source_target_pairs={{1,0},{3,2},{5,4},{7,6},{9,8},{11,10},{13,12},{15,14},{17,16},{19,... | collective-permute-start | bytes 3145736 | tf_op jit(solution)/shard_map/cond/branch_1_fun/ppermute | solution.py:44
  36.9 3.3 %collective-permute-done.refs_0_.refs_1_ = bf16[512,1024]{1,0:T(8,128)(2,1)S(1)} collective-permute-done((bf16[512,1024]{1,0:T(8,128)(2,1)S(1)}, bf16[512,1024]{1,0:T(8,128)(2,1)S(1)}, u32[]{:S(2)}, u32[]{:S(2)}) %collective-permute-start) | collective-permute-done | bytes 1048608 | tf_op jit(solution)/shard_map/cond/branch_1_fun/ppermute | solution.py:44
  40.2 11.6 %attend.3 = (bf16[256,4096]{1,0:T(8,128)(2,1)S(1)}, bf16[512,1024]{1,0:T(8,128)(2,1)S(1)}, bf16[512,1024]{1,0:T(8,128)(2,1)S(1)}, bf16[512,1024]{1,0:T(8,128)(2,1)S(1)}) custom-call(s32[8]{0:T(128)S(1)} %get-tuple-element.50.starts_ref, bf16[256,4096]{1,0:T(8,128)(2,1)S(1)} %get-tuple-element.51.q_ref, bf16[256,4096]{1,0:T(8,128)(2,1)S(1)} %get-tuple-element.52.g_ref, ...), custom_call_target="tpu_custom_call" | custom-call | flops 1 | bytes 1 | tf_op jit(solution)/shard_map/cond/branch_1_fun/attend/pallas_call | solution.py:234
  51.8 0.2 collective-permute-start.1
  52.0 2.5 %collective-permute-done.1.back_ref = bf16[512,1024]{1,0:T(8,128)(2,1)S(1)} collective-permute-done((bf16[512,1024]{1,0:T(8,128)(2,1)S(1)}, bf16[512,1024]{1,0:T(8,128)(2,1)S(1)}, u32[]{:S(2)}, u32[]{:S(2)}) %collective-permute-start.1) | collective-permute-done | bytes 1048608 | tf_op jit(solution)/shard_map/cond/branch_1_fun/ppermute | solution.py:36
  54.5 1.3 %merge.3 = (bf16[512,1024]{1,0:T(8,128)(2,1)}, bf16[512,1024]{1,0:T(8,128)(2,1)S(1)}) custom-call(bf16[512,1024]{1,0:T(8,128)(2,1)S(1)} %get-tuple-element.58.far_ref, bf16[512,1024]{1,0:T(8,128)(2,1)S(1)} %get-tuple-element.59.own_ref, bf16[512,1024]{1,0:T(8,128)(2,1)S(1)} %collective-permute-done.1.back_ref), custom_call_target="tpu_custom_call" | custom-call | flops 1 | bytes 1 | tf_op jit(solution)/shard_map/cond/branch_1_fun/merge/pallas_call | solution.py:307
  55.8 0.0 copy-start
  55.8 1.0 copy-done
  56.8 3.3 %collective-permute-start.11 = (bf16[512,1024]{1,0:T(8,128)(2,1)}, bf16[512,1024]{1,0:T(8,128)(2,1)}, u32[]{:S(2)}, u32[]{:S(2)}) collective-permute-start(bf16[512,1024]{1,0:T(8,128)(2,1)} %get-tuple-element.126), channel_id=1, source_target_pairs={{2,0},{3,1},{4,2},{5,3},{6,4},{7,5},{8,6},{9,7},{10,8},{11,9},{12,... | collective-permute-start | bytes 3145736 | tf_op jit(solution)/shard_map/ppermute | solution.py:32
  60.1 0.0 collective-permute-done.8
  60.1 14.8 %conditional.4 = (bf16[512,1024]{1,0:T(8,128)(2,1)}, bf16[256,4096]{1,0:T(8,128)(2,1)S(1)}, bf16[512,512]{1,0:T(8,128)(2,1)}, bf16[512,512]{1,0:T(8,128)(2,1)}) conditional(s32[]{:T(128)} %bitcast, bf16[256,4096]{1,0:T(8,128)(2,1)S(1)} %get-tuple-element.117, (bf16[512,1024]{1,0:T(8,128)(2,1)S(1)}, s32[8]{0:T(128)S(1)}, bf16[256,4096]{1,0:T(8,128)(2,1)}, ...), branch_computations={%region_2.0_spmd, %region_3.0_spmd} | conditional | flops 2 | bytes 8388750 | solution.py:400
  60.1 1.3 %collective-permute-start.2 = (bf16[512,1024]{1,0:T(8,128)(2,1)S(1)}, bf16[512,1024]{1,0:T(8,128)(2,1)}, u32[]{:S(2)}, u32[]{:S(2)}) collective-permute-start(bf16[512,1024]{1,0:T(8,128)(2,1)S(1)} %get-tuple-element.63.refs_4_.refs_5_), channel_id=1, source_target_pairs={{1,0},{3,2},{5,4},{7,6},{9,8},{11,10},{13,12},{15,14},{17,16},{19,... | collective-permute-start | bytes 3145736 | tf_op jit(solution)/shard_map/cond/branch_1_fun/ppermute | solution.py:44
  61.4 3.4 %collective-permute-done.2.refs_0_.refs_1_ = bf16[512,1024]{1,0:T(8,128)(2,1)} collective-permute-done((bf16[512,1024]{1,0:T(8,128)(2,1)S(1)}, bf16[512,1024]{1,0:T(8,128)(2,1)}, u32[]{:S(2)}, u32[]{:S(2)}) %collective-permute-start.2) | collective-permute-done | bytes 1048608 | tf_op jit(solution)/shard_map/cond/branch_1_fun/ppermute | solution.py:44
  64.8 6.4 %attend.4 = (bf16[256,4096]{1,0:T(8,128)(2,1)S(1)}, bf16[512,512]{1,0:T(8,128)(2,1)S(1)}, bf16[512,512]{1,0:T(8,128)(2,1)S(1)}, bf16[512,512]{1,0:T(8,128)(2,1)S(1)}) custom-call(s32[8]{0:T(128)S(1)} %get-tuple-element.64.starts_ref, bf16[256,4096]{1,0:T(8,128)(2,1)} %get-tuple-element.65.q_ref, ...), custom_call_target="tpu_custom_call", output_to_operand_aliasing={{0}: (11, {})} | custom-call | flops 1 | bytes 1 | tf_op jit(solution)/shard_map/cond/branch_1_fun/attend/pallas_call | solution.py:234
  71.2 0.2 collective-permute-start.3
  71.4 1.8 %collective-permute-done.3.back_ref = bf16[512,512]{1,0:T(8,128)(2,1)S(1)} collective-permute-done((bf16[512,512]{1,0:T(8,128)(2,1)S(1)}, bf16[512,512]{1,0:T(8,128)(2,1)S(1)}, u32[]{:S(2)}, u32[]{:S(2)}) %collective-permute-start.3) | collective-permute-done | bytes 524320 | tf_op jit(solution)/shard_map/cond/branch_1_fun/ppermute | solution.py:36
  73.1 0.9 merge.4
  74.1 0.0 copy-start.2
  74.1 0.8 copy-done.2
  74.9 2.5 %collective-permute-start.10 = (bf16[512,512]{1,0:T(8,128)(2,1)}, bf16[512,512]{1,0:T(8,128)(2,1)}, u32[]{:S(2)}, u32[]{:S(2)}) collective-permute-start(bf16[512,512]{1,0:T(8,128)(2,1)} %get-tuple-element.124), channel_id=1, source_target_pairs={{2,0},{3,1},{4,2},{5,3},{6,4},{7,5},{8,6},{9,7},{10,8},{11,9},{12,... | collective-permute-start | bytes 1572872 | tf_op jit(solution)/shard_map/ppermute | solution.py:32
  77.4 0.0 copy-start.1
  77.4 8.7 %conditional.5 = (bf16[256,4096]{1,0:T(8,128)(2,1)S(1)}, bf16[512,512]{1,0:T(8,128)(2,1)S(1)}, bf16[512,512]{1,0:T(8,128)(2,1)S(1)}) conditional(s32[]{:T(128)} %bitcast, bf16[256,4096]{1,0:T(8,128)(2,1)S(1)} %get-tuple-element.118, (s32[8]{0:T(128)S(1)}, bf16[256,4096]{1,0:T(8,128)(2,1)}, bf16[256,4096]{1,0:T(8,128)(2,1)}, ...), branch_computations={%region_4.0_spmd, %region_5.0_spmd} | conditional | flops 2 | bytes 2097218 | solution.py:400
  77.4 6.6 %attend.5 = (bf16[256,4096]{1,0:T(8,128)(2,1)S(1)}, bf16[512,512]{1,0:T(8,128)(2,1)S(1)}, bf16[512,512]{1,0:T(8,128)(2,1)S(1)}, bf16[512,512]{1,0:T(8,128)(2,1)S(1)}) custom-call(s32[8]{0:T(128)S(1)} %get-tuple-element.77.starts_ref, bf16[256,4096]{1,0:T(8,128)(2,1)} %get-tuple-element.78.q_ref, ...), custom_call_target="tpu_custom_call", output_to_operand_aliasing={{0}: (11, {})} | custom-call | flops 1 | bytes 1 | tf_op jit(solution)/shard_map/cond/branch_1_fun/attend/pallas_call | solution.py:234
  84.0 0.1 collective-permute-start.4
  84.1 1.9 %collective-permute-done.4.back_ref = bf16[512,512]{1,0:T(8,128)(2,1)S(1)} collective-permute-done((bf16[512,512]{1,0:T(8,128)(2,1)S(1)}, bf16[512,512]{1,0:T(8,128)(2,1)S(1)}, u32[]{:S(2)}, u32[]{:S(2)}) %collective-permute-start.4) | collective-permute-done | bytes 524320 | tf_op jit(solution)/shard_map/cond/branch_1_fun/ppermute | solution.py:36
  86.0 0.2 merge.5
  86.1 0.0 copy-start.8
  86.1 0.0 copy-start.3
  86.1 4.3 %collective-permute-start.9 = (bf16[512,512]{1,0:T(8,128)(2,1)S(1)}, bf16[512,512]{1,0:T(8,128)(2,1)S(1)}, u32[]{:S(2)}, u32[]{:S(2)}) collective-permute-start(bf16[512,512]{1,0:T(8,128)(2,1)S(1)} %get-tuple-element.122), channel_id=1, source_target_pairs={{2,0},{3,1},{4,2},{5,3},{6,4},{7,5},{8,6},{9,7},{10,8},{11,9},{12,... | collective-permute-start | bytes 1572872 | tf_op jit(solution)/shard_map/ppermute | solution.py:32
  90.5 0.0 collective-permute-done.11.home_ref
  90.5 0.0 copy-done.1
  90.5 2.3 %finish.3 = (bf16[256,2048]{1,0:T(8,128)(2,1)}, bf16[256,2048]{1,0:T(8,128)(2,1)}) custom-call(bf16[512,1024]{1,0:T(8,128)(2,1)S(1)} %copy-done.1, bf16[512,1024]{1,0:T(8,128)(2,1)} %collective-permute-done.11.home_ref), custom_call_target="tpu_custom_call" | custom-call | flops 1 | bytes 1 | tf_op jit(solution)/shard_map/finish/pallas_call | solution.py:343
  92.8 5.2 %collective-permute-done.10.home_ref = bf16[512,512]{1,0:T(8,128)(2,1)} collective-permute-done((bf16[512,512]{1,0:T(8,128)(2,1)}, bf16[512,512]{1,0:T(8,128)(2,1)}, u32[]{:S(2)}, u32[]{:S(2)}) %collective-permute-start.10) | collective-permute-done | bytes 524320 | tf_op jit(solution)/shard_map/ppermute | solution.py:32
  98.0 0.0 copy-done.3
  98.0 1.9 %finish.4 = (bf16[256,2048]{1,0:T(8,128)(2,1)}, bf16[256,2048]{1,0:T(8,128)(2,1)}) custom-call(bf16[512,512]{1,0:T(8,128)(2,1)S(1)} %copy-done.3, bf16[512,512]{1,0:T(8,128)(2,1)} %collective-permute-done.10.home_ref, bf16[256,2048]{1,0:T(8,128)(2,1)} %get-tuple-element.127.refs_0_, ...), custom_call_target="tpu_custom_call", output_to_operand_aliasing={{0}: (2, {}), {1}: (3, {})} | custom-call | flops 1 | bytes 1 | tf_op jit(solution)/shard_map/finish/pallas_call | solution.py:343
  99.9 0.0 copy-done.8
  99.9 8.4 %collective-permute-done.9.home_ref = bf16[512,512]{1,0:T(8,128)(2,1)S(1)} collective-permute-done((bf16[512,512]{1,0:T(8,128)(2,1)S(1)}, bf16[512,512]{1,0:T(8,128)(2,1)S(1)}, u32[]{:S(2)}, u32[]{:S(2)}) %collective-permute-start.9) | collective-permute-done | bytes 524320 | tf_op jit(solution)/shard_map/ppermute | solution.py:32
  108.3 0.9 finish.5
Async XLA Ops:
  0.6 35.0 %copy-start.6 = (bf16[256,4096]{1,0:T(8,128)(2,1)S(1)}, bf16[256,4096]{1,0:T(8,128)(2,1)}, u32[]{:S(2)}) copy-start(bf16[256,4096]{1,0:T(8,128)(2,1)} %param.11) | copy-start | bytes 6291460
  0.6 34.9 %copy-start.7 = (bf16[256,4096]{1,0:T(8,128)(2,1)S(1)}, bf16[256,4096]{1,0:T(8,128)(2,1)}, u32[]{:S(2)}) copy-start(bf16[256,4096]{1,0:T(8,128)(2,1)} %param.14) | copy-start | bytes 6291460
  3.0 11.4 %copy-start.9 = (s32[8]{0:T(128)S(1)}, s32[8]{0:T(128)}, u32[]{:S(2)}) copy-start(s32[8]{0:T(128)} %param.15) | copy-start | bytes 100
  3.0 32.6 %copy-start.4 = (bf16[256,2048]{1,0:T(8,128)(2,1)S(1)}, bf16[256,2048]{1,0:T(8,128)(2,1)}, u32[]{:S(2)}) copy-start(bf16[256,2048]{1,0:T(8,128)(2,1)} %k_ref.3) | copy-start | bytes 3145732
  3.0 32.6 %copy-start.5 = (bf16[256,2048]{1,0:T(8,128)(2,1)S(1)}, bf16[256,2048]{1,0:T(8,128)(2,1)}, u32[]{:S(2)}) copy-start(bf16[256,2048]{1,0:T(8,128)(2,1)} %v_ref.3) | copy-start | bytes 3145732
  4.4 10.1 %collective-permute-start.6 = (bf16[512,1024]{1,0:T(8,128)(2,1)S(1)}, bf16[512,1024]{1,0:T(8,128)(2,1)S(1)}, u32[]{:S(2)}, u32[]{:S(2)}) collective-permute-start(bf16[512,1024]{1,0:T(8,128)(2,1)S(1)} %pack.2), channel_id=1, source_target_pairs={{0,1},{2,3},{4,5},{6,7},{8,9},{10,11},{12,13},{14,15},{16,17},{18,... | collective-permute-start | bytes 3145736 | tf_op jit(solution)/shard_map/ppermute | solution.py:40
  6.2 8.3 %collective-permute-start.7 = (bf16[512,1024]{1,0:T(8,128)(2,1)}, bf16[512,1024]{1,0:T(8,128)(2,1)S(1)}, u32[]{:S(2)}, u32[]{:S(2)}) collective-permute-start(bf16[512,1024]{1,0:T(8,128)(2,1)} %pack.3), channel_id=1, source_target_pairs={{0,1},{2,3},{4,5},{6,7},{8,9},{10,11},{12,13},{14,15},{16,17},{18,... | collective-permute-start | bytes 3145736 | tf_op jit(solution)/shard_map/ppermute | solution.py:40
  7.6 28.0 %collective-permute-start.5 = (bf16[512,1024]{1,0:T(8,128)(2,1)S(1)}, bf16[512,1024]{1,0:T(8,128)(2,1)S(1)}, u32[]{:S(2)}, u32[]{:S(2)}) collective-permute-start(bf16[512,1024]{1,0:T(8,128)(2,1)S(1)} %pack.2), channel_id=1, source_target_pairs={{0,2},{1,3},{2,4},{3,5},{4,6},{5,7},{6,8},{7,9},{8,10},{9,11},{10,... | collective-permute-start | bytes 3145736 | tf_op jit(solution)/shard_map/ppermute | solution.py:32
  11.0 49.1 %collective-permute-start.8 = (bf16[512,1024]{1,0:T(8,128)(2,1)}, bf16[512,1024]{1,0:T(8,128)(2,1)S(1)}, u32[]{:S(2)}, u32[]{:S(2)}) collective-permute-start(bf16[512,1024]{1,0:T(8,128)(2,1)} %pack.3), channel_id=1, source_target_pairs={{0,2},{1,3},{2,4},{3,5},{4,6},{5,7},{6,8},{7,9},{8,10},{9,11},{10,... | collective-permute-start | bytes 3145736 | tf_op jit(solution)/shard_map/ppermute | solution.py:32
  35.6 4.6 %collective-permute-start = (bf16[512,1024]{1,0:T(8,128)(2,1)S(1)}, bf16[512,1024]{1,0:T(8,128)(2,1)S(1)}, u32[]{:S(2)}, u32[]{:S(2)}) collective-permute-start(bf16[512,1024]{1,0:T(8,128)(2,1)S(1)} %get-tuple-element.55.refs_4_.refs_5_), channel_id=1, source_target_pairs={{1,0},{3,2},{5,4},{7,6},{9,8},{11,10},{13,12},{15,14},{17,16},{19,... | collective-permute-start | bytes 3145736 | tf_op jit(solution)/shard_map/cond/branch_1_fun/ppermute | solution.py:44
  51.8 2.7 %collective-permute-start.1 = (bf16[512,1024]{1,0:T(8,128)(2,1)S(1)}, bf16[512,1024]{1,0:T(8,128)(2,1)S(1)}, u32[]{:S(2)}, u32[]{:S(2)}) collective-permute-start(bf16[512,1024]{1,0:T(8,128)(2,1)S(1)} %get-tuple-element.60), channel_id=1, source_target_pairs={{0,1},{1,0},{2,3},{3,2},{4,5},{5,4},{6,7},{7,6},{8,9},{9,8},{10,11... | collective-permute-start | bytes 3145736 | tf_op jit(solution)/shard_map/cond/branch_1_fun/ppermute | solution.py:36
  55.8 1.0 copy-start
  56.8 33.7 %collective-permute-start.11 = (bf16[512,1024]{1,0:T(8,128)(2,1)}, bf16[512,1024]{1,0:T(8,128)(2,1)}, u32[]{:S(2)}, u32[]{:S(2)}) collective-permute-start(bf16[512,1024]{1,0:T(8,128)(2,1)} %get-tuple-element.126), channel_id=1, source_target_pairs={{2,0},{3,1},{4,2},{5,3},{6,4},{7,5},{8,6},{9,7},{10,8},{11,9},{12,... | collective-permute-start | bytes 3145736 | tf_op jit(solution)/shard_map/ppermute | solution.py:32
  60.1 4.7 %collective-permute-start.2 = (bf16[512,1024]{1,0:T(8,128)(2,1)S(1)}, bf16[512,1024]{1,0:T(8,128)(2,1)}, u32[]{:S(2)}, u32[]{:S(2)}) collective-permute-start(bf16[512,1024]{1,0:T(8,128)(2,1)S(1)} %get-tuple-element.63.refs_4_.refs_5_), channel_id=1, source_target_pairs={{1,0},{3,2},{5,4},{7,6},{9,8},{11,10},{13,12},{15,14},{17,16},{19,... | collective-permute-start | bytes 3145736 | tf_op jit(solution)/shard_map/cond/branch_1_fun/ppermute | solution.py:44
  71.2 2.0 %collective-permute-start.3 = (bf16[512,512]{1,0:T(8,128)(2,1)S(1)}, bf16[512,512]{1,0:T(8,128)(2,1)S(1)}, u32[]{:S(2)}, u32[]{:S(2)}) collective-permute-start(bf16[512,512]{1,0:T(8,128)(2,1)S(1)} %get-tuple-element.74), channel_id=1, source_target_pairs={{0,1},{1,0},{2,3},{3,2},{4,5},{5,4},{6,7},{7,6},{8,9},{9,8},{10,11... | collective-permute-start | bytes 1572872 | tf_op jit(solution)/shard_map/cond/branch_1_fun/ppermute | solution.py:36
  74.1 0.8 copy-start.2
  74.9 23.1 %collective-permute-start.10 = (bf16[512,512]{1,0:T(8,128)(2,1)}, bf16[512,512]{1,0:T(8,128)(2,1)}, u32[]{:S(2)}, u32[]{:S(2)}) collective-permute-start(bf16[512,512]{1,0:T(8,128)(2,1)} %get-tuple-element.124), channel_id=1, source_target_pairs={{2,0},{3,1},{4,2},{5,3},{6,4},{7,5},{8,6},{9,7},{10,8},{11,9},{12,... | collective-permute-start | bytes 1572872 | tf_op jit(solution)/shard_map/ppermute | solution.py:32
  77.4 13.1 %copy-start.1 = (bf16[512,1024]{1,0:T(8,128)(2,1)S(1)}, bf16[512,1024]{1,0:T(8,128)(2,1)}, u32[]{:S(2)}) copy-start(bf16[512,1024]{1,0:T(8,128)(2,1)} %get-tuple-element.125.kept_ref) | copy-start | bytes 3145732
  84.0 2.0 %collective-permute-start.4 = (bf16[512,512]{1,0:T(8,128)(2,1)S(1)}, bf16[512,512]{1,0:T(8,128)(2,1)S(1)}, u32[]{:S(2)}, u32[]{:S(2)}) collective-permute-start(bf16[512,512]{1,0:T(8,128)(2,1)S(1)} %get-tuple-element.89), channel_id=1, source_target_pairs={{0,1},{1,0},{2,3},{3,2},{4,5},{5,4},{6,7},{7,6},{8,9},{9,8},{10,11... | collective-permute-start | bytes 1572872 | tf_op jit(solution)/shard_map/cond/branch_1_fun/ppermute | solution.py:36
  86.1 13.8 %copy-start.8 = (bf16[256,4096]{1,0:T(8,128)(2,1)}, bf16[256,4096]{1,0:T(8,128)(2,1)S(1)}, u32[]{:S(2)}) copy-start(bf16[256,4096]{1,0:T(8,128)(2,1)S(1)} %get-tuple-element.111) | copy-start | bytes 6291460
  86.1 11.9 %copy-start.3 = (bf16[512,512]{1,0:T(8,128)(2,1)S(1)}, bf16[512,512]{1,0:T(8,128)(2,1)}, u32[]{:S(2)}) copy-start(bf16[512,512]{1,0:T(8,128)(2,1)} %get-tuple-element.123.kept_ref) | copy-start | bytes 1572868
  86.1 22.2 %collective-permute-start.9 = (bf16[512,512]{1,0:T(8,128)(2,1)S(1)}, bf16[512,512]{1,0:T(8,128)(2,1)S(1)}, u32[]{:S(2)}, u32[]{:S(2)}) collective-permute-start(bf16[512,512]{1,0:T(8,128)(2,1)S(1)} %get-tuple-element.122), channel_id=1, source_target_pairs={{2,0},{3,1},{4,2},{5,3},{6,4},{7,5},{8,6},{9,7},{10,8},{11,9},{12,... | collective-permute-start | bytes 1572872 | tf_op jit(solution)/shard_map/ppermute | solution.py:32

commit v3 on v2

--- a/solution.py
+++ b/solution.py
@@ -11,7 +11,7 @@
 HEAD_SIZE = 128
 WINDOW_LENGTH = 512
 AXES = ("seq", "head")
-GROUPS = ((8,), (4, 4))
+GROUPS = ((6,), (6,), (4,))
 STEP = 2
 UNIT = 128
 STRIP = 32
@@ -374,8 +374,8 @@
     starts = [sum(map(sum, GROUPS[:c])) for c in range(len(GROUPS))]
     packed = [pack(keys, values, start, sum(group), 1)[0] for start, group in zip(starts, GROUPS)]
     far = [shifted(x, 2, devices) for x in packed]
-    early = [to_odd(after(x, *packed), devices) for x in packed]
-    far[0] = after(far[0], *early)
+    early = [to_odd(x, devices) for x in packed]
+    far[0] = after(far[0], early[-1])
 
     def work(start, first, heads, received, own_near, near, dquery):
         if near is None:
@@ -406,6 +406,8 @@
                 near,
                 dquery,
             )
+            if len(sums) == 1:
+                send = after(send, *far)
             sums.append((first, kept, shifted(send, -2, devices)))
             first += heads
     grads = None

time: 110 us -> 115 us (1.045)
  starting transfers between devices: 23.2 us -> 29.2 us
    ppermute x5 -> x6, starting transfers between devices: 17 us -> 20.3 us  [shifted(): return lax.ppermute(x, AXES, pairs)]
    ppermute x5 -> x6, waiting for transfers between devices: 34.6 us -> 32.9 us  [shifted(): return lax.ppermute(x, AXES, pairs)]
    ppermute x2 -> x3, waiting for transfers between devices: 6.64 us -> 8.26 us  [to_even(): return lax.ppermute(x, AXES, [(i + 1, i) for i in range(0, devices, 2)])]
    pallas_call x2 -> x3, Pallas kernels: 3.7 us -> 5.29 us  [pack(): pl.pallas_call(functools.partial(pack_kernel, first), in_specs=[pl.BlockS...]
    ppermute x2 -> x3, starting transfers between devices: 3.16 us -> 4.45 us  [to_odd(): return lax.ppermute(x, AXES, [(i, i + 1) for i in range(0, devices, 2)])]
    ppermute x2 -> x3, starting transfers between devices: 2.58 us -> 3.86 us  [to_even(): return lax.ppermute(x, AXES, [(i + 1, i) for i in range(0, devices, 2)])]
  transfers between devices with their start and end apart: 12 -> 15, of which waited for: 8 -> 11; matrix products, arithmetic and copies ran while one was open for 0% -> 0% of each run, Pallas kernels for 29% -> 29%
where the time goes in v3:
time: 115 us; the launch traced here: 114 us
  waiting for transfers between devices  47.2 us (41%)
  Pallas kernels  35.8 us (31%)
  starting transfers between devices  29.2 us (25%)
    ppermute x6, waiting for transfers between devices, shifted(): return lax.ppermute(x, AXES, pairs)  32.9 us
    pallas_call x3, Pallas kernels, attend(): pl.pallas_call(functools.partial(kernel, rows, back, group, len(near) ==...  23.9 us
    ppermute x6, starting transfers between devices, shifted(): return lax.ppermute(x, AXES, pairs)  20.3 us
    ppermute x3, waiting for transfers between devices, to_even(): return lax.ppermute(x, AXES, [(i + 1, i) for i in range(0, devices, 2)])  8.26 us
    ppermute x3, waiting for transfers between devices, swapped(): return lax.ppermute(x, AXES, [(i, i ^ 1) for i in range(devices)])  6.07 us
    pallas_call x3, Pallas kernels, pack(): pl.pallas_call(functools.partial(pack_kernel, first), in_specs=[pl.BlockS...  5.29 us
    pallas_call x3, Pallas kernels, finish(): pl.pallas_call(functools.partial(finish_kernel, first), in_specs=in_specs...  5.1 us
    ppermute x3, starting transfers between devices, to_odd(): return lax.ppermute(x, AXES, [(i, i + 1) for i in range(0, devices, 2)])  4.45 us
  transfers between devices with their start and end apart: 15, of which 11 were waited for; matrix products, arithmetic and copies ran while one was open for 0% of the time, Pallas kernels for 29%

profile of v3, /device:TPU:14, one launch (start us, length us, event | category | flops | bytes accessed | tf_op | source)
XLA Modules:
  0.0 114.1 jit_solution(4328640039694234415)
XLA Ops:
  0.6 0.0 copy-start.5
  0.6 2.0 %pack.4 = bf16[512,512]{1,0:T(8,128)(2,1)} custom-call(bf16[256,2048]{1,0:T(8,128)(2,1)} %k_ref.5, bf16[256,2048]{1,0:T(8,128)(2,1)} %v_ref.5), custom_call_target="tpu_custom_call" | custom-call | tf_op jit(solution)/shard_map/pack/pallas_call | solution.py:270
  2.6 1.8 %collective-permute-start.7 = (bf16[512,512]{1,0:T(8,128)(2,1)}, bf16[512,512]{1,0:T(8,128)(2,1)S(1)}, u32[]{:S(2)}, u32[]{:S(2)}) collective-permute-start(bf16[512,512]{1,0:T(8,128)(2,1)} %pack.4), channel_id=1, source_target_pairs={{0,1},{2,3},{4,5},{6,7},{8,9},{10,11},{12,13},{14,15},{16,17},{18,... | collective-permute-start | bytes 1572872 | tf_op jit(solution)/shard_map/ppermute | solution.py:40
  4.4 0.0 copy-start.4
  4.4 1.3 %pack.3 = bf16[512,768]{1,0:T(8,128)(2,1)S(1)} custom-call(bf16[256,2048]{1,0:T(8,128)(2,1)} %k_ref.5, bf16[256,2048]{1,0:T(8,128)(2,1)} %v_ref.5), custom_call_target="tpu_custom_call" | custom-call | tf_op jit(solution)/shard_map/pack/pallas_call | solution.py:270
  5.7 0.0 copy-start.6
  5.7 0.0 copy-start.1
  5.7 0.0 copy-start.2
  5.8 3.5 %collective-permute-start.6 = (bf16[512,768]{1,0:T(8,128)(2,1)S(1)}, bf16[512,768]{1,0:T(8,128)(2,1)S(1)}, u32[]{:S(2)}, u32[]{:S(2)}) collective-permute-start(bf16[512,768]{1,0:T(8,128)(2,1)S(1)} %pack.3), channel_id=1, source_target_pairs={{0,2},{1,3},{2,4},{3,5},{4,6},{5,7},{6,8},{7,9},{8,10},{9,11},{10,... | collective-permute-start | bytes 2359304 | tf_op jit(solution)/shard_map/ppermute | solution.py:32
  9.3 1.3 %collective-permute-start.8 = (bf16[512,768]{1,0:T(8,128)(2,1)S(1)}, bf16[512,768]{1,0:T(8,128)(2,1)S(1)}, u32[]{:S(2)}, u32[]{:S(2)}) collective-permute-start(bf16[512,768]{1,0:T(8,128)(2,1)S(1)} %pack.3), channel_id=1, source_target_pairs={{0,1},{2,3},{4,5},{6,7},{8,9},{10,11},{12,13},{14,15},{16,17},{18,... | collective-permute-start | bytes 2359304 | tf_op jit(solution)/shard_map/ppermute | solution.py:40
  10.6 2.0 %pack.5 = bf16[512,768]{1,0:T(8,128)(2,1)} custom-call(bf16[256,2048]{1,0:T(8,128)(2,1)} %k_ref.5, bf16[256,2048]{1,0:T(8,128)(2,1)} %v_ref.5), custom_call_target="tpu_custom_call" | custom-call | tf_op jit(solution)/shard_map/pack/pallas_call | solution.py:270
  12.7 1.3 %collective-permute-start.10 = (bf16[512,768]{1,0:T(8,128)(2,1)}, bf16[512,768]{1,0:T(8,128)(2,1)S(1)}, u32[]{:S(2)}, u32[]{:S(2)}) collective-permute-start(bf16[512,768]{1,0:T(8,128)(2,1)} %pack.5), channel_id=1, source_target_pairs={{0,1},{2,3},{4,5},{6,7},{8,9},{10,11},{12,13},{14,15},{16,17},{18,... | collective-permute-start | bytes 2359304 | tf_op jit(solution)/shard_map/ppermute | solution.py:40
  14.0 3.4 %collective-permute-start.9 = (bf16[512,768]{1,0:T(8,128)(2,1)}, bf16[512,768]{1,0:T(8,128)(2,1)S(1)}, u32[]{:S(2)}, u32[]{:S(2)}) collective-permute-start(bf16[512,768]{1,0:T(8,128)(2,1)} %pack.5), channel_id=1, source_target_pairs={{0,2},{1,3},{2,4},{3,5},{4,6},{5,7},{6,8},{7,9},{8,10},{9,11},{10,... | collective-permute-start | bytes 2359304 | tf_op jit(solution)/shard_map/ppermute | solution.py:32
  17.5 0.0 collective-permute-done.7
  17.5 3.3 %collective-permute-start.11 = (bf16[512,512]{1,0:T(8,128)(2,1)}, bf16[512,512]{1,0:T(8,128)(2,1)S(1)}, u32[]{:S(2)}, u32[]{:S(2)}) collective-permute-start(bf16[512,512]{1,0:T(8,128)(2,1)} %pack.4), channel_id=1, source_target_pairs={{0,2},{1,3},{2,4},{3,5},{4,6},{5,7},{6,8},{7,9},{8,10},{9,11},{10,... | collective-permute-start | bytes 1572872 | tf_op jit(solution)/shard_map/ppermute | solution.py:32
  20.8 0.0 copy-done.6
  20.9 7.4 %collective-permute-done.6 = bf16[512,768]{1,0:T(8,128)(2,1)S(1)} collective-permute-done((bf16[512,768]{1,0:T(8,128)(2,1)S(1)}, bf16[512,768]{1,0:T(8,128)(2,1)S(1)}, u32[]{:S(2)}, u32[]{:S(2)}) %collective-permute-start.6) | collective-permute-done | bytes 786464 | tf_op jit(solution)/shard_map/ppermute | solution.py:32
  28.3 0.0 collective-permute-done.8
  28.3 0.0 copy-done.5
  28.3 0.0 copy-done.4
  28.3 0.0 copy-done.1
  28.3 0.0 copy-done.2
  28.3 16.3 %conditional.3 = (bf16[256,4096]{1,0:T(8,128)(2,1)S(1)}, bf16[512,768]{1,0:T(8,128)(2,1)}, bf16[512,768]{1,0:T(8,128)(2,1)S(1)}) conditional(s32[]{:T(128)} %bitcast, () %tuple.34, (bf16[512,768]{1,0:T(8,128)(2,1)S(1)}, s32[8]{0:T(128)S(1)}, bf16[256,4096]{1,0:T(8,128)(2,1)S(1)}, bf16[256,4096]{1,0:T(8,128)(2,1)S(1)}, ...), branch_computations={%region_0.0_spmd, %region_1.0_spmd} | conditional | flops 2 | bytes 9437318 | solution.py:400
  28.3 1.3 %collective-permute-start = (bf16[512,768]{1,0:T(8,128)(2,1)S(1)}, bf16[512,768]{1,0:T(8,128)(2,1)S(1)}, u32[]{:S(2)}, u32[]{:S(2)}) collective-permute-start(bf16[512,768]{1,0:T(8,128)(2,1)S(1)} %get-tuple-element.53.refs_4_.refs_5_), channel_id=1, source_target_pairs={{1,0},{3,2},{5,4},{7,6},{9,8},{11,10},{13,12},{15,14},{17,16},{19,... | collective-permute-start | bytes 2359304 | tf_op jit(solution)/shard_map/cond/branch_1_fun/ppermute | solution.py:44
  29.6 2.9 %collective-permute-done.refs_0_.refs_1_ = bf16[512,768]{1,0:T(8,128)(2,1)S(1)} collective-permute-done((bf16[512,768]{1,0:T(8,128)(2,1)S(1)}, bf16[512,768]{1,0:T(8,128)(2,1)S(1)}, u32[]{:S(2)}, u32[]{:S(2)}) %collective-permute-start) | collective-permute-done | bytes 786464 | tf_op jit(solution)/shard_map/cond/branch_1_fun/ppermute | solution.py:44
  32.5 8.6 %attend.3 = (bf16[256,4096]{1,0:T(8,128)(2,1)S(1)}, bf16[512,768]{1,0:T(8,128)(2,1)S(1)}, bf16[512,768]{1,0:T(8,128)(2,1)S(1)}, bf16[512,768]{1,0:T(8,128)(2,1)S(1)}) custom-call(s32[8]{0:T(128)S(1)} %get-tuple-element.48.starts_ref, bf16[256,4096]{1,0:T(8,128)(2,1)S(1)} %get-tuple-element.49.q_ref, bf16[256,4096]{1,0:T(8,128)(2,1)S(1)} %get-tuple-element.50.g_ref, ...), custom_call_target="tpu_custom_call" | custom-call | flops 1 | bytes 1 | tf_op jit(solution)/shard_map/cond/branch_1_fun/attend/pallas_call | solution.py:234
  41.1 0.2 collective-permute-start.1
  41.3 2.2 %collective-permute-done.1.back_ref = bf16[512,768]{1,0:T(8,128)(2,1)S(1)} collective-permute-done((bf16[512,768]{1,0:T(8,128)(2,1)S(1)}, bf16[512,768]{1,0:T(8,128)(2,1)S(1)}, u32[]{:S(2)}, u32[]{:S(2)}) %collective-permute-start.1) | collective-permute-done | bytes 786464 | tf_op jit(solution)/shard_map/cond/branch_1_fun/ppermute | solution.py:36
  43.4 0.2 merge.3
  43.7 0.0 copy-start
  43.7 0.9 copy-done
  44.5 0.0 collective-permute-done.10
  44.6 0.6 collective-permute-done.9
  45.1 16.6 %conditional.4 = (bf16[256,4096]{1,0:T(8,128)(2,1)S(1)}, bf16[512,768]{1,0:T(8,128)(2,1)}, bf16[512,768]{1,0:T(8,128)(2,1)S(1)}) conditional(s32[]{:T(128)} %bitcast, bf16[256,4096]{1,0:T(8,128)(2,1)S(1)} %get-tuple-element.110, (bf16[512,768]{1,0:T(8,128)(2,1)S(1)}, s32[8]{0:T(128)S(1)}, bf16[256,4096]{1,0:T(8,128)(2,1)}, ...), branch_computations={%region_2.0_spmd, %region_3.0_spmd} | conditional | flops 2 | bytes 6291562 | solution.py:400
  45.1 1.3 %collective-permute-start.2 = (bf16[512,768]{1,0:T(8,128)(2,1)S(1)}, bf16[512,768]{1,0:T(8,128)(2,1)S(1)}, u32[]{:S(2)}, u32[]{:S(2)}) collective-permute-start(bf16[512,768]{1,0:T(8,128)(2,1)S(1)} %get-tuple-element.66.refs_4_.refs_5_), channel_id=1, source_target_pairs={{1,0},{3,2},{5,4},{7,6},{9,8},{11,10},{13,12},{15,14},{17,16},{19,... | collective-permute-start | bytes 2359304 | tf_op jit(solution)/shard_map/cond/branch_1_fun/ppermute | solution.py:44
  46.4 2.9 %collective-permute-done.2.refs_0_.refs_1_ = bf16[512,768]{1,0:T(8,128)(2,1)S(1)} collective-permute-done((bf16[512,768]{1,0:T(8,128)(2,1)S(1)}, bf16[512,768]{1,0:T(8,128)(2,1)S(1)}, u32[]{:S(2)}, u32[]{:S(2)}) %collective-permute-start.2) | collective-permute-done | bytes 786464 | tf_op jit(solution)/shard_map/cond/branch_1_fun/ppermute | solution.py:44
  49.3 9.0 %attend.4 = (bf16[256,4096]{1,0:T(8,128)(2,1)S(1)}, bf16[512,768]{1,0:T(8,128)(2,1)S(1)}, bf16[512,768]{1,0:T(8,128)(2,1)S(1)}, bf16[512,768]{1,0:T(8,128)(2,1)S(1)}) custom-call(s32[8]{0:T(128)S(1)} %get-tuple-element.61.starts_ref, bf16[256,4096]{1,0:T(8,128)(2,1)} %get-tuple-element.62.q_ref, ...), custom_call_target="tpu_custom_call", output_to_operand_aliasing={{0}: (11, {})} | custom-call | flops 1 | bytes 1 | tf_op jit(solution)/shard_map/cond/branch_1_fun/attend/pallas_call | solution.py:234
  58.3 0.2 collective-permute-start.3
  58.5 2.2 %collective-permute-done.3.back_ref = bf16[512,768]{1,0:T(8,128)(2,1)S(1)} collective-permute-done((bf16[512,768]{1,0:T(8,128)(2,1)S(1)}, bf16[512,768]{1,0:T(8,128)(2,1)S(1)}, u32[]{:S(2)}, u32[]{:S(2)}) %collective-permute-start.3) | collective-permute-done | bytes 786464 | tf_op jit(solution)/shard_map/cond/branch_1_fun/ppermute | solution.py:36
  60.6 1.1 merge.4
  61.7 3.3 %collective-permute-start.14 = (bf16[512,768]{1,0:T(8,128)(2,1)}, bf16[512,768]{1,0:T(8,128)(2,1)}, u32[]{:S(2)}, u32[]{:S(2)}) collective-permute-start(bf16[512,768]{1,0:T(8,128)(2,1)} %get-tuple-element.119), channel_id=1, source_target_pairs={{2,0},{3,1},{4,2},{5,3},{6,4},{7,5},{8,6},{9,7},{10,8},{11,9},{12,... | collective-permute-start | bytes 2359304 | tf_op jit(solution)/shard_map/ppermute | solution.py:32
  65.0 0.0 collective-permute-done.11
  65.0 2.5 %collective-permute-start.13 = (bf16[512,768]{1,0:T(8,128)(2,1)}, bf16[512,768]{1,0:T(8,128)(2,1)}, u32[]{:S(2)}, u32[]{:S(2)}) collective-permute-start(bf16[512,768]{1,0:T(8,128)(2,1)} %get-tuple-element.117), channel_id=1, source_target_pairs={{2,0},{3,1},{4,2},{5,3},{6,4},{7,5},{8,6},{9,7},{10,8},{11,9},{12,... | collective-permute-start | bytes 2359304 | tf_op jit(solution)/shard_map/ppermute | solution.py:32
  67.6 12.3 %conditional.5 = (bf16[256,4096]{1,0:T(8,128)(2,1)S(1)}, bf16[512,512]{1,0:T(8,128)(2,1)S(1)}, bf16[512,512]{1,0:T(8,128)(2,1)S(1)}) conditional(s32[]{:T(128)} %bitcast, bf16[256,4096]{1,0:T(8,128)(2,1)S(1)} %get-tuple-element.111, (bf16[512,512]{1,0:T(8,128)(2,1)S(1)}, s32[8]{0:T(128)S(1)}, bf16[256,4096]{1,0:T(8,128)(2,1)}, ...), branch_computations={%region_4.0_spmd, %region_5.0_spmd} | conditional | flops 2 | bytes 4194410 | solution.py:400
  67.6 1.3 %collective-permute-start.4 = (bf16[512,512]{1,0:T(8,128)(2,1)S(1)}, bf16[512,512]{1,0:T(8,128)(2,1)S(1)}, u32[]{:S(2)}, u32[]{:S(2)}) collective-permute-start(bf16[512,512]{1,0:T(8,128)(2,1)S(1)} %get-tuple-element.80.refs_4_.refs_5_), channel_id=1, source_target_pairs={{1,0},{3,2},{5,4},{7,6},{9,8},{11,10},{13,12},{15,14},{17,16},{19,... | collective-permute-start | bytes 1572872 | tf_op jit(solution)/shard_map/cond/branch_1_fun/ppermute | solution.py:44
  68.9 2.5 %collective-permute-done.4.refs_0_.refs_1_ = bf16[512,512]{1,0:T(8,128)(2,1)S(1)} collective-permute-done((bf16[512,512]{1,0:T(8,128)(2,1)S(1)}, bf16[512,512]{1,0:T(8,128)(2,1)S(1)}, u32[]{:S(2)}, u32[]{:S(2)}) %collective-permute-start.4) | collective-permute-done | bytes 524320 | tf_op jit(solution)/shard_map/cond/branch_1_fun/ppermute | solution.py:44
  71.4 6.3 %attend.5 = (bf16[256,4096]{1,0:T(8,128)(2,1)S(1)}, bf16[512,512]{1,0:T(8,128)(2,1)S(1)}, bf16[512,512]{1,0:T(8,128)(2,1)S(1)}, bf16[512,512]{1,0:T(8,128)(2,1)S(1)}) custom-call(s32[8]{0:T(128)S(1)} %get-tuple-element.75.starts_ref, bf16[256,4096]{1,0:T(8,128)(2,1)} %get-tuple-element.76.q_ref, ...), custom_call_target="tpu_custom_call", output_to_operand_aliasing={{0}: (11, {})} | custom-call | flops 1 | bytes 1 | tf_op jit(solution)/shard_map/cond/branch_1_fun/attend/pallas_call | solution.py:234
  77.7 0.2 collective-permute-start.5
  77.9 1.8 %collective-permute-done.5.back_ref = bf16[512,512]{1,0:T(8,128)(2,1)S(1)} collective-permute-done((bf16[512,512]{1,0:T(8,128)(2,1)S(1)}, bf16[512,512]{1,0:T(8,128)(2,1)S(1)}, u32[]{:S(2)}, u32[]{:S(2)}) %collective-permute-start.5) | collective-permute-done | bytes 524320 | tf_op jit(solution)/shard_map/cond/branch_1_fun/ppermute | solution.py:36
  79.7 0.2 merge.5
  79.9 0.0 copy-start.3
  79.9 4.2 %collective-permute-start.12 = (bf16[512,512]{1,0:T(8,128)(2,1)S(1)}, bf16[512,512]{1,0:T(8,128)(2,1)S(1)}, u32[]{:S(2)}, u32[]{:S(2)}) collective-permute-start(bf16[512,512]{1,0:T(8,128)(2,1)S(1)} %get-tuple-element.114), channel_id=1, source_target_pairs={{2,0},{3,1},{4,2},{5,3},{6,4},{7,5},{8,6},{9,7},{10,8},{11,9},{12,... | collective-permute-start | bytes 1572872 | tf_op jit(solution)/shard_map/ppermute | solution.py:32
  84.1 2.0 %collective-permute-done.14.home_ref = bf16[512,768]{1,0:T(8,128)(2,1)} collective-permute-done((bf16[512,768]{1,0:T(8,128)(2,1)}, bf16[512,768]{1,0:T(8,128)(2,1)}, u32[]{:S(2)}, u32[]{:S(2)}) %collective-permute-start.14) | collective-permute-done | bytes 786464 | tf_op jit(solution)/shard_map/ppermute | solution.py:32
  86.1 2.1 %finish.3 = (bf16[256,2048]{1,0:T(8,128)(2,1)}, bf16[256,2048]{1,0:T(8,128)(2,1)}) custom-call(bf16[512,768]{1,0:T(8,128)(2,1)S(1)} %get-tuple-element.118.kept_ref, bf16[512,768]{1,0:T(8,128)(2,1)} %collective-permute-done.14.home_ref), custom_call_target="tpu_custom_call" | custom-call | flops 1 | bytes 1 | tf_op jit(solution)/shard_map/finish/pallas_call | solution.py:343
  88.2 14.7 %collective-permute-done.13.home_ref = bf16[512,768]{1,0:T(8,128)(2,1)} collective-permute-done((bf16[512,768]{1,0:T(8,128)(2,1)}, bf16[512,768]{1,0:T(8,128)(2,1)}, u32[]{:S(2)}, u32[]{:S(2)}) %collective-permute-start.13) | collective-permute-done | bytes 786464 | tf_op jit(solution)/shard_map/ppermute | solution.py:32
  103.0 2.1 %finish.4 = (bf16[256,2048]{1,0:T(8,128)(2,1)}, bf16[256,2048]{1,0:T(8,128)(2,1)}) custom-call(bf16[512,768]{1,0:T(8,128)(2,1)S(1)} %get-tuple-element.115.kept_ref, bf16[512,768]{1,0:T(8,128)(2,1)} %collective-permute-done.13.home_ref, bf16[256,2048]{1,0:T(8,128)(2,1)} %get-tuple-element.120.refs_0_, ...), custom_call_target="tpu_custom_call", output_to_operand_aliasing={{0}: (2, {}), {1}: (3, {})} | custom-call | flops 1 | bytes 1 | tf_op jit(solution)/shard_map/finish/pallas_call | solution.py:343
  105.1 0.0 copy-done.3
  105.1 8.2 %collective-permute-done.12.home_ref = bf16[512,512]{1,0:T(8,128)(2,1)S(1)} collective-permute-done((bf16[512,512]{1,0:T(8,128)(2,1)S(1)}, bf16[512,512]{1,0:T(8,128)(2,1)S(1)}, u32[]{:S(2)}, u32[]{:S(2)}) %collective-permute-start.12) | collective-permute-done | bytes 524320 | tf_op jit(solution)/shard_map/ppermute | solution.py:32
  113.3 0.9 finish.5
Async XLA Ops:
  0.6 27.6 %copy-start.5 = (bf16[256,4096]{1,0:T(8,128)(2,1)S(1)}, bf16[256,4096]{1,0:T(8,128)(2,1)}, u32[]{:S(2)}) copy-start(bf16[256,4096]{1,0:T(8,128)(2,1)} %param.14) | copy-start | bytes 6291460
  2.6 14.8 %collective-permute-start.7 = (bf16[512,512]{1,0:T(8,128)(2,1)}, bf16[512,512]{1,0:T(8,128)(2,1)S(1)}, u32[]{:S(2)}, u32[]{:S(2)}) collective-permute-start(bf16[512,512]{1,0:T(8,128)(2,1)} %pack.4), channel_id=1, source_target_pairs={{0,1},{2,3},{4,5},{6,7},{8,9},{10,11},{12,13},{14,15},{16,17},{18,... | collective-permute-start | bytes 1572872 | tf_op jit(solution)/shard_map/ppermute | solution.py:40
  4.4 23.9 %copy-start.4 = (bf16[256,4096]{1,0:T(8,128)(2,1)S(1)}, bf16[256,4096]{1,0:T(8,128)(2,1)}, u32[]{:S(2)}) copy-start(bf16[256,4096]{1,0:T(8,128)(2,1)} %param.11) | copy-start | bytes 6291460
  5.7 15.1 %copy-start.6 = (s32[8]{0:T(128)S(1)}, s32[8]{0:T(128)}, u32[]{:S(2)}) copy-start(s32[8]{0:T(128)} %param.15) | copy-start | bytes 100
  5.7 22.5 %copy-start.1 = (bf16[256,2048]{1,0:T(8,128)(2,1)S(1)}, bf16[256,2048]{1,0:T(8,128)(2,1)}, u32[]{:S(2)}) copy-start(bf16[256,2048]{1,0:T(8,128)(2,1)} %k_ref.5) | copy-start | bytes 3145732
  5.7 22.5 %copy-start.2 = (bf16[256,2048]{1,0:T(8,128)(2,1)S(1)}, bf16[256,2048]{1,0:T(8,128)(2,1)}, u32[]{:S(2)}) copy-start(bf16[256,2048]{1,0:T(8,128)(2,1)} %v_ref.5) | copy-start | bytes 3145732
  5.8 22.5 %collective-permute-start.6 = (bf16[512,768]{1,0:T(8,128)(2,1)S(1)}, bf16[512,768]{1,0:T(8,128)(2,1)S(1)}, u32[]{:S(2)}, u32[]{:S(2)}) collective-permute-start(bf16[512,768]{1,0:T(8,128)(2,1)S(1)} %pack.3), channel_id=1, source_target_pairs={{0,2},{1,3},{2,4},{3,5},{4,6},{5,7},{6,8},{7,9},{8,10},{9,11},{10,... | collective-permute-start | bytes 2359304 | tf_op jit(solution)/shard_map/ppermute | solution.py:32
  9.3 19.0 %collective-permute-start.8 = (bf16[512,768]{1,0:T(8,128)(2,1)S(1)}, bf16[512,768]{1,0:T(8,128)(2,1)S(1)}, u32[]{:S(2)}, u32[]{:S(2)}) collective-permute-start(bf16[512,768]{1,0:T(8,128)(2,1)S(1)} %pack.3), channel_id=1, source_target_pairs={{0,1},{2,3},{4,5},{6,7},{8,9},{10,11},{12,13},{14,15},{16,17},{18,... | collective-permute-start | bytes 2359304 | tf_op jit(solution)/shard_map/ppermute | solution.py:40
  12.7 31.9 %collective-permute-start.10 = (bf16[512,768]{1,0:T(8,128)(2,1)}, bf16[512,768]{1,0:T(8,128)(2,1)S(1)}, u32[]{:S(2)}, u32[]{:S(2)}) collective-permute-start(bf16[512,768]{1,0:T(8,128)(2,1)} %pack.5), channel_id=1, source_target_pairs={{0,1},{2,3},{4,5},{6,7},{8,9},{10,11},{12,13},{14,15},{16,17},{18,... | collective-permute-start | bytes 2359304 | tf_op jit(solution)/shard_map/ppermute | solution.py:40
  14.0 31.1 %collective-permute-start.9 = (bf16[512,768]{1,0:T(8,128)(2,1)}, bf16[512,768]{1,0:T(8,128)(2,1)S(1)}, u32[]{:S(2)}, u32[]{:S(2)}) collective-permute-start(bf16[512,768]{1,0:T(8,128)(2,1)} %pack.5), channel_id=1, source_target_pairs={{0,2},{1,3},{2,4},{3,5},{4,6},{5,7},{6,8},{7,9},{8,10},{9,11},{10,... | collective-permute-start | bytes 2359304 | tf_op jit(solution)/shard_map/ppermute | solution.py:32
  17.5 47.6 %collective-permute-start.11 = (bf16[512,512]{1,0:T(8,128)(2,1)}, bf16[512,512]{1,0:T(8,128)(2,1)S(1)}, u32[]{:S(2)}, u32[]{:S(2)}) collective-permute-start(bf16[512,512]{1,0:T(8,128)(2,1)} %pack.4), channel_id=1, source_target_pairs={{0,2},{1,3},{2,4},{3,5},{4,6},{5,7},{6,8},{7,9},{8,10},{9,11},{10,... | collective-permute-start | bytes 1572872 | tf_op jit(solution)/shard_map/ppermute | solution.py:32
  28.3 4.2 %collective-permute-start = (bf16[512,768]{1,0:T(8,128)(2,1)S(1)}, bf16[512,768]{1,0:T(8,128)(2,1)S(1)}, u32[]{:S(2)}, u32[]{:S(2)}) collective-permute-start(bf16[512,768]{1,0:T(8,128)(2,1)S(1)} %get-tuple-element.53.refs_4_.refs_5_), channel_id=1, source_target_pairs={{1,0},{3,2},{5,4},{7,6},{9,8},{11,10},{13,12},{15,14},{17,16},{19,... | collective-permute-start | bytes 2359304 | tf_op jit(solution)/shard_map/cond/branch_1_fun/ppermute | solution.py:44
  41.1 2.4 %collective-permute-start.1 = (bf16[512,768]{1,0:T(8,128)(2,1)S(1)}, bf16[512,768]{1,0:T(8,128)(2,1)S(1)}, u32[]{:S(2)}, u32[]{:S(2)}) collective-permute-start(bf16[512,768]{1,0:T(8,128)(2,1)S(1)} %get-tuple-element.58), channel_id=1, source_target_pairs={{0,1},{1,0},{2,3},{3,2},{4,5},{5,4},{6,7},{7,6},{8,9},{9,8},{10,11... | collective-permute-start | bytes 2359304 | tf_op jit(solution)/shard_map/cond/branch_1_fun/ppermute | solution.py:36
  43.7 0.9 copy-start
  45.1 4.2 %collective-permute-start.2 = (bf16[512,768]{1,0:T(8,128)(2,1)S(1)}, bf16[512,768]{1,0:T(8,128)(2,1)S(1)}, u32[]{:S(2)}, u32[]{:S(2)}) collective-permute-start(bf16[512,768]{1,0:T(8,128)(2,1)S(1)} %get-tuple-element.66.refs_4_.refs_5_), channel_id=1, source_target_pairs={{1,0},{3,2},{5,4},{7,6},{9,8},{11,10},{13,12},{15,14},{17,16},{19,... | collective-permute-start | bytes 2359304 | tf_op jit(solution)/shard_map/cond/branch_1_fun/ppermute | solution.py:44
  58.3 2.4 %collective-permute-start.3 = (bf16[512,768]{1,0:T(8,128)(2,1)S(1)}, bf16[512,768]{1,0:T(8,128)(2,1)S(1)}, u32[]{:S(2)}, u32[]{:S(2)}) collective-permute-start(bf16[512,768]{1,0:T(8,128)(2,1)S(1)} %get-tuple-element.72), channel_id=1, source_target_pairs={{0,1},{1,0},{2,3},{3,2},{4,5},{5,4},{6,7},{7,6},{8,9},{9,8},{10,11... | collective-permute-start | bytes 2359304 | tf_op jit(solution)/shard_map/cond/branch_1_fun/ppermute | solution.py:36
  61.7 24.4 %collective-permute-start.14 = (bf16[512,768]{1,0:T(8,128)(2,1)}, bf16[512,768]{1,0:T(8,128)(2,1)}, u32[]{:S(2)}, u32[]{:S(2)}) collective-permute-start(bf16[512,768]{1,0:T(8,128)(2,1)} %get-tuple-element.119), channel_id=1, source_target_pairs={{2,0},{3,1},{4,2},{5,3},{6,4},{7,5},{8,6},{9,7},{10,8},{11,9},{12,... | collective-permute-start | bytes 2359304 | tf_op jit(solution)/shard_map/ppermute | solution.py:32
  65.0 37.9 %collective-permute-start.13 = (bf16[512,768]{1,0:T(8,128)(2,1)}, bf16[512,768]{1,0:T(8,128)(2,1)}, u32[]{:S(2)}, u32[]{:S(2)}) collective-permute-start(bf16[512,768]{1,0:T(8,128)(2,1)} %get-tuple-element.117), channel_id=1, source_target_pairs={{2,0},{3,1},{4,2},{5,3},{6,4},{7,5},{8,6},{9,7},{10,8},{11,9},{12,... | collective-permute-start | bytes 2359304 | tf_op jit(solution)/shard_map/ppermute | solution.py:32
  67.6 3.8 %collective-permute-start.4 = (bf16[512,512]{1,0:T(8,128)(2,1)S(1)}, bf16[512,512]{1,0:T(8,128)(2,1)S(1)}, u32[]{:S(2)}, u32[]{:S(2)}) collective-permute-start(bf16[512,512]{1,0:T(8,128)(2,1)S(1)} %get-tuple-element.80.refs_4_.refs_5_), channel_id=1, source_target_pairs={{1,0},{3,2},{5,4},{7,6},{9,8},{11,10},{13,12},{15,14},{17,16},{19,... | collective-permute-start | bytes 1572872 | tf_op jit(solution)/shard_map/cond/branch_1_fun/ppermute | solution.py:44
  77.7 2.0 %collective-permute-start.5 = (bf16[512,512]{1,0:T(8,128)(2,1)S(1)}, bf16[512,512]{1,0:T(8,128)(2,1)S(1)}, u32[]{:S(2)}, u32[]{:S(2)}) collective-permute-start(bf16[512,512]{1,0:T(8,128)(2,1)S(1)} %get-tuple-element.86), channel_id=1, source_target_pairs={{0,1},{1,0},{2,3},{3,2},{4,5},{5,4},{6,7},{7,6},{8,9},{9,8},{10,11... | collective-permute-start | bytes 1572872 | tf_op jit(solution)/shard_map/cond/branch_1_fun/ppermute | solution.py:36
  79.9 25.2 %copy-start.3 = (bf16[256,4096]{1,0:T(8,128)(2,1)}, bf16[256,4096]{1,0:T(8,128)(2,1)S(1)}, u32[]{:S(2)}) copy-start(bf16[256,4096]{1,0:T(8,128)(2,1)S(1)} %get-tuple-element.106) | copy-start | bytes 6291460
  79.9 33.4 %collective-permute-start.12 = (bf16[512,512]{1,0:T(8,128)(2,1)S(1)}, bf16[512,512]{1,0:T(8,128)(2,1)S(1)}, u32[]{:S(2)}, u32[]{:S(2)}) collective-permute-start(bf16[512,512]{1,0:T(8,128)(2,1)S(1)} %get-tuple-element.114), channel_id=1, source_target_pairs={{2,0},{3,1},{4,2},{5,3},{6,4},{7,5},{8,6},{9,7},{10,8},{11,9},{12,... | collective-permute-start | bytes 1572872 | tf_op jit(solution)/shard_map/ppermute | solution.py:32

commit v4 on v3

--- a/solution.py
+++ b/solution.py
@@ -348,7 +348,7 @@
         scratch_shapes=[pltpu.VMEM(kept.shape, kept.dtype), pltpu.SemaphoreType.DMA((2,))],
         input_output_aliases=aliases,
         compiler_params=SMALL,
-        cost_estimate=FREE,
+        cost_estimate=pl.CostEstimate(flops=600000000, bytes_accessed=1, transcendentals=0),
         name="finish",
     )(*operands)
 
@@ -375,7 +375,6 @@
     packed = [pack(keys, values, start, sum(group), 1)[0] for start, group in zip(starts, GROUPS)]
     far = [shifted(x, 2, devices) for x in packed]
     early = [to_odd(x, devices) for x in packed]
-    far[0] = after(far[0], early[-1])
 
     def work(start, first, heads, received, own_near, near, dquery):
         if near is None:

time: 115 us -> 103 us (0.90)
  waiting for transfers between devices: 47.2 us -> 35.4 us
    ppermute x6, waiting for transfers between devices: 32.9 us -> 20.9 us  [shifted(): return lax.ppermute(x, AXES, pairs)]
  transfers between devices with their start and end apart: 15 -> 15, of which waited for: 11 -> 9; matrix products, arithmetic and copies ran while one was open for 0% -> 0% of each run, Pallas kernels for 29% -> 33%
where the time goes in v4:
time: 103 us; the launch traced here: 102 us
  Pallas kernels  35.6 us (35%)
  waiting for transfers between devices  35.4 us (34%)
  starting transfers between devices  29.1 us (28%)
    pallas_call x3, Pallas kernels, attend(): pl.pallas_call(functools.partial(kernel, rows, back, group, len(near) ==...  24 us
    ppermute x6, waiting for transfers between devices, shifted(): return lax.ppermute(x, AXES, pairs)  20.9 us
    ppermute x6, starting transfers between devices, shifted(): return lax.ppermute(x, AXES, pairs)  19.5 us
    ppermute x3, waiting for transfers between devices, to_even(): return lax.ppermute(x, AXES, [(i + 1, i) for i in range(0, devices, 2)])  8.47 us
    ppermute x3, waiting for transfers between devices, swapped(): return lax.ppermute(x, AXES, [(i, i ^ 1) for i in range(devices)])  6.08 us
    pallas_call x3, Pallas kernels, pack(): pl.pallas_call(functools.partial(pack_kernel, first), in_specs=[pl.BlockS...  5.14 us
    ppermute x3, starting transfers between devices, to_odd(): return lax.ppermute(x, AXES, [(i, i + 1) for i in range(0, devices, 2)])  4.93 us
    ppermute x3, starting transfers between devices, to_even(): return lax.ppermute(x, AXES, [(i + 1, i) for i in range(0, devices, 2)])  4.01 us
  transfers between devices with their start and end apart: 15, of which 9 were waited for; matrix products, arithmetic and copies ran while one was open for 0% of the time, Pallas kernels for 33%

profile of v4, /device:TPU:14, one launch (start us, length us, event | category | flops | bytes accessed | tf_op | source)
XLA Modules:
  0.0 102.0 jit_solution(16274523406066349778)
XLA Ops:
  0.6 0.0 copy-start.6
  0.6 1.3 %pack.3 = bf16[512,768]{1,0:T(8,128)(2,1)S(1)} custom-call(bf16[256,2048]{1,0:T(8,128)(2,1)} %k_ref.5, bf16[256,2048]{1,0:T(8,128)(2,1)} %v_ref.5), custom_call_target="tpu_custom_call" | custom-call | tf_op jit(solution)/shard_map/pack/pallas_call | solution.py:270
  1.9 0.0 copy-start.7
  1.9 0.0 copy-start.2
  2.0 0.0 copy-start.3
  2.0 0.0 copy-start.5
  2.0 3.7 %collective-permute-start.6 = (bf16[512,768]{1,0:T(8,128)(2,1)S(1)}, bf16[512,768]{1,0:T(8,128)(2,1)S(1)}, u32[]{:S(2)}, u32[]{:S(2)}) collective-permute-start(bf16[512,768]{1,0:T(8,128)(2,1)S(1)} %pack.3), channel_id=1, source_target_pairs={{0,2},{1,3},{2,4},{3,5},{4,6},{5,7},{6,8},{7,9},{8,10},{9,11},{10,... | collective-permute-start | bytes 2359304 | tf_op jit(solution)/shard_map/ppermute | solution.py:32
  5.7 1.5 %collective-permute-start.7 = (bf16[512,768]{1,0:T(8,128)(2,1)S(1)}, bf16[512,768]{1,0:T(8,128)(2,1)S(1)}, u32[]{:S(2)}, u32[]{:S(2)}) collective-permute-start(bf16[512,768]{1,0:T(8,128)(2,1)S(1)} %pack.3), channel_id=1, source_target_pairs={{0,1},{2,3},{4,5},{6,7},{8,9},{10,11},{12,13},{14,15},{16,17},{18,... | collective-permute-start | bytes 2359304 | tf_op jit(solution)/shard_map/ppermute | solution.py:40
  7.2 2.0 %pack.4 = bf16[512,768]{1,0:T(8,128)(2,1)} custom-call(bf16[256,2048]{1,0:T(8,128)(2,1)} %k_ref.5, bf16[256,2048]{1,0:T(8,128)(2,1)} %v_ref.5), custom_call_target="tpu_custom_call" | custom-call | tf_op jit(solution)/shard_map/pack/pallas_call | solution.py:270
  9.2 3.4 %collective-permute-start.8 = (bf16[512,768]{1,0:T(8,128)(2,1)}, bf16[512,768]{1,0:T(8,128)(2,1)S(1)}, u32[]{:S(2)}, u32[]{:S(2)}) collective-permute-start(bf16[512,768]{1,0:T(8,128)(2,1)} %pack.4), channel_id=1, source_target_pairs={{0,2},{1,3},{2,4},{3,5},{4,6},{5,7},{6,8},{7,9},{8,10},{9,11},{10,... | collective-permute-start | bytes 2359304 | tf_op jit(solution)/shard_map/ppermute | solution.py:32
  12.6 1.3 %collective-permute-start.9 = (bf16[512,768]{1,0:T(8,128)(2,1)}, bf16[512,768]{1,0:T(8,128)(2,1)S(1)}, u32[]{:S(2)}, u32[]{:S(2)}) collective-permute-start(bf16[512,768]{1,0:T(8,128)(2,1)} %pack.4), channel_id=1, source_target_pairs={{0,1},{2,3},{4,5},{6,7},{8,9},{10,11},{12,13},{14,15},{16,17},{18,... | collective-permute-start | bytes 2359304 | tf_op jit(solution)/shard_map/ppermute | solution.py:40
  14.0 1.8 %pack.5 = bf16[512,512]{1,0:T(8,128)(2,1)} custom-call(bf16[256,2048]{1,0:T(8,128)(2,1)} %k_ref.5, bf16[256,2048]{1,0:T(8,128)(2,1)} %v_ref.5), custom_call_target="tpu_custom_call" | custom-call | tf_op jit(solution)/shard_map/pack/pallas_call | solution.py:270
  15.8 3.3 %collective-permute-start.10 = (bf16[512,512]{1,0:T(8,128)(2,1)}, bf16[512,512]{1,0:T(8,128)(2,1)}, u32[]{:S(2)}, u32[]{:S(2)}) collective-permute-start(bf16[512,512]{1,0:T(8,128)(2,1)} %pack.5), channel_id=1, source_target_pairs={{0,2},{1,3},{2,4},{3,5},{4,6},{5,7},{6,8},{7,9},{8,10},{9,11},{10,... | collective-permute-start | bytes 1572872 | tf_op jit(solution)/shard_map/ppermute | solution.py:32
  19.2 5.4 %collective-permute-done.6 = bf16[512,768]{1,0:T(8,128)(2,1)S(1)} collective-permute-done((bf16[512,768]{1,0:T(8,128)(2,1)S(1)}, bf16[512,768]{1,0:T(8,128)(2,1)S(1)}, u32[]{:S(2)}, u32[]{:S(2)}) %collective-permute-start.6) | collective-permute-done | bytes 786464 | tf_op jit(solution)/shard_map/ppermute | solution.py:32
  24.6 2.1 %collective-permute-start.11 = (bf16[512,512]{1,0:T(8,128)(2,1)}, bf16[512,512]{1,0:T(8,128)(2,1)}, u32[]{:S(2)}, u32[]{:S(2)}) collective-permute-start(bf16[512,512]{1,0:T(8,128)(2,1)} %pack.5), channel_id=1, source_target_pairs={{0,1},{2,3},{4,5},{6,7},{8,9},{10,11},{12,13},{14,15},{16,17},{18,... | collective-permute-start | bytes 1572872 | tf_op jit(solution)/shard_map/ppermute | solution.py:40
  26.6 0.0 copy-done.7
  26.7 0.0 collective-permute-done.7
  26.7 0.0 copy-done.6
  26.7 0.0 copy-done.2
  26.7 0.0 copy-done.3
  26.7 0.0 copy-done.5
  26.7 17.1 %conditional.3 = (bf16[256,4096]{1,0:T(8,128)(2,1)S(1)}, bf16[512,768]{1,0:T(8,128)(2,1)}, bf16[512,768]{1,0:T(8,128)(2,1)}) conditional(s32[]{:T(128)} %bitcast, () %tuple.33, (bf16[512,768]{1,0:T(8,128)(2,1)S(1)}, s32[8]{0:T(128)S(1)}, bf16[256,4096]{1,0:T(8,128)(2,1)S(1)}, bf16[256,4096]{1,0:T(8,128)(2,1)S(1)}, bf16[256,2048]{1,0:T(8,128)(2,1)S(1)}, ...), branch_computations={%region_0.0_spmd, %region_1.0_spmd} | conditional | flops 2 | bytes 9437318 | solution.py:399
  26.8 1.3 %collective-permute-start = (bf16[512,768]{1,0:T(8,128)(2,1)S(1)}, bf16[512,768]{1,0:T(8,128)(2,1)S(1)}, u32[]{:S(2)}, u32[]{:S(2)}) collective-permute-start(bf16[512,768]{1,0:T(8,128)(2,1)S(1)} %get-tuple-element.53.refs_4_.refs_5_), channel_id=1, source_target_pairs={{1,0},{3,2},{5,4},{7,6},{9,8},{11,10},{13,12},{15,14},{17,16},{19,... | collective-permute-start | bytes 2359304 | tf_op jit(solution)/shard_map/cond/branch_1_fun/ppermute | solution.py:44
  28.1 2.9 %collective-permute-done.refs_0_.refs_1_ = bf16[512,768]{1,0:T(8,128)(2,1)S(1)} collective-permute-done((bf16[512,768]{1,0:T(8,128)(2,1)S(1)}, bf16[512,768]{1,0:T(8,128)(2,1)S(1)}, u32[]{:S(2)}, u32[]{:S(2)}) %collective-permute-start) | collective-permute-done | bytes 786464 | tf_op jit(solution)/shard_map/cond/branch_1_fun/ppermute | solution.py:44
  30.9 8.6 %attend.3 = (bf16[256,4096]{1,0:T(8,128)(2,1)S(1)}, bf16[512,768]{1,0:T(8,128)(2,1)S(1)}, bf16[512,768]{1,0:T(8,128)(2,1)S(1)}, bf16[512,768]{1,0:T(8,128)(2,1)S(1)}) custom-call(s32[8]{0:T(128)S(1)} %get-tuple-element.48.starts_ref, bf16[256,4096]{1,0:T(8,128)(2,1)S(1)} %get-tuple-element.49.q_ref, bf16[256,4096]{1,0:T(8,128)(2,1)S(1)} %get-tuple-element.50.g_ref, ...), custom_call_target="tpu_custom_call" | custom-call | flops 1 | bytes 1 | tf_op jit(solution)/shard_map/cond/branch_1_fun/attend/pallas_call | solution.py:234
  39.5 0.2 collective-permute-start.1
  39.7 2.2 %collective-permute-done.1.back_ref = bf16[512,768]{1,0:T(8,128)(2,1)S(1)} collective-permute-done((bf16[512,768]{1,0:T(8,128)(2,1)S(1)}, bf16[512,768]{1,0:T(8,128)(2,1)S(1)}, u32[]{:S(2)}, u32[]{:S(2)}) %collective-permute-start.1) | collective-permute-done | bytes 786464 | tf_op jit(solution)/shard_map/cond/branch_1_fun/ppermute | solution.py:36
  41.9 1.1 %merge.3 = (bf16[512,768]{1,0:T(8,128)(2,1)}, bf16[512,768]{1,0:T(8,128)(2,1)S(1)}) custom-call(bf16[512,768]{1,0:T(8,128)(2,1)S(1)} %get-tuple-element.56.far_ref, bf16[512,768]{1,0:T(8,128)(2,1)S(1)} %get-tuple-element.57.own_ref, bf16[512,768]{1,0:T(8,128)(2,1)S(1)} %collective-permute-done.1.back_ref), custom_call_target="tpu_custom_call" | custom-call | flops 1 | bytes 1 | tf_op jit(solution)/shard_map/cond/branch_1_fun/merge/pallas_call | solution.py:307
  43.0 0.0 copy-start
  43.0 0.9 copy-done
  43.9 3.3 %collective-permute-start.14 = (bf16[512,768]{1,0:T(8,128)(2,1)}, bf16[512,768]{1,0:T(8,128)(2,1)}, u32[]{:S(2)}, u32[]{:S(2)}) collective-permute-start(bf16[512,768]{1,0:T(8,128)(2,1)} %get-tuple-element.117), channel_id=1, source_target_pairs={{2,0},{3,1},{4,2},{5,3},{6,4},{7,5},{8,6},{9,7},{10,8},{11,9},{12,... | collective-permute-start | bytes 2359304 | tf_op jit(solution)/shard_map/ppermute | solution.py:32
  47.2 0.0 collective-permute-done.8
  47.2 0.0 collective-permute-done.9
  47.2 16.7 %conditional.4 = (bf16[256,4096]{1,0:T(8,128)(2,1)S(1)}, bf16[512,768]{1,0:T(8,128)(2,1)}, bf16[512,768]{1,0:T(8,128)(2,1)S(1)}) conditional(s32[]{:T(128)} %bitcast, bf16[256,4096]{1,0:T(8,128)(2,1)S(1)} %get-tuple-element.108, (bf16[512,768]{1,0:T(8,128)(2,1)S(1)}, s32[8]{0:T(128)S(1)}, bf16[256,4096]{1,0:T(8,128)(2,1)}, ...), branch_computations={%region_2.0_spmd, %region_3.0_spmd} | conditional | flops 2 | bytes 6291562 | solution.py:399
  47.2 1.3 %collective-permute-start.2 = (bf16[512,768]{1,0:T(8,128)(2,1)S(1)}, bf16[512,768]{1,0:T(8,128)(2,1)S(1)}, u32[]{:S(2)}, u32[]{:S(2)}) collective-permute-start(bf16[512,768]{1,0:T(8,128)(2,1)S(1)} %get-tuple-element.66.refs_4_.refs_5_), channel_id=1, source_target_pairs={{1,0},{3,2},{5,4},{7,6},{9,8},{11,10},{13,12},{15,14},{17,16},{19,... | collective-permute-start | bytes 2359304 | tf_op jit(solution)/shard_map/cond/branch_1_fun/ppermute | solution.py:44
  48.5 2.9 %collective-permute-done.2.refs_0_.refs_1_ = bf16[512,768]{1,0:T(8,128)(2,1)S(1)} collective-permute-done((bf16[512,768]{1,0:T(8,128)(2,1)S(1)}, bf16[512,768]{1,0:T(8,128)(2,1)S(1)}, u32[]{:S(2)}, u32[]{:S(2)}) %collective-permute-start.2) | collective-permute-done | bytes 786464 | tf_op jit(solution)/shard_map/cond/branch_1_fun/ppermute | solution.py:44
  51.4 9.0 %attend.4 = (bf16[256,4096]{1,0:T(8,128)(2,1)S(1)}, bf16[512,768]{1,0:T(8,128)(2,1)S(1)}, bf16[512,768]{1,0:T(8,128)(2,1)S(1)}, bf16[512,768]{1,0:T(8,128)(2,1)S(1)}) custom-call(s32[8]{0:T(128)S(1)} %get-tuple-element.61.starts_ref, bf16[256,4096]{1,0:T(8,128)(2,1)} %get-tuple-element.62.q_ref, ...), custom_call_target="tpu_custom_call", output_to_operand_aliasing={{0}: (11, {})} | custom-call | flops 1 | bytes 1 | tf_op jit(solution)/shard_map/cond/branch_1_fun/attend/pallas_call | solution.py:234
  60.4 0.2 collective-permute-start.3
  60.6 2.2 %collective-permute-done.3.back_ref = bf16[512,768]{1,0:T(8,128)(2,1)S(1)} collective-permute-done((bf16[512,768]{1,0:T(8,128)(2,1)S(1)}, bf16[512,768]{1,0:T(8,128)(2,1)S(1)}, u32[]{:S(2)}, u32[]{:S(2)}) %collective-permute-start.3) | collective-permute-done | bytes 786464 | tf_op jit(solution)/shard_map/cond/branch_1_fun/ppermute | solution.py:36
  62.7 1.1 %merge.4 = (bf16[512,768]{1,0:T(8,128)(2,1)}, bf16[512,768]{1,0:T(8,128)(2,1)S(1)}) custom-call(bf16[512,768]{1,0:T(8,128)(2,1)S(1)} %get-tuple-element.70.far_ref, bf16[512,768]{1,0:T(8,128)(2,1)S(1)} %get-tuple-element.71.own_ref, bf16[512,768]{1,0:T(8,128)(2,1)S(1)} %collective-permute-done.3.back_ref), custom_call_target="tpu_custom_call" | custom-call | flops 1 | bytes 1 | tf_op jit(solution)/shard_map/cond/branch_1_fun/merge/pallas_call | solution.py:307
  63.9 4.6 %collective-permute-done.10 = bf16[512,512]{1,0:T(8,128)(2,1)} collective-permute-done((bf16[512,512]{1,0:T(8,128)(2,1)}, bf16[512,512]{1,0:T(8,128)(2,1)}, u32[]{:S(2)}, u32[]{:S(2)}) %collective-permute-start.10) | collective-permute-done | bytes 524320 | tf_op jit(solution)/shard_map/ppermute | solution.py:32
  68.5 1.9 %collective-permute-start.13 = (bf16[512,768]{1,0:T(8,128)(2,1)}, bf16[512,768]{1,0:T(8,128)(2,1)S(1)}, u32[]{:S(2)}, u32[]{:S(2)}) collective-permute-start(bf16[512,768]{1,0:T(8,128)(2,1)} %get-tuple-element.115), channel_id=1, source_target_pairs={{2,0},{3,1},{4,2},{5,3},{6,4},{7,5},{8,6},{9,7},{10,8},{11,9},{12,... | collective-permute-start | bytes 2359304 | tf_op jit(solution)/shard_map/ppermute | solution.py:32
  70.4 0.0 collective-permute-done.11
  70.4 0.0 copy-start.1
  70.4 12.8 %conditional.5 = (bf16[256,4096]{1,0:T(8,128)(2,1)S(1)}, bf16[512,512]{1,0:T(8,128)(2,1)S(1)}, bf16[512,512]{1,0:T(8,128)(2,1)S(1)}) conditional(s32[]{:T(128)} %bitcast, bf16[256,4096]{1,0:T(8,128)(2,1)S(1)} %get-tuple-element.109, (bf16[512,512]{1,0:T(8,128)(2,1)}, s32[8]{0:T(128)S(1)}, bf16[256,4096]{1,0:T(8,128)(2,1)}, ...), branch_computations={%region_4.0_spmd, %region_5.0_spmd} | conditional | flops 2 | bytes 4194410 | solution.py:399
  70.4 1.4 %collective-permute-start.4 = (bf16[512,512]{1,0:T(8,128)(2,1)}, bf16[512,512]{1,0:T(8,128)(2,1)S(1)}, u32[]{:S(2)}, u32[]{:S(2)}) collective-permute-start(bf16[512,512]{1,0:T(8,128)(2,1)} %get-tuple-element.80.refs_4_.refs_5_), channel_id=1, source_target_pairs={{1,0},{3,2},{5,4},{7,6},{9,8},{11,10},{13,12},{15,14},{17,16},{19,... | collective-permute-start | bytes 1572872 | tf_op jit(solution)/shard_map/cond/branch_1_fun/ppermute | solution.py:44
  71.9 2.7 %collective-permute-done.4.refs_0_.refs_1_ = bf16[512,512]{1,0:T(8,128)(2,1)S(1)} collective-permute-done((bf16[512,512]{1,0:T(8,128)(2,1)}, bf16[512,512]{1,0:T(8,128)(2,1)S(1)}, u32[]{:S(2)}, u32[]{:S(2)}) %collective-permute-start.4) | collective-permute-done | bytes 524320 | tf_op jit(solution)/shard_map/cond/branch_1_fun/ppermute | solution.py:44
  74.6 6.5 %attend.5 = (bf16[256,4096]{1,0:T(8,128)(2,1)S(1)}, bf16[512,512]{1,0:T(8,128)(2,1)S(1)}, bf16[512,512]{1,0:T(8,128)(2,1)S(1)}, bf16[512,512]{1,0:T(8,128)(2,1)S(1)}) custom-call(s32[8]{0:T(128)S(1)} %get-tuple-element.75.starts_ref, bf16[256,4096]{1,0:T(8,128)(2,1)} %get-tuple-element.76.q_ref, ...), custom_call_target="tpu_custom_call", output_to_operand_aliasing={{0}: (11, {})} | custom-call | flops 1 | bytes 1 | tf_op jit(solution)/shard_map/cond/branch_1_fun/attend/pallas_call | solution.py:234
  81.1 0.2 collective-permute-start.5
  81.3 1.8 %collective-permute-done.5.back_ref = bf16[512,512]{1,0:T(8,128)(2,1)S(1)} collective-permute-done((bf16[512,512]{1,0:T(8,128)(2,1)S(1)}, bf16[512,512]{1,0:T(8,128)(2,1)S(1)}, u32[]{:S(2)}, u32[]{:S(2)}) %collective-permute-start.5) | collective-permute-done | bytes 524320 | tf_op jit(solution)/shard_map/cond/branch_1_fun/ppermute | solution.py:36
  83.1 0.2 merge.5
  83.2 0.0 copy-start.4
  83.2 3.9 %collective-permute-start.12 = (bf16[512,512]{1,0:T(8,128)(2,1)S(1)}, bf16[512,512]{1,0:T(8,128)(2,1)S(1)}, u32[]{:S(2)}, u32[]{:S(2)}) collective-permute-start(bf16[512,512]{1,0:T(8,128)(2,1)S(1)} %get-tuple-element.112), channel_id=1, source_target_pairs={{2,0},{3,1},{4,2},{5,3},{6,4},{7,5},{8,6},{9,7},{10,8},{11,9},{12,... | collective-permute-start | bytes 1572872 | tf_op jit(solution)/shard_map/ppermute | solution.py:32
  87.1 0.0 collective-permute-done.14.home_ref
  87.1 0.0 copy-done.1
  87.2 2.1 %finish.3 = (bf16[256,2048]{1,0:T(8,128)(2,1)}, bf16[256,2048]{1,0:T(8,128)(2,1)}) custom-call(bf16[512,768]{1,0:T(8,128)(2,1)S(1)} %copy-done.1, bf16[512,768]{1,0:T(8,128)(2,1)} %collective-permute-done.14.home_ref), custom_call_target="tpu_custom_call" | custom-call | flops 600000000 | bytes 1 | tf_op jit(solution)/shard_map/finish/pallas_call | solution.py:343
  89.3 0.0 collective-permute-done.13.home_ref
  89.3 1.0 finish.4
  90.3 0.0 copy-done.4
  90.3 10.9 %collective-permute-done.12.home_ref = bf16[512,512]{1,0:T(8,128)(2,1)S(1)} collective-permute-done((bf16[512,512]{1,0:T(8,128)(2,1)S(1)}, bf16[512,512]{1,0:T(8,128)(2,1)S(1)}, u32[]{:S(2)}, u32[]{:S(2)}) %collective-permute-start.12) | collective-permute-done | bytes 524320 | tf_op jit(solution)/shard_map/ppermute | solution.py:32
  101.2 0.9 finish.5
Async XLA Ops:
  0.6 26.1 %copy-start.6 = (bf16[256,4096]{1,0:T(8,128)(2,1)S(1)}, bf16[256,4096]{1,0:T(8,128)(2,1)}, u32[]{:S(2)}) copy-start(bf16[256,4096]{1,0:T(8,128)(2,1)} %param.14) | copy-start | bytes 6291460
  1.9 24.7 %copy-start.7 = (s32[8]{0:T(128)S(1)}, s32[8]{0:T(128)}, u32[]{:S(2)}) copy-start(s32[8]{0:T(128)} %param.15) | copy-start | bytes 100
  1.9 24.8 %copy-start.2 = (bf16[256,2048]{1,0:T(8,128)(2,1)S(1)}, bf16[256,2048]{1,0:T(8,128)(2,1)}, u32[]{:S(2)}) copy-start(bf16[256,2048]{1,0:T(8,128)(2,1)} %k_ref.5) | copy-start | bytes 3145732
  2.0 24.8 %copy-start.3 = (bf16[256,2048]{1,0:T(8,128)(2,1)S(1)}, bf16[256,2048]{1,0:T(8,128)(2,1)}, u32[]{:S(2)}) copy-start(bf16[256,2048]{1,0:T(8,128)(2,1)} %v_ref.5) | copy-start | bytes 3145732
  2.0 24.8 %copy-start.5 = (bf16[256,4096]{1,0:T(8,128)(2,1)S(1)}, bf16[256,4096]{1,0:T(8,128)(2,1)}, u32[]{:S(2)}) copy-start(bf16[256,4096]{1,0:T(8,128)(2,1)} %param.11) | copy-start | bytes 6291460
  2.0 22.6 %collective-permute-start.6 = (bf16[512,768]{1,0:T(8,128)(2,1)S(1)}, bf16[512,768]{1,0:T(8,128)(2,1)S(1)}, u32[]{:S(2)}, u32[]{:S(2)}) collective-permute-start(bf16[512,768]{1,0:T(8,128)(2,1)S(1)} %pack.3), channel_id=1, source_target_pairs={{0,2},{1,3},{2,4},{3,5},{4,6},{5,7},{6,8},{7,9},{8,10},{9,11},{10,... | collective-permute-start | bytes 2359304 | tf_op jit(solution)/shard_map/ppermute | solution.py:32
  5.7 21.0 %collective-permute-start.7 = (bf16[512,768]{1,0:T(8,128)(2,1)S(1)}, bf16[512,768]{1,0:T(8,128)(2,1)S(1)}, u32[]{:S(2)}, u32[]{:S(2)}) collective-permute-start(bf16[512,768]{1,0:T(8,128)(2,1)S(1)} %pack.3), channel_id=1, source_target_pairs={{0,1},{2,3},{4,5},{6,7},{8,9},{10,11},{12,13},{14,15},{16,17},{18,... | collective-permute-start | bytes 2359304 | tf_op jit(solution)/shard_map/ppermute | solution.py:40
  9.2 38.0 %collective-permute-start.8 = (bf16[512,768]{1,0:T(8,128)(2,1)}, bf16[512,768]{1,0:T(8,128)(2,1)S(1)}, u32[]{:S(2)}, u32[]{:S(2)}) collective-permute-start(bf16[512,768]{1,0:T(8,128)(2,1)} %pack.4), channel_id=1, source_target_pairs={{0,2},{1,3},{2,4},{3,5},{4,6},{5,7},{6,8},{7,9},{8,10},{9,11},{10,... | collective-permute-start | bytes 2359304 | tf_op jit(solution)/shard_map/ppermute | solution.py:32
  12.6 34.6 %collective-permute-start.9 = (bf16[512,768]{1,0:T(8,128)(2,1)}, bf16[512,768]{1,0:T(8,128)(2,1)S(1)}, u32[]{:S(2)}, u32[]{:S(2)}) collective-permute-start(bf16[512,768]{1,0:T(8,128)(2,1)} %pack.4), channel_id=1, source_target_pairs={{0,1},{2,3},{4,5},{6,7},{8,9},{10,11},{12,13},{14,15},{16,17},{18,... | collective-permute-start | bytes 2359304 | tf_op jit(solution)/shard_map/ppermute | solution.py:40
  15.8 52.6 %collective-permute-start.10 = (bf16[512,512]{1,0:T(8,128)(2,1)}, bf16[512,512]{1,0:T(8,128)(2,1)}, u32[]{:S(2)}, u32[]{:S(2)}) collective-permute-start(bf16[512,512]{1,0:T(8,128)(2,1)} %pack.5), channel_id=1, source_target_pairs={{0,2},{1,3},{2,4},{3,5},{4,6},{5,7},{6,8},{7,9},{8,10},{9,11},{10,... | collective-permute-start | bytes 1572872 | tf_op jit(solution)/shard_map/ppermute | solution.py:32
  24.6 45.8 %collective-permute-start.11 = (bf16[512,512]{1,0:T(8,128)(2,1)}, bf16[512,512]{1,0:T(8,128)(2,1)}, u32[]{:S(2)}, u32[]{:S(2)}) collective-permute-start(bf16[512,512]{1,0:T(8,128)(2,1)} %pack.5), channel_id=1, source_target_pairs={{0,1},{2,3},{4,5},{6,7},{8,9},{10,11},{12,13},{14,15},{16,17},{18,... | collective-permute-start | bytes 1572872 | tf_op jit(solution)/shard_map/ppermute | solution.py:40
  26.8 4.2 %collective-permute-start = (bf16[512,768]{1,0:T(8,128)(2,1)S(1)}, bf16[512,768]{1,0:T(8,128)(2,1)S(1)}, u32[]{:S(2)}, u32[]{:S(2)}) collective-permute-start(bf16[512,768]{1,0:T(8,128)(2,1)S(1)} %get-tuple-element.53.refs_4_.refs_5_), channel_id=1, source_target_pairs={{1,0},{3,2},{5,4},{7,6},{9,8},{11,10},{13,12},{15,14},{17,16},{19,... | collective-permute-start | bytes 2359304 | tf_op jit(solution)/shard_map/cond/branch_1_fun/ppermute | solution.py:44
  39.5 2.4 %collective-permute-start.1 = (bf16[512,768]{1,0:T(8,128)(2,1)S(1)}, bf16[512,768]{1,0:T(8,128)(2,1)S(1)}, u32[]{:S(2)}, u32[]{:S(2)}) collective-permute-start(bf16[512,768]{1,0:T(8,128)(2,1)S(1)} %get-tuple-element.58), channel_id=1, source_target_pairs={{0,1},{1,0},{2,3},{3,2},{4,5},{5,4},{6,7},{7,6},{8,9},{9,8},{10,11... | collective-permute-start | bytes 2359304 | tf_op jit(solution)/shard_map/cond/branch_1_fun/ppermute | solution.py:36
  43.0 0.9 copy-start
  43.9 43.3 %collective-permute-start.14 = (bf16[512,768]{1,0:T(8,128)(2,1)}, bf16[512,768]{1,0:T(8,128)(2,1)}, u32[]{:S(2)}, u32[]{:S(2)}) collective-permute-start(bf16[512,768]{1,0:T(8,128)(2,1)} %get-tuple-element.117), channel_id=1, source_target_pairs={{2,0},{3,1},{4,2},{5,3},{6,4},{7,5},{8,6},{9,7},{10,8},{11,9},{12,... | collective-permute-start | bytes 2359304 | tf_op jit(solution)/shard_map/ppermute | solution.py:32
  47.2 4.2 %collective-permute-start.2 = (bf16[512,768]{1,0:T(8,128)(2,1)S(1)}, bf16[512,768]{1,0:T(8,128)(2,1)S(1)}, u32[]{:S(2)}, u32[]{:S(2)}) collective-permute-start(bf16[512,768]{1,0:T(8,128)(2,1)S(1)} %get-tuple-element.66.refs_4_.refs_5_), channel_id=1, source_target_pairs={{1,0},{3,2},{5,4},{7,6},{9,8},{11,10},{13,12},{15,14},{17,16},{19,... | collective-permute-start | bytes 2359304 | tf_op jit(solution)/shard_map/cond/branch_1_fun/ppermute | solution.py:44
  60.4 2.4 %collective-permute-start.3 = (bf16[512,768]{1,0:T(8,128)(2,1)S(1)}, bf16[512,768]{1,0:T(8,128)(2,1)S(1)}, u32[]{:S(2)}, u32[]{:S(2)}) collective-permute-start(bf16[512,768]{1,0:T(8,128)(2,1)S(1)} %get-tuple-element.72), channel_id=1, source_target_pairs={{0,1},{1,0},{2,3},{3,2},{4,5},{5,4},{6,7},{7,6},{8,9},{9,8},{10,11... | collective-permute-start | bytes 2359304 | tf_op jit(solution)/shard_map/cond/branch_1_fun/ppermute | solution.py:36
  68.5 20.8 %collective-permute-start.13 = (bf16[512,768]{1,0:T(8,128)(2,1)}, bf16[512,768]{1,0:T(8,128)(2,1)S(1)}, u32[]{:S(2)}, u32[]{:S(2)}) collective-permute-start(bf16[512,768]{1,0:T(8,128)(2,1)} %get-tuple-element.115), channel_id=1, source_target_pairs={{2,0},{3,1},{4,2},{5,3},{6,4},{7,5},{8,6},{9,7},{10,8},{11,9},{12,... | collective-permute-start | bytes 2359304 | tf_op jit(solution)/shard_map/ppermute | solution.py:32
  70.4 16.8 %copy-start.1 = (bf16[512,768]{1,0:T(8,128)(2,1)S(1)}, bf16[512,768]{1,0:T(8,128)(2,1)}, u32[]{:S(2)}) copy-start(bf16[512,768]{1,0:T(8,128)(2,1)} %get-tuple-element.116.kept_ref) | copy-start | bytes 2359300
  70.4 4.1 %collective-permute-start.4 = (bf16[512,512]{1,0:T(8,128)(2,1)}, bf16[512,512]{1,0:T(8,128)(2,1)S(1)}, u32[]{:S(2)}, u32[]{:S(2)}) collective-permute-start(bf16[512,512]{1,0:T(8,128)(2,1)} %get-tuple-element.80.refs_4_.refs_5_), channel_id=1, source_target_pairs={{1,0},{3,2},{5,4},{7,6},{9,8},{11,10},{13,12},{15,14},{17,16},{19,... | collective-permute-start | bytes 1572872 | tf_op jit(solution)/shard_map/cond/branch_1_fun/ppermute | solution.py:44
  81.1 2.0 %collective-permute-start.5 = (bf16[512,512]{1,0:T(8,128)(2,1)S(1)}, bf16[512,512]{1,0:T(8,128)(2,1)S(1)}, u32[]{:S(2)}, u32[]{:S(2)}) collective-permute-start(bf16[512,512]{1,0:T(8,128)(2,1)S(1)} %get-tuple-element.86), channel_id=1, source_target_pairs={{0,1},{1,0},{2,3},{3,2},{4,5},{5,4},{6,7},{7,6},{8,9},{9,8},{10,11... | collective-permute-start | bytes 1572872 | tf_op jit(solution)/shard_map/cond/branch_1_fun/ppermute | solution.py:36
  83.2 7.1 %copy-start.4 = (bf16[256,4096]{1,0:T(8,128)(2,1)}, bf16[256,4096]{1,0:T(8,128)(2,1)S(1)}, u32[]{:S(2)}) copy-start(bf16[256,4096]{1,0:T(8,128)(2,1)S(1)} %get-tuple-element.105) | copy-start | bytes 6291460
  83.2 17.9 %collective-permute-start.12 = (bf16[512,512]{1,0:T(8,128)(2,1)S(1)}, bf16[512,512]{1,0:T(8,128)(2,1)S(1)}, u32[]{:S(2)}, u32[]{:S(2)}) collective-permute-start(bf16[512,512]{1,0:T(8,128)(2,1)S(1)} %get-tuple-element.112), channel_id=1, source_target_pairs={{2,0},{3,1},{4,2},{5,3},{6,4},{7,5},{8,6},{9,7},{10,8},{11,9},{12,... | collective-permute-start | bytes 1572872 | tf_op jit(solution)/shard_map/ppermute | solution.py:32

commit v5 on v4

--- a/solution.py
+++ b/solution.py
@@ -11,8 +11,9 @@
 HEAD_SIZE = 128
 WINDOW_LENGTH = 512
 AXES = ("seq", "head")
-GROUPS = ((6,), (6,), (4,))
+GROUPS = ((6,), (8,), (2,))
 STEP = 2
+PIECES = 4
 UNIT = 128
 STRIP = 32
 VMEM_LIMIT = 16 * 1024 * 1024
@@ -250,36 +251,59 @@
     )(*operands)
 
 
-def pack_kernel(first, k_ref, v_ref, *refs):
-    outs, sems = refs[:-1], refs[-1]
-    rows, wide = k_ref.shape[0], outs[0].shape[1]
+def pack_kernel(first, k_ref, v_ref, out_ref, sems):
+    rows, wide = k_ref.shape[0], out_ref.shape[1]
     columns = pl.ds(first * HEAD_SIZE, wide)
+    height = rows // PIECES
     copies = []
-    for i, ref in enumerate((k_ref, v_ref)):
-        place = outs[i] if len(outs) == 2 else outs[0].at[pl.ds(i * rows, rows)]
-        copies.append(pltpu.make_async_copy(ref.at[:, columns], place, sems.at[i]))
+    for i in range(2 * PIECES):
+        ref = (k_ref, v_ref)[i // PIECES]
+        source = ref.at[pl.ds(i % PIECES * height, height), columns]
+        copies.append(
+            pltpu.make_async_copy(source, out_ref.at[pl.ds(i * height, height)], sems.at[i])
+        )
         copies[-1].start()
     for copy in copies:
         copy.wait()
 
 
-def pack(keys, values, first, heads, arrays):
+def pack(keys, values, first, heads):
     rows, wide = keys.shape[0], heads * HEAD_SIZE
     keys, values = (pltpu.with_memory_space_constraint(x, pltpu.HBM) for x in (keys, values))
-    shape = (2 * rows // arrays, wide)
+    shape = (2 * rows, wide)
     return pl.pallas_call(
         functools.partial(pack_kernel, first),
         in_specs=[pl.BlockSpec(memory_space=pl.ANY)] * 2,
-        out_specs=[pl.BlockSpec(memory_space=pltpu.VMEM)] * arrays,
-        out_shape=[pltpu.VMEM(shape, keys.dtype)] * arrays,
-        scratch_shapes=[pltpu.SemaphoreType.DMA((2,))],
+        out_specs=pl.BlockSpec(memory_space=pltpu.VMEM),
+        out_shape=pltpu.VMEM(shape, keys.dtype),
+        scratch_shapes=[pltpu.SemaphoreType.DMA((2 * PIECES,))],
         compiler_params=pltpu.CompilerParams(vmem_limit_bytes=4 * 1024 * 1024),
         name="pack",
     )(keys, values)
 
 
 SMALL = pltpu.CompilerParams(vmem_limit_bytes=6 * 1024 * 1024)
-FREE = pl.CostEstimate(flops=1, bytes_accessed=1, transcendentals=0)
+
+
+def cost(flops):
+    return pl.CostEstimate(flops=flops, bytes_accessed=1, transcendentals=0)
+
+
+FREE = cost(1)
+
+
+def step(x, flops):
+    anywhere = pl.BlockSpec(memory_space=pl.ANY)
+    return pl.pallas_call(
+        lambda x_ref, out_ref: None,
+        in_specs=[anywhere],
+        out_specs=anywhere,
+        out_shape=jax.ShapeDtypeStruct(x.shape, x.dtype),
+        input_output_aliases={0: 0},
+        compiler_params=SMALL,
+        cost_estimate=cost(flops),
+        name="step",
+    )(x)
 
 
 def in_vmem(*arrays):
@@ -348,7 +372,7 @@
         scratch_shapes=[pltpu.VMEM(kept.shape, kept.dtype), pltpu.SemaphoreType.DMA((2,))],
         input_output_aliases=aliases,
         compiler_params=SMALL,
-        cost_estimate=pl.CostEstimate(flops=600000000, bytes_accessed=1, transcendentals=0),
+        cost_estimate=cost(3000000000 if first == 0 else 1),
         name="finish",
     )(*operands)
 
@@ -372,9 +396,11 @@
         return (dquery, total[:rows], total[rows:])
 
     starts = [sum(map(sum, GROUPS[:c])) for c in range(len(GROUPS))]
-    packed = [pack(keys, values, start, sum(group), 1)[0] for start, group in zip(starts, GROUPS)]
+    packed = [pack(keys, values, start, sum(group)) for start, group in zip(starts, GROUPS)]
     far = [shifted(x, 2, devices) for x in packed]
     early = [to_odd(x, devices) for x in packed]
+    far[-1], early[-1] = lax.optimization_barrier((far[-1], early[-1]))
+    far[0], far[-1] = step(far[0], 3000000000), step(far[-1], 6500000000)
 
     def work(start, first, heads, received, own_near, near, dquery):
         if near is None:
@@ -405,8 +431,6 @@
                 near,
                 dquery,
             )
-            if len(sums) == 1:
-                send = after(send, *far)
             sums.append((first, kept, shifted(send, -2, devices)))
             first += heads
     grads = None

time: 103 us -> 104 us (level)
  waiting for transfers between devices: 35.4 us -> 36.8 us
    ppermute x6, waiting for transfers between devices: 20.9 us -> 22.3 us  [shifted(): return lax.ppermute(x, AXES, pairs)]
  transfers between devices with their start and end apart: 15 -> 15, of which waited for: 9 -> 10; matrix products, arithmetic and copies ran while one was open for 0% -> 0% of each run, Pallas kernels for 33% -> 33%
where the time goes in v5:
time: 104 us; the launch traced here: 103 us
  waiting for transfers between devices  36.8 us (35%)
  Pallas kernels  35.7 us (34%)
  starting transfers between devices  28.4 us (27%)
    pallas_call x3, Pallas kernels, attend(): pl.pallas_call(functools.partial(kernel, rows, back, group, len(near) ==...  24 us
    ppermute x6, waiting for transfers between devices, shifted(): return lax.ppermute(x, AXES, pairs)  22.3 us
    ppermute x6, starting transfers between devices, shifted(): return lax.ppermute(x, AXES, pairs)  19.8 us
    ppermute x3, waiting for transfers between devices, to_even(): return lax.ppermute(x, AXES, [(i + 1, i) for i in range(0, devices, 2)])  8.47 us
    ppermute x3, waiting for transfers between devices, swapped(): return lax.ppermute(x, AXES, [(i, i ^ 1) for i in range(devices)])  6.06 us
    pallas_call x3, Pallas kernels, pack(): pl.pallas_call(functools.partial(pack_kernel, first), in_specs=[pl.BlockS...  5.26 us
    ppermute x3, starting transfers between devices, to_even(): return lax.ppermute(x, AXES, [(i + 1, i) for i in range(0, devices, 2)])  4 us
    ppermute x3, starting transfers between devices, to_odd(): return lax.ppermute(x, AXES, [(i, i + 1) for i in range(0, devices, 2)])  3.99 us
  transfers between devices with their start and end apart: 15, of which 10 were waited for; matrix products, arithmetic and copies ran while one was open for 0% of the time, Pallas kernels for 33%

profile of v5, /device:TPU:14, one launch (start us, length us, event | category | flops | bytes accessed | tf_op | source)
XLA Modules:
  0.0 103.0 jit_solution(8611433985188794765)
XLA Ops:
  0.6 1.3 %pack.3 = bf16[512,768]{1,0:T(8,128)(2,1)S(1)} custom-call(bf16[256,2048]{1,0:T(8,128)(2,1)} %k_ref.5, bf16[256,2048]{1,0:T(8,128)(2,1)} %v_ref.5), custom_call_target="tpu_custom_call" | custom-call | tf_op jit(solution)/shard_map/pack/pallas_call | solution.py:274
  1.9 0.0 copy-start.11
  1.9 3.4 %collective-permute-start.6 = (bf16[512,768]{1,0:T(8,128)(2,1)S(1)}, bf16[512,768]{1,0:T(8,128)(2,1)S(1)}, u32[]{:S(2)}, u32[]{:S(2)}) collective-permute-start(bf16[512,768]{1,0:T(8,128)(2,1)S(1)} %pack.3), channel_id=1, source_target_pairs={{0,2},{1,3},{2,4},{3,5},{4,6},{5,7},{6,8},{7,9},{8,10},{9,11},{10,... | collective-permute-start | bytes 2359304 | tf_op jit(solution)/shard_map/ppermute | solution.py:33
  5.3 2.3 %pack.4 = bf16[512,1024]{1,0:T(8,128)(2,1)} custom-call(bf16[256,2048]{1,0:T(8,128)(2,1)} %k_ref.5, bf16[256,2048]{1,0:T(8,128)(2,1)} %v_ref.5), custom_call_target="tpu_custom_call" | custom-call | tf_op jit(solution)/shard_map/pack/pallas_call | solution.py:274
  7.7 3.4 %collective-permute-start.8 = (bf16[512,1024]{1,0:T(8,128)(2,1)}, bf16[512,1024]{1,0:T(8,128)(2,1)S(1)}, u32[]{:S(2)}, u32[]{:S(2)}) collective-permute-start(bf16[512,1024]{1,0:T(8,128)(2,1)} %pack.4), channel_id=1, source_target_pairs={{0,2},{1,3},{2,4},{3,5},{4,6},{5,7},{6,8},{7,9},{8,10},{9,11},{10,... | collective-permute-start | bytes 3145736 | tf_op jit(solution)/shard_map/ppermute | solution.py:33
  11.1 1.4 %collective-permute-start.9 = (bf16[512,1024]{1,0:T(8,128)(2,1)}, bf16[512,1024]{1,0:T(8,128)(2,1)S(1)}, u32[]{:S(2)}, u32[]{:S(2)}) collective-permute-start(bf16[512,1024]{1,0:T(8,128)(2,1)} %pack.4), channel_id=1, source_target_pairs={{0,1},{2,3},{4,5},{6,7},{8,9},{10,11},{12,13},{14,15},{16,17},{18,... | collective-permute-start | bytes 3145736 | tf_op jit(solution)/shard_map/ppermute | solution.py:41
  12.5 1.3 %collective-permute-start.7 = (bf16[512,768]{1,0:T(8,128)(2,1)S(1)}, bf16[512,768]{1,0:T(8,128)(2,1)S(1)}, u32[]{:S(2)}, u32[]{:S(2)}) collective-permute-start(bf16[512,768]{1,0:T(8,128)(2,1)S(1)} %pack.3), channel_id=1, source_target_pairs={{0,1},{2,3},{4,5},{6,7},{8,9},{10,11},{12,13},{14,15},{16,17},{18,... | collective-permute-start | bytes 2359304 | tf_op jit(solution)/shard_map/ppermute | solution.py:41
  13.8 1.6 %pack.5 = bf16[512,256]{1,0:T(8,128)(2,1)} custom-call(bf16[256,2048]{1,0:T(8,128)(2,1)} %k_ref.5, bf16[256,2048]{1,0:T(8,128)(2,1)} %v_ref.5), custom_call_target="tpu_custom_call" | custom-call | tf_op jit(solution)/shard_map/pack/pallas_call | solution.py:274
  15.5 3.3 %collective-permute-start.10 = (bf16[512,256]{1,0:T(8,128)(2,1)}, bf16[512,256]{1,0:T(8,128)(2,1)}, u32[]{:S(2)}, u32[]{:S(2)}) collective-permute-start(bf16[512,256]{1,0:T(8,128)(2,1)} %pack.5), channel_id=1, source_target_pairs={{0,2},{1,3},{2,4},{3,5},{4,6},{5,7},{6,8},{7,9},{8,10},{9,11},{10,... | collective-permute-start | bytes 786440 | tf_op jit(solution)/shard_map/ppermute | solution.py:33
  18.8 0.0 copy-done.11
  18.9 0.0 copy-start.2
  18.9 0.0 copy-start.4
  18.9 0.0 copy-start.7
  18.9 0.0 copy-start.9
  18.9 5.3 %collective-permute-done.6.x_ref = bf16[512,768]{1,0:T(8,128)(2,1)S(1)} collective-permute-done((bf16[512,768]{1,0:T(8,128)(2,1)S(1)}, bf16[512,768]{1,0:T(8,128)(2,1)S(1)}, u32[]{:S(2)}, u32[]{:S(2)}) %collective-permute-start.6) | collective-permute-done | bytes 786464 | tf_op jit(solution)/shard_map/ppermute | solution.py:33
  24.3 1.3 %collective-permute-start.11 = (bf16[512,256]{1,0:T(8,128)(2,1)}, bf16[512,256]{1,0:T(8,128)(2,1)S(1)}, u32[]{:S(2)}, u32[]{:S(2)}) collective-permute-start(bf16[512,256]{1,0:T(8,128)(2,1)} %pack.5), channel_id=1, source_target_pairs={{0,1},{2,3},{4,5},{6,7},{8,9},{10,11},{12,13},{14,15},{16,17},{18,... | collective-permute-start | bytes 786440 | tf_op jit(solution)/shard_map/ppermute | solution.py:41
  25.6 0.0 collective-permute-done.7
  25.6 0.0 copy-done.2
  25.6 0.0 copy-done.4
  25.6 0.0 copy-done.7
  25.6 0.0 copy-done.9
  25.6 17.1 %conditional.3 = (bf16[256,4096]{1,0:T(8,128)(2,1)S(1)}, bf16[512,768]{1,0:T(8,128)(2,1)}, bf16[512,768]{1,0:T(8,128)(2,1)}) conditional(s32[]{:T(128)} %bitcast, () %tuple.33, (bf16[512,768]{1,0:T(8,128)(2,1)S(1)}, s32[8]{0:T(128)S(1)}, bf16[256,4096]{1,0:T(8,128)(2,1)S(1)}, bf16[256,4096]{1,0:T(8,128)(2,1)S(1)}, bf16[256,2048]{1,0:T(8,128)(2,1)S(1)}, ...), branch_computations={%region_0.0_spmd, %region_1.0_spmd} | conditional | flops 2 | bytes 9437318 | solution.py:425
  25.6 1.3 %collective-permute-start = (bf16[512,768]{1,0:T(8,128)(2,1)S(1)}, bf16[512,768]{1,0:T(8,128)(2,1)S(1)}, u32[]{:S(2)}, u32[]{:S(2)}) collective-permute-start(bf16[512,768]{1,0:T(8,128)(2,1)S(1)} %get-tuple-element.53.refs_4_.refs_5_), channel_id=1, source_target_pairs={{1,0},{3,2},{5,4},{7,6},{9,8},{11,10},{13,12},{15,14},{17,16},{19,... | collective-permute-start | bytes 2359304 | tf_op jit(solution)/shard_map/cond/branch_1_fun/ppermute | solution.py:45
  26.9 2.9 %collective-permute-done.refs_0_.refs_1_ = bf16[512,768]{1,0:T(8,128)(2,1)S(1)} collective-permute-done((bf16[512,768]{1,0:T(8,128)(2,1)S(1)}, bf16[512,768]{1,0:T(8,128)(2,1)S(1)}, u32[]{:S(2)}, u32[]{:S(2)}) %collective-permute-start) | collective-permute-done | bytes 786464 | tf_op jit(solution)/shard_map/cond/branch_1_fun/ppermute | solution.py:45
  29.8 8.6 %attend.3 = (bf16[256,4096]{1,0:T(8,128)(2,1)S(1)}, bf16[512,768]{1,0:T(8,128)(2,1)S(1)}, bf16[512,768]{1,0:T(8,128)(2,1)S(1)}, bf16[512,768]{1,0:T(8,128)(2,1)S(1)}) custom-call(s32[8]{0:T(128)S(1)} %get-tuple-element.48.starts_ref, bf16[256,4096]{1,0:T(8,128)(2,1)S(1)} %get-tuple-element.49.q_ref, bf16[256,4096]{1,0:T(8,128)(2,1)S(1)} %get-tuple-element.50.g_ref, ...), custom_call_target="tpu_custom_call" | custom-call | flops 1 | bytes 1 | tf_op jit(solution)/shard_map/cond/branch_1_fun/attend/pallas_call | solution.py:235
  38.4 0.2 collective-permute-start.1
  38.6 2.1 %collective-permute-done.1.back_ref = bf16[512,768]{1,0:T(8,128)(2,1)S(1)} collective-permute-done((bf16[512,768]{1,0:T(8,128)(2,1)S(1)}, bf16[512,768]{1,0:T(8,128)(2,1)S(1)}, u32[]{:S(2)}, u32[]{:S(2)}) %collective-permute-start.1) | collective-permute-done | bytes 786464 | tf_op jit(solution)/shard_map/cond/branch_1_fun/ppermute | solution.py:37
  40.8 1.1 %merge.3 = (bf16[512,768]{1,0:T(8,128)(2,1)}, bf16[512,768]{1,0:T(8,128)(2,1)S(1)}) custom-call(bf16[512,768]{1,0:T(8,128)(2,1)S(1)} %get-tuple-element.56.far_ref, bf16[512,768]{1,0:T(8,128)(2,1)S(1)} %get-tuple-element.57.own_ref, bf16[512,768]{1,0:T(8,128)(2,1)S(1)} %collective-permute-done.1.back_ref), custom_call_target="tpu_custom_call" | custom-call | flops 1 | bytes 1 | tf_op jit(solution)/shard_map/cond/branch_1_fun/merge/pallas_call | solution.py:331
  41.9 0.9 copy-done
  42.7 3.3 %collective-permute-start.14 = (bf16[512,768]{1,0:T(8,128)(2,1)}, bf16[512,768]{1,0:T(8,128)(2,1)}, u32[]{:S(2)}, u32[]{:S(2)}) collective-permute-start(bf16[512,768]{1,0:T(8,128)(2,1)} %get-tuple-element.119), channel_id=1, source_target_pairs={{2,0},{3,1},{4,2},{5,3},{6,4},{7,5},{8,6},{9,7},{10,8},{11,9},{12,... | collective-permute-start | bytes 2359304 | tf_op jit(solution)/shard_map/ppermute | solution.py:33
  46.1 0.7 collective-permute-done.8
  46.7 0.0 collective-permute-done.9
  46.7 20.4 %conditional.4 = (bf16[256,4096]{1,0:T(8,128)(2,1)S(1)}, bf16[512,1024]{1,0:T(8,128)(2,1)}, bf16[512,1024]{1,0:T(8,128)(2,1)S(1)}) conditional(s32[]{:T(128)} %bitcast, bf16[256,4096]{1,0:T(8,128)(2,1)S(1)} %get-tuple-element.109, (bf16[512,1024]{1,0:T(8,128)(2,1)S(1)}, s32[8]{0:T(128)S(1)}, bf16[256,4096]{1,0:T(8,128)(2,1)}, ...), branch_computations={%region_2.0_spmd, %region_3.0_spmd} | conditional | flops 2 | bytes 8388714 | solution.py:425
  46.7 1.3 %collective-permute-start.2 = (bf16[512,1024]{1,0:T(8,128)(2,1)S(1)}, bf16[512,1024]{1,0:T(8,128)(2,1)S(1)}, u32[]{:S(2)}, u32[]{:S(2)}) collective-permute-start(bf16[512,1024]{1,0:T(8,128)(2,1)S(1)} %get-tuple-element.66.refs_4_.refs_5_), channel_id=1, source_target_pairs={{1,0},{3,2},{5,4},{7,6},{9,8},{11,10},{13,12},{15,14},{17,16},{19,... | collective-permute-start | bytes 3145736 | tf_op jit(solution)/shard_map/cond/branch_1_fun/ppermute | solution.py:45
  48.0 3.3 %collective-permute-done.2.refs_0_.refs_1_ = bf16[512,1024]{1,0:T(8,128)(2,1)S(1)} collective-permute-done((bf16[512,1024]{1,0:T(8,128)(2,1)S(1)}, bf16[512,1024]{1,0:T(8,128)(2,1)S(1)}, u32[]{:S(2)}, u32[]{:S(2)}) %collective-permute-start.2) | collective-permute-done | bytes 1048608 | tf_op jit(solution)/shard_map/cond/branch_1_fun/ppermute | solution.py:45
  51.3 11.8 %attend.4 = (bf16[256,4096]{1,0:T(8,128)(2,1)S(1)}, bf16[512,1024]{1,0:T(8,128)(2,1)S(1)}, bf16[512,1024]{1,0:T(8,128)(2,1)S(1)}, bf16[512,1024]{1,0:T(8,128)(2,1)S(1)}) custom-call(s32[8]{0:T(128)S(1)} %get-tuple-element.61.starts_ref, bf16[256,4096]{1,0:T(8,128)(2,1)} %get-tuple-element.62.q_ref, ...), custom_call_target="tpu_custom_call", output_to_operand_aliasing={{0}: (11, {})} | custom-call | flops 1 | bytes 1 | tf_op jit(solution)/shard_map/cond/branch_1_fun/attend/pallas_call | solution.py:235
  63.1 0.2 collective-permute-start.3
  63.3 2.5 %collective-permute-done.3.back_ref = bf16[512,1024]{1,0:T(8,128)(2,1)S(1)} collective-permute-done((bf16[512,1024]{1,0:T(8,128)(2,1)S(1)}, bf16[512,1024]{1,0:T(8,128)(2,1)S(1)}, u32[]{:S(2)}, u32[]{:S(2)}) %collective-permute-start.3) | collective-permute-done | bytes 1048608 | tf_op jit(solution)/shard_map/cond/branch_1_fun/ppermute | solution.py:37
  65.8 1.3 %merge.4 = (bf16[512,1024]{1,0:T(8,128)(2,1)}, bf16[512,1024]{1,0:T(8,128)(2,1)S(1)}) custom-call(bf16[512,1024]{1,0:T(8,128)(2,1)S(1)} %get-tuple-element.70.far_ref, bf16[512,1024]{1,0:T(8,128)(2,1)S(1)} %get-tuple-element.71.own_ref, bf16[512,1024]{1,0:T(8,128)(2,1)S(1)} %collective-permute-done.3.back_ref), custom_call_target="tpu_custom_call" | custom-call | flops 1 | bytes 1 | tf_op jit(solution)/shard_map/cond/branch_1_fun/merge/pallas_call | solution.py:331
  67.1 3.6 %collective-permute-start.13 = (bf16[512,1024]{1,0:T(8,128)(2,1)}, bf16[512,1024]{1,0:T(8,128)(2,1)S(1)}, u32[]{:S(2)}, u32[]{:S(2)}) collective-permute-start(bf16[512,1024]{1,0:T(8,128)(2,1)} %get-tuple-element.117), channel_id=1, source_target_pairs={{2,0},{3,1},{4,2},{5,3},{6,4},{7,5},{8,6},{9,7},{10,8},{11,9},{12,... | collective-permute-start | bytes 3145736 | tf_op jit(solution)/shard_map/ppermute | solution.py:33
  70.7 0.0 collective-permute-done.10.x_ref
  70.7 0.0 collective-permute-done.11
  70.8 0.0 copy-done.3
  70.8 0.0 copy-done.5
  70.8 0.0 copy-done.8
  70.8 0.0 copy-done.10
  70.8 0.0 copy-start.1
  70.8 9.1 %conditional.5 = (bf16[256,4096]{1,0:T(8,128)(2,1)S(1)}, bf16[512,256]{1,0:T(8,128)(2,1)S(1)}, bf16[512,256]{1,0:T(8,128)(2,1)S(1)}) conditional(s32[]{:T(128)} %bitcast, bf16[256,4096]{1,0:T(8,128)(2,1)S(1)} %get-tuple-element.110, (bf16[512,256]{1,0:T(8,128)(2,1)}, s32[8]{0:T(128)S(1)}, bf16[256,4096]{1,0:T(8,128)(2,1)S(1)}, ...), branch_computations={%region_4.0_spmd, %region_5.0_spmd} | conditional | flops 2 | bytes 2097258 | solution.py:425
  70.8 1.4 %collective-permute-start.4 = (bf16[512,256]{1,0:T(8,128)(2,1)}, bf16[512,256]{1,0:T(8,128)(2,1)S(1)}, u32[]{:S(2)}, u32[]{:S(2)}) collective-permute-start(bf16[512,256]{1,0:T(8,128)(2,1)} %get-tuple-element.80.refs_4_.refs_5_), channel_id=1, source_target_pairs={{1,0},{3,2},{5,4},{7,6},{9,8},{11,10},{13,12},{15,14},{17,16},{19,... | collective-permute-start | bytes 786440 | tf_op jit(solution)/shard_map/cond/branch_1_fun/ppermute | solution.py:45
  72.3 2.3 %collective-permute-done.4.refs_0_.refs_1_ = bf16[512,256]{1,0:T(8,128)(2,1)S(1)} collective-permute-done((bf16[512,256]{1,0:T(8,128)(2,1)}, bf16[512,256]{1,0:T(8,128)(2,1)S(1)}, u32[]{:S(2)}, u32[]{:S(2)}) %collective-permute-start.4) | collective-permute-done | bytes 262176 | tf_op jit(solution)/shard_map/cond/branch_1_fun/ppermute | solution.py:45
  74.6 3.6 %attend.5 = (bf16[256,4096]{1,0:T(8,128)(2,1)S(1)}, bf16[512,256]{1,0:T(8,128)(2,1)S(1)}, bf16[512,256]{1,0:T(8,128)(2,1)S(1)}, bf16[512,256]{1,0:T(8,128)(2,1)S(1)}) custom-call(s32[8]{0:T(128)S(1)} %get-tuple-element.75.starts_ref, bf16[256,4096]{1,0:T(8,128)(2,1)S(1)} %get-tuple-element.76.q_ref, ...), custom_call_target="tpu_custom_call", output_to_operand_aliasing={{0}: (11, {})} | custom-call | flops 1 | bytes 1 | tf_op jit(solution)/shard_map/cond/branch_1_fun/attend/pallas_call | solution.py:235
  78.2 0.2 collective-permute-start.5
  78.4 1.4 %collective-permute-done.5.back_ref = bf16[512,256]{1,0:T(8,128)(2,1)S(1)} collective-permute-done((bf16[512,256]{1,0:T(8,128)(2,1)S(1)}, bf16[512,256]{1,0:T(8,128)(2,1)S(1)}, u32[]{:S(2)}, u32[]{:S(2)}) %collective-permute-start.5) | collective-permute-done | bytes 262176 | tf_op jit(solution)/shard_map/cond/branch_1_fun/ppermute | solution.py:37
  79.8 0.1 merge.5
  79.9 0.0 copy-start.6
  79.9 2.8 %collective-permute-start.12 = (bf16[512,256]{1,0:T(8,128)(2,1)S(1)}, bf16[512,256]{1,0:T(8,128)(2,1)S(1)}, u32[]{:S(2)}, u32[]{:S(2)}) collective-permute-start(bf16[512,256]{1,0:T(8,128)(2,1)S(1)} %get-tuple-element.115), channel_id=1, source_target_pairs={{2,0},{3,1},{4,2},{5,3},{6,4},{7,5},{8,6},{9,7},{10,8},{11,9},{12,... | collective-permute-start | bytes 786440 | tf_op jit(solution)/shard_map/ppermute | solution.py:33
  82.7 0.0 collective-permute-done.14.home_ref
  82.7 0.0 copy-done.1
  82.7 2.1 %finish.3 = (bf16[256,2048]{1,0:T(8,128)(2,1)}, bf16[256,2048]{1,0:T(8,128)(2,1)}) custom-call(bf16[512,768]{1,0:T(8,128)(2,1)S(1)} %copy-done.1, bf16[512,768]{1,0:T(8,128)(2,1)} %collective-permute-done.14.home_ref), custom_call_target="tpu_custom_call" | custom-call | flops 3000000000 | bytes 1 | tf_op jit(solution)/shard_map/finish/pallas_call | solution.py:367
  84.8 0.0 copy-done.6
  84.9 12.5 %collective-permute-done.13.home_ref = bf16[512,1024]{1,0:T(8,128)(2,1)S(1)} collective-permute-done((bf16[512,1024]{1,0:T(8,128)(2,1)}, bf16[512,1024]{1,0:T(8,128)(2,1)S(1)}, u32[]{:S(2)}, u32[]{:S(2)}) %collective-permute-start.13) | collective-permute-done | bytes 1048608 | tf_op jit(solution)/shard_map/ppermute | solution.py:33
  97.3 1.1 %finish.4 = (bf16[256,2048]{1,0:T(8,128)(2,1)}, bf16[256,2048]{1,0:T(8,128)(2,1)}) custom-call(bf16[512,1024]{1,0:T(8,128)(2,1)S(1)} %get-tuple-element.116.kept_ref, bf16[512,1024]{1,0:T(8,128)(2,1)S(1)} %collective-permute-done.13.home_ref, bf16[256,2048]{1,0:T(8,128)(2,1)} %get-tuple-element.120.refs_0_, ...), custom_call_target="tpu_custom_call", output_to_operand_aliasing={{0}: (2, {}), {1}: (3, {})} | custom-call | flops 1 | bytes 1 | tf_op jit(solution)/shard_map/finish/pallas_call | solution.py:367
  98.4 3.8 %collective-permute-done.12.home_ref = bf16[512,256]{1,0:T(8,128)(2,1)S(1)} collective-permute-done((bf16[512,256]{1,0:T(8,128)(2,1)S(1)}, bf16[512,256]{1,0:T(8,128)(2,1)S(1)}, u32[]{:S(2)}, u32[]{:S(2)}) %collective-permute-start.12) | collective-permute-done | bytes 262176 | tf_op jit(solution)/shard_map/ppermute | solution.py:33
  102.2 0.7 finish.5
  (7 shorter events, 0.0 us)
Async XLA Ops:
  1.9 16.9 %copy-start.11 = (s32[8]{0:T(128)S(1)}, s32[8]{0:T(128)}, u32[]{:S(2)}) copy-start(s32[8]{0:T(128)} %param.15) | copy-start | bytes 100
  1.9 22.3 %collective-permute-start.6 = (bf16[512,768]{1,0:T(8,128)(2,1)S(1)}, bf16[512,768]{1,0:T(8,128)(2,1)S(1)}, u32[]{:S(2)}, u32[]{:S(2)}) collective-permute-start(bf16[512,768]{1,0:T(8,128)(2,1)S(1)} %pack.3), channel_id=1, source_target_pairs={{0,2},{1,3},{2,4},{3,5},{4,6},{5,7},{6,8},{7,9},{8,10},{9,11},{10,... | collective-permute-start | bytes 2359304 | tf_op jit(solution)/shard_map/ppermute | solution.py:33
  7.7 39.1 %collective-permute-start.8 = (bf16[512,1024]{1,0:T(8,128)(2,1)}, bf16[512,1024]{1,0:T(8,128)(2,1)S(1)}, u32[]{:S(2)}, u32[]{:S(2)}) collective-permute-start(bf16[512,1024]{1,0:T(8,128)(2,1)} %pack.4), channel_id=1, source_target_pairs={{0,2},{1,3},{2,4},{3,5},{4,6},{5,7},{6,8},{7,9},{8,10},{9,11},{10,... | collective-permute-start | bytes 3145736 | tf_op jit(solution)/shard_map/ppermute | solution.py:33
  11.1 35.6 %collective-permute-start.9 = (bf16[512,1024]{1,0:T(8,128)(2,1)}, bf16[512,1024]{1,0:T(8,128)(2,1)S(1)}, u32[]{:S(2)}, u32[]{:S(2)}) collective-permute-start(bf16[512,1024]{1,0:T(8,128)(2,1)} %pack.4), channel_id=1, source_target_pairs={{0,1},{2,3},{4,5},{6,7},{8,9},{10,11},{12,13},{14,15},{16,17},{18,... | collective-permute-start | bytes 3145736 | tf_op jit(solution)/shard_map/ppermute | solution.py:41
  12.5 13.1 %collective-permute-start.7 = (bf16[512,768]{1,0:T(8,128)(2,1)S(1)}, bf16[512,768]{1,0:T(8,128)(2,1)S(1)}, u32[]{:S(2)}, u32[]{:S(2)}) collective-permute-start(bf16[512,768]{1,0:T(8,128)(2,1)S(1)} %pack.3), channel_id=1, source_target_pairs={{0,1},{2,3},{4,5},{6,7},{8,9},{10,11},{12,13},{14,15},{16,17},{18,... | collective-permute-start | bytes 2359304 | tf_op jit(solution)/shard_map/ppermute | solution.py:41
  15.5 55.3 %collective-permute-start.10 = (bf16[512,256]{1,0:T(8,128)(2,1)}, bf16[512,256]{1,0:T(8,128)(2,1)}, u32[]{:S(2)}, u32[]{:S(2)}) collective-permute-start(bf16[512,256]{1,0:T(8,128)(2,1)} %pack.5), channel_id=1, source_target_pairs={{0,2},{1,3},{2,4},{3,5},{4,6},{5,7},{6,8},{7,9},{8,10},{9,11},{10,... | collective-permute-start | bytes 786440 | tf_op jit(solution)/shard_map/ppermute | solution.py:33
  18.9 6.7 %copy-start.2 = (bf16[256,2048]{1,0:T(8,128)(2,1)S(1)}, bf16[256,2048]{1,0:T(8,128)(2,1)}, u32[]{:S(2)}) copy-start(bf16[256,2048]{1,0:T(8,128)(2,1)} %k_ref.5) | copy-start | bytes 3145732
  18.9 6.7 %copy-start.4 = (bf16[256,2048]{1,0:T(8,128)(2,1)S(1)}, bf16[256,2048]{1,0:T(8,128)(2,1)}, u32[]{:S(2)}) copy-start(bf16[256,2048]{1,0:T(8,128)(2,1)} %v_ref.5) | copy-start | bytes 3145732
  18.9 6.7 %copy-start.7 = (bf16[256,4096]{1,0:T(8,128)(2,1)S(1)}, bf16[256,4096]{1,0:T(8,128)(2,1)}, u32[]{:S(2)}) copy-start(bf16[256,4096]{1,0:T(8,128)(2,1)} %param.11) | copy-start | bytes 6291460
  18.9 6.7 %copy-start.9 = (bf16[256,4096]{1,0:T(8,128)(2,1)S(1)}, bf16[256,4096]{1,0:T(8,128)(2,1)}, u32[]{:S(2)}) copy-start(bf16[256,4096]{1,0:T(8,128)(2,1)} %param.14) | copy-start | bytes 6291460
  24.3 46.5 %collective-permute-start.11 = (bf16[512,256]{1,0:T(8,128)(2,1)}, bf16[512,256]{1,0:T(8,128)(2,1)S(1)}, u32[]{:S(2)}, u32[]{:S(2)}) collective-permute-start(bf16[512,256]{1,0:T(8,128)(2,1)} %pack.5), channel_id=1, source_target_pairs={{0,1},{2,3},{4,5},{6,7},{8,9},{10,11},{12,13},{14,15},{16,17},{18,... | collective-permute-start | bytes 786440 | tf_op jit(solution)/shard_map/ppermute | solution.py:41
  25.6 4.2 %collective-permute-start = (bf16[512,768]{1,0:T(8,128)(2,1)S(1)}, bf16[512,768]{1,0:T(8,128)(2,1)S(1)}, u32[]{:S(2)}, u32[]{:S(2)}) collective-permute-start(bf16[512,768]{1,0:T(8,128)(2,1)S(1)} %get-tuple-element.53.refs_4_.refs_5_), channel_id=1, source_target_pairs={{1,0},{3,2},{5,4},{7,6},{9,8},{11,10},{13,12},{15,14},{17,16},{19,... | collective-permute-start | bytes 2359304 | tf_op jit(solution)/shard_map/cond/branch_1_fun/ppermute | solution.py:45
  38.4 2.4 %collective-permute-start.1 = (bf16[512,768]{1,0:T(8,128)(2,1)S(1)}, bf16[512,768]{1,0:T(8,128)(2,1)S(1)}, u32[]{:S(2)}, u32[]{:S(2)}) collective-permute-start(bf16[512,768]{1,0:T(8,128)(2,1)S(1)} %get-tuple-element.58), channel_id=1, source_target_pairs={{0,1},{1,0},{2,3},{3,2},{4,5},{5,4},{6,7},{7,6},{8,9},{9,8},{10,11... | collective-permute-start | bytes 2359304 | tf_op jit(solution)/shard_map/cond/branch_1_fun/ppermute | solution.py:37
  41.9 0.9 copy-start
  42.7 40.0 %collective-permute-start.14 = (bf16[512,768]{1,0:T(8,128)(2,1)}, bf16[512,768]{1,0:T(8,128)(2,1)}, u32[]{:S(2)}, u32[]{:S(2)}) collective-permute-start(bf16[512,768]{1,0:T(8,128)(2,1)} %get-tuple-element.119), channel_id=1, source_target_pairs={{2,0},{3,1},{4,2},{5,3},{6,4},{7,5},{8,6},{9,7},{10,8},{11,9},{12,... | collective-permute-start | bytes 2359304 | tf_op jit(solution)/shard_map/ppermute | solution.py:33
  46.7 4.5 %collective-permute-start.2 = (bf16[512,1024]{1,0:T(8,128)(2,1)S(1)}, bf16[512,1024]{1,0:T(8,128)(2,1)S(1)}, u32[]{:S(2)}, u32[]{:S(2)}) collective-permute-start(bf16[512,1024]{1,0:T(8,128)(2,1)S(1)} %get-tuple-element.66.refs_4_.refs_5_), channel_id=1, source_target_pairs={{1,0},{3,2},{5,4},{7,6},{9,8},{11,10},{13,12},{15,14},{17,16},{19,... | collective-permute-start | bytes 3145736 | tf_op jit(solution)/shard_map/cond/branch_1_fun/ppermute | solution.py:45
  63.1 2.7 %collective-permute-start.3 = (bf16[512,1024]{1,0:T(8,128)(2,1)S(1)}, bf16[512,1024]{1,0:T(8,128)(2,1)S(1)}, u32[]{:S(2)}, u32[]{:S(2)}) collective-permute-start(bf16[512,1024]{1,0:T(8,128)(2,1)S(1)} %get-tuple-element.72), channel_id=1, source_target_pairs={{0,1},{1,0},{2,3},{3,2},{4,5},{5,4},{6,7},{7,6},{8,9},{9,8},{10,11... | collective-permute-start | bytes 3145736 | tf_op jit(solution)/shard_map/cond/branch_1_fun/ppermute | solution.py:37
  67.1 3.6 %copy-start.3 = (bf16[256,2048]{1,0:T(8,128)(2,1)S(1)}, bf16[256,2048]{1,0:T(8,128)(2,1)}, u32[]{:S(2)}) copy-start(bf16[256,2048]{1,0:T(8,128)(2,1)} %k_ref.5) | copy-start | bytes 3145732
  67.1 3.6 %copy-start.5 = (bf16[256,2048]{1,0:T(8,128)(2,1)S(1)}, bf16[256,2048]{1,0:T(8,128)(2,1)}, u32[]{:S(2)}) copy-start(bf16[256,2048]{1,0:T(8,128)(2,1)} %v_ref.5) | copy-start | bytes 3145732
  67.1 3.6 %copy-start.8 = (bf16[256,4096]{1,0:T(8,128)(2,1)S(1)}, bf16[256,4096]{1,0:T(8,128)(2,1)}, u32[]{:S(2)}) copy-start(bf16[256,4096]{1,0:T(8,128)(2,1)} %param.11) | copy-start | bytes 6291460
  67.1 3.7 %copy-start.10 = (bf16[256,4096]{1,0:T(8,128)(2,1)S(1)}, bf16[256,4096]{1,0:T(8,128)(2,1)}, u32[]{:S(2)}) copy-start(bf16[256,4096]{1,0:T(8,128)(2,1)} %param.14) | copy-start | bytes 6291460
  67.1 30.2 %collective-permute-start.13 = (bf16[512,1024]{1,0:T(8,128)(2,1)}, bf16[512,1024]{1,0:T(8,128)(2,1)S(1)}, u32[]{:S(2)}, u32[]{:S(2)}) collective-permute-start(bf16[512,1024]{1,0:T(8,128)(2,1)} %get-tuple-element.117), channel_id=1, source_target_pairs={{2,0},{3,1},{4,2},{5,3},{6,4},{7,5},{8,6},{9,7},{10,8},{11,9},{12,... | collective-permute-start | bytes 3145736 | tf_op jit(solution)/shard_map/ppermute | solution.py:33
  70.8 11.9 %copy-start.1 = (bf16[512,768]{1,0:T(8,128)(2,1)S(1)}, bf16[512,768]{1,0:T(8,128)(2,1)}, u32[]{:S(2)}) copy-start(bf16[512,768]{1,0:T(8,128)(2,1)} %get-tuple-element.118.kept_ref) | copy-start | bytes 2359300
  70.8 3.8 %collective-permute-start.4 = (bf16[512,256]{1,0:T(8,128)(2,1)}, bf16[512,256]{1,0:T(8,128)(2,1)S(1)}, u32[]{:S(2)}, u32[]{:S(2)}) collective-permute-start(bf16[512,256]{1,0:T(8,128)(2,1)} %get-tuple-element.80.refs_4_.refs_5_), channel_id=1, source_target_pairs={{1,0},{3,2},{5,4},{7,6},{9,8},{11,10},{13,12},{15,14},{17,16},{19,... | collective-permute-start | bytes 786440 | tf_op jit(solution)/shard_map/cond/branch_1_fun/ppermute | solution.py:45
  78.2 1.6 %collective-permute-start.5 = (bf16[512,256]{1,0:T(8,128)(2,1)S(1)}, bf16[512,256]{1,0:T(8,128)(2,1)S(1)}, u32[]{:S(2)}, u32[]{:S(2)}) collective-permute-start(bf16[512,256]{1,0:T(8,128)(2,1)S(1)} %get-tuple-element.86), channel_id=1, source_target_pairs={{0,1},{1,0},{2,3},{3,2},{4,5},{5,4},{6,7},{7,6},{8,9},{9,8},{10,11... | collective-permute-start | bytes 786440 | tf_op jit(solution)/shard_map/cond/branch_1_fun/ppermute | solution.py:37
  79.9 5.0 %copy-start.6 = (bf16[256,4096]{1,0:T(8,128)(2,1)}, bf16[256,4096]{1,0:T(8,128)(2,1)S(1)}, u32[]{:S(2)}) copy-start(bf16[256,4096]{1,0:T(8,128)(2,1)S(1)} %get-tuple-element.106) | copy-start | bytes 6291460
  79.9 22.3 %collective-permute-start.12 = (bf16[512,256]{1,0:T(8,128)(2,1)S(1)}, bf16[512,256]{1,0:T(8,128)(2,1)S(1)}, u32[]{:S(2)}, u32[]{:S(2)}) collective-permute-start(bf16[512,256]{1,0:T(8,128)(2,1)S(1)} %get-tuple-element.115), channel_id=1, source_target_pairs={{2,0},{3,1},{4,2},{5,3},{6,4},{7,5},{8,6},{9,7},{10,8},{11,9},{12,... | collective-permute-start | bytes 786440 | tf_op jit(solution)/shard_map/ppermute | solution.py:33

commit v6 on v3

--- a/solution.py
+++ b/solution.py
@@ -11,7 +11,7 @@
 HEAD_SIZE = 128
 WINDOW_LENGTH = 512
 AXES = ("seq", "head")
-GROUPS = ((6,), (6,), (4,))
+GROUPS = (6, 6, 4)
 STEP = 2
 UNIT = 128
 STRIP = 32
@@ -202,7 +202,7 @@
 
 
 def attend(
-    doc_starts, queries, dout, keys, values, near, others, start, first, heads, buffer, pieces
+    doc_starts, queries, dout, keys, values, near, others, first, heads, buffer, pieces
 ):
     rows, width = keys.shape
     back = 1 + len(others)
@@ -220,7 +220,7 @@
     in_specs = [smem, wide, wide, narrow, narrow]
     for pair in near + others:
         operands += [pair[0], pair[-1]]
-        in_specs += [part(rows, step, first - start, row) for row in (0, 2 - len(pair))]
+        in_specs += [part(rows, step, 0), part(rows, step, 0, 2 - len(pair))]
     if len(near) == 2:
         operands[5:] = [pltpu.with_memory_space_constraint(x, pltpu.VMEM) for x in operands[5:]]
     aliases = {}
@@ -286,7 +286,34 @@
     return [pltpu.with_memory_space_constraint(x, pltpu.VMEM) for x in arrays]
 
 
-def merge_kernel(far_ref, own_ref, back_ref, send_ref, kept_ref):
+def merge_kernel(far_ref, back_ref, out_ref):
+    odd = device_index() % 2 == 1
+
+    @pl.when(odd)
+    def _():
+        out_ref[...] = (
+            far_ref[...].astype(jnp.float32) + back_ref[...].astype(jnp.float32)
+        ).astype(out_ref.dtype)
+
+    @pl.when(jnp.logical_not(odd))
+    def _():
+        out_ref[...] = far_ref[...]
+
+
+def merge(far, back):
+    whole = pl.BlockSpec(memory_space=pltpu.VMEM)
+    return pl.pallas_call(
+        merge_kernel,
+        in_specs=[whole] * 2,
+        out_specs=whole,
+        out_shape=pltpu.VMEM(far.shape, far.dtype),
+        compiler_params=SMALL,
+        cost_estimate=FREE,
+        name="merge",
+    )(*in_vmem(far, back))
+
+
+def merge_kept_kernel(far_ref, own_ref, back_ref, send_ref, kept_ref):
     odd = device_index() % 2 == 1
 
     @pl.when(odd)
@@ -302,26 +329,29 @@
         kept_ref[...] = total.astype(kept_ref.dtype)
 
 
-def merge(far, own, back):
+def merge_kept(far, own, back):
     whole = pl.BlockSpec(memory_space=pltpu.VMEM)
     return pl.pallas_call(
-        merge_kernel,
+        merge_kept_kernel,
         in_specs=[whole] * 3,
         out_specs=[whole] * 2,
         out_shape=[pltpu.VMEM(far.shape, far.dtype)] * 2,
         compiler_params=SMALL,
         cost_estimate=FREE,
-        name="merge",
+        name="merge_kept",
     )(*in_vmem(far, own, back))
 
 
-def finish_kernel(first, kept_ref, home_ref, *refs):
+def finish_kernel(first, terms, own_ref, home_ref, *refs):
     outs, total_ref, sems = refs[-4:-2], refs[-2], refs[-1]
-    rows, wide = kept_ref.shape[0] // 2, kept_ref.shape[1]
+    rows, wide = own_ref.shape[0] // 2, own_ref.shape[1]
+    share = (1 - device_index() % 2).astype(jnp.float32)
     copies = []
     for i, out in enumerate(outs):
         half = slice(i * rows, (i + 1) * rows)
-        total = kept_ref[half].astype(jnp.float32) + home_ref[half].astype(jnp.float32)
+        total = own_ref[half].astype(jnp.float32) + home_ref[half].astype(jnp.float32)
+        if terms == 3:
+            total = total + share * refs[0][half].astype(jnp.float32)
         total_ref[half] = total.astype(total_ref.dtype)
         place = out.at[:, pl.ds(first * HEAD_SIZE, wide)]
         copies.append(pltpu.make_async_copy(total_ref.at[half], place, sems.at[i]))
@@ -330,22 +360,23 @@
         copy.wait()
 
 
-def finish(kept, home, first, width, buffers):
+def finish(own, home, back, first, width, buffers):
     whole = pl.BlockSpec(memory_space=pltpu.VMEM)
     anywhere = pl.BlockSpec(memory_space=pl.ANY)
-    operands = in_vmem(kept, home)
-    in_specs = [whole] * 2
+    operands = in_vmem(own, home, *back)
+    terms = len(operands)
+    in_specs = [whole] * terms
     aliases = {}
     if buffers is not None:
-        aliases = {2: 0, 3: 1}
+        aliases = {terms: 0, terms + 1: 1}
         operands += buffers
         in_specs += [anywhere] * 2
     return pl.pallas_call(
-        functools.partial(finish_kernel, first),
+        functools.partial(finish_kernel, first, terms),
         in_specs=in_specs,
         out_specs=[anywhere] * 2,
-        out_shape=[pltpu.HBM((kept.shape[0] // 2, width), kept.dtype)] * 2,
-        scratch_shapes=[pltpu.VMEM(kept.shape, kept.dtype), pltpu.SemaphoreType.DMA((2,))],
+        out_shape=[pltpu.HBM((own.shape[0] // 2, width), own.dtype)] * 2,
+        scratch_shapes=[pltpu.VMEM(own.shape, own.dtype), pltpu.SemaphoreType.DMA((2,))],
         input_output_aliases=aliases,
         compiler_params=SMALL,
         cost_estimate=FREE,
@@ -362,7 +393,7 @@
         both = jnp.concatenate([keys, values], axis=0)
         halos = [shifted(both, j, devices) for j in range(1, back + 1)]
         dquery, own, *sent = attend(
-            doc_starts, queries, dout, keys, values, [[halos[0]]], [[x] for x in halos[1:]], 0, 0,
+            doc_starts, queries, dout, keys, values, [[halos[0]]], [[x] for x in halos[1:]], 0,
             kv_heads, None, 1,
         )
         total = own.astype(jnp.float32)
@@ -371,48 +402,38 @@
         total = total.astype(jnp.bfloat16)
         return (dquery, total[:rows], total[rows:])
 
-    starts = [sum(map(sum, GROUPS[:c])) for c in range(len(GROUPS))]
-    packed = [pack(keys, values, start, sum(group), 1)[0] for start, group in zip(starts, GROUPS)]
+    starts = [sum(GROUPS[:c]) for c in range(len(GROUPS))]
+    packed = [pack(keys, values, start, heads, 1)[0] for start, heads in zip(starts, GROUPS)]
     far = [shifted(x, 2, devices) for x in packed]
     early = [to_odd(x, devices) for x in packed]
-    far[0] = after(far[0], early[-1])
-
-    def work(start, first, heads, received, own_near, near, dquery):
-        if near is None:
-            near = to_even(received, devices)
+
+    def work(start, heads, received, own_near, dquery):
+        near = to_even(received, devices)
         dquery, own, to_near, to_far = attend(
             doc_starts, queries, dout, keys, values, [[near], [own_near]], [[received]],
-            start, first, heads, dquery, 1,
+            start, heads, dquery, 1,
         )
         returned = swapped(to_near, devices)
-        return near, dquery, *merge(to_far, own, returned)
+        if start == starts[-1]:
+            return dquery, *merge_kept(to_far, own, returned)
+        return dquery, merge(to_far, returned), own, returned
 
     always = (doc_starts[0] | 1) != 0
-    dquery, sums = None, []
-    for start, group, received, own_near in zip(starts, GROUPS, far, early):
-        near, first = None, start
-        for heads in group:
-            def skip(received, own_near, near, dquery):
-                part = jnp.zeros((2 * rows, heads * HEAD_SIZE), received.dtype)
-                near = jnp.zeros_like(received) if near is None else near
-                return near, jnp.zeros_like(queries) if dquery is None else dquery, part, part
-
-            near, dquery, send, kept = lax.cond(
-                always,
-                functools.partial(work, start, first, heads),
-                skip,
-                received,
-                own_near,
-                near,
-                dquery,
-            )
-            if len(sums) == 1:
-                send = after(send, *far)
-            sums.append((first, kept, shifted(send, -2, devices)))
-            first += heads
+    dquery, homes, kept = None, [], []
+    for start, heads, received, own_near in zip(starts, GROUPS, far, early):
+        def skip(received, own_near, dquery):
+            zeros = jnp.zeros_like(received)
+            parts = [zeros] * (2 if start == starts[-1] else 3)
+            return jnp.zeros_like(queries) if dquery is None else dquery, *parts
+
+        dquery, send, own, *returned = lax.cond(
+            always, functools.partial(work, start, heads), skip, received, own_near, dquery
+        )
+        homes.append(shifted(send, -2, devices))
+        kept.append((own, returned))
     grads = None
-    for first, kept, home in sums:
-        grads = finish(kept, home, first, width, grads)
+    for start, home, (own, returned) in zip(starts, homes, kept):
+        grads = finish(own, home, returned, start, width, grads)
     dkey, dvalue = grads
     return (dquery, dkey, dvalue)
 

time: 115 us -> 101 us (0.88)
  waiting for transfers between devices: 47.2 us -> 31.7 us
  Pallas kernels: 35.8 us -> 39.1 us
    ppermute x6, waiting for transfers between devices: 32.9 us -> 16.9 us  [shifted(): return lax.ppermute(x, AXES, pairs)]
    pallas_call x6, Pallas kernels: 6.61 us -> 9.89 us  [the longest x3 5.56 us: finish(): pl.pallas_call(functools.partial(finish_kernel, first, terms), in_specs=i...]
  transfers between devices with their start and end apart: 15 -> 15, of which waited for: 11 -> 10; matrix products, arithmetic and copies ran while one was open for 0% -> 0% of each run, Pallas kernels for 29% -> 37%
where the time goes in v6:
time: 101 us
  Pallas kernels  39.1 us (39%)
  waiting for transfers between devices  31.7 us (31%)
  starting transfers between devices  29.1 us (29%)
    pallas_call x3, Pallas kernels, attend(): pl.pallas_call(functools.partial(kernel, rows, back, group, len(near) ==...  24 us
    ppermute x6, starting transfers between devices, shifted(): return lax.ppermute(x, AXES, pairs)  19.7 us
    ppermute x6, waiting for transfers between devices, shifted(): return lax.ppermute(x, AXES, pairs)  16.9 us
    ppermute x3, waiting for transfers between devices, to_even(): return lax.ppermute(x, AXES, [(i + 1, i) for i in range(0, devices, 2)])  8.47 us
    ppermute x3, waiting for transfers between devices, swapped(): return lax.ppermute(x, AXES, [(i, i ^ 1) for i in range(devices)])  6.34 us
    pallas_call x3, Pallas kernels, finish(): pl.pallas_call(functools.partial(finish_kernel, first, terms), in_specs=i...  5.56 us
    pallas_call x3, Pallas kernels, pack(): pl.pallas_call(functools.partial(pack_kernel, first), in_specs=[pl.BlockS...  5.14 us
    ppermute x3, starting transfers between devices, to_odd(): return lax.ppermute(x, AXES, [(i, i + 1) for i in range(0, devices, 2)])  4.93 us
  transfers between devices with their start and end apart: 15, of which 10 were waited for; matrix products, arithmetic and copies ran while one was open for 0% of the time, Pallas kernels for 37%

profile of v6, /device:TPU:14, one launch (start us, length us, event | category | flops | bytes accessed | tf_op | source)
XLA Modules:
  0.0 100.9 jit_solution(7458715621903064016)
XLA Ops:
  0.6 0.0 copy-start.4
  0.6 1.3 %pack.3 = bf16[512,768]{1,0:T(8,128)(2,1)S(1)} custom-call(bf16[256,2048]{1,0:T(8,128)(2,1)} %k_ref.5, bf16[256,2048]{1,0:T(8,128)(2,1)} %v_ref.5), custom_call_target="tpu_custom_call" | custom-call | tf_op jit(solution)/shard_map/pack/pallas_call | solution.py:270
  1.9 0.0 copy-start.5
  1.9 0.0 copy-start
  2.0 0.0 copy-start.1
  2.0 0.0 copy-start.3
  2.0 3.7 %collective-permute-start.6 = (bf16[512,768]{1,0:T(8,128)(2,1)S(1)}, bf16[512,768]{1,0:T(8,128)(2,1)S(1)}, u32[]{:S(2)}, u32[]{:S(2)}) collective-permute-start(bf16[512,768]{1,0:T(8,128)(2,1)S(1)} %pack.3), channel_id=1, source_target_pairs={{0,2},{1,3},{2,4},{3,5},{4,6},{5,7},{6,8},{7,9},{8,10},{9,11},{10,... | collective-permute-start | bytes 2359304 | tf_op jit(solution)/shard_map/ppermute | solution.py:32
  5.7 1.5 %collective-permute-start.7 = (bf16[512,768]{1,0:T(8,128)(2,1)S(1)}, bf16[512,768]{1,0:T(8,128)(2,1)S(1)}, u32[]{:S(2)}, u32[]{:S(2)}) collective-permute-start(bf16[512,768]{1,0:T(8,128)(2,1)S(1)} %pack.3), channel_id=1, source_target_pairs={{0,1},{2,3},{4,5},{6,7},{8,9},{10,11},{12,13},{14,15},{16,17},{18,... | collective-permute-start | bytes 2359304 | tf_op jit(solution)/shard_map/ppermute | solution.py:40
  7.2 2.0 %pack.4 = bf16[512,768]{1,0:T(8,128)(2,1)} custom-call(bf16[256,2048]{1,0:T(8,128)(2,1)} %k_ref.5, bf16[256,2048]{1,0:T(8,128)(2,1)} %v_ref.5), custom_call_target="tpu_custom_call" | custom-call | tf_op jit(solution)/shard_map/pack/pallas_call | solution.py:270
  9.2 3.4 %collective-permute-start.8 = (bf16[512,768]{1,0:T(8,128)(2,1)}, bf16[512,768]{1,0:T(8,128)(2,1)S(1)}, u32[]{:S(2)}, u32[]{:S(2)}) collective-permute-start(bf16[512,768]{1,0:T(8,128)(2,1)} %pack.4), channel_id=1, source_target_pairs={{0,2},{1,3},{2,4},{3,5},{4,6},{5,7},{6,8},{7,9},{8,10},{9,11},{10,... | collective-permute-start | bytes 2359304 | tf_op jit(solution)/shard_map/ppermute | solution.py:32
  12.6 1.3 %collective-permute-start.9 = (bf16[512,768]{1,0:T(8,128)(2,1)}, bf16[512,768]{1,0:T(8,128)(2,1)S(1)}, u32[]{:S(2)}, u32[]{:S(2)}) collective-permute-start(bf16[512,768]{1,0:T(8,128)(2,1)} %pack.4), channel_id=1, source_target_pairs={{0,1},{2,3},{4,5},{6,7},{8,9},{10,11},{12,13},{14,15},{16,17},{18,... | collective-permute-start | bytes 2359304 | tf_op jit(solution)/shard_map/ppermute | solution.py:40
  14.0 1.8 %pack.5 = bf16[512,512]{1,0:T(8,128)(2,1)} custom-call(bf16[256,2048]{1,0:T(8,128)(2,1)} %k_ref.5, bf16[256,2048]{1,0:T(8,128)(2,1)} %v_ref.5), custom_call_target="tpu_custom_call" | custom-call | tf_op jit(solution)/shard_map/pack/pallas_call | solution.py:270
  15.8 3.3 %collective-permute-start.10 = (bf16[512,512]{1,0:T(8,128)(2,1)}, bf16[512,512]{1,0:T(8,128)(2,1)}, u32[]{:S(2)}, u32[]{:S(2)}) collective-permute-start(bf16[512,512]{1,0:T(8,128)(2,1)} %pack.5), channel_id=1, source_target_pairs={{0,2},{1,3},{2,4},{3,5},{4,6},{5,7},{6,8},{7,9},{8,10},{9,11},{10,... | collective-permute-start | bytes 1572872 | tf_op jit(solution)/shard_map/ppermute | solution.py:32
  19.2 5.4 %collective-permute-done.6 = bf16[512,768]{1,0:T(8,128)(2,1)S(1)} collective-permute-done((bf16[512,768]{1,0:T(8,128)(2,1)S(1)}, bf16[512,768]{1,0:T(8,128)(2,1)S(1)}, u32[]{:S(2)}, u32[]{:S(2)}) %collective-permute-start.6) | collective-permute-done | bytes 786464 | tf_op jit(solution)/shard_map/ppermute | solution.py:32
  24.6 2.1 %collective-permute-start.11 = (bf16[512,512]{1,0:T(8,128)(2,1)}, bf16[512,512]{1,0:T(8,128)(2,1)}, u32[]{:S(2)}, u32[]{:S(2)}) collective-permute-start(bf16[512,512]{1,0:T(8,128)(2,1)} %pack.5), channel_id=1, source_target_pairs={{0,1},{2,3},{4,5},{6,7},{8,9},{10,11},{12,13},{14,15},{16,17},{18,... | collective-permute-start | bytes 1572872 | tf_op jit(solution)/shard_map/ppermute | solution.py:40
  26.6 0.0 copy-done.5
  26.7 0.0 collective-permute-done.7
  26.7 0.0 copy-done.4
  26.7 0.0 copy-done
  26.7 0.0 copy-done.1
  26.7 0.0 copy-done.3
  26.7 17.3 %conditional.3 = (bf16[256,4096]{1,0:T(8,128)(2,1)S(1)}, bf16[512,768]{1,0:T(8,128)(2,1)}, bf16[512,768]{1,0:T(8,128)(2,1)S(1)}, bf16[512,768]{1,0:T(8,128)(2,1)}) conditional(s32[]{:T(128)} %bitcast, () %tuple.32, (bf16[512,768]{1,0:T(8,128)(2,1)S(1)}, s32[8]{0:T(128)S(1)}, bf16[256,4096]{1,0:T(8,128)(2,1)S(1)}, bf16[256,4096]{1,0:T(8,128)(2,1)S(1)}, ...), branch_computations={%region_0.0_spmd, %region_1.0_spmd} | conditional | flops 2 | bytes 6291570 | solution.py:429
  26.8 1.3 %collective-permute-start = (bf16[512,768]{1,0:T(8,128)(2,1)S(1)}, bf16[512,768]{1,0:T(8,128)(2,1)S(1)}, u32[]{:S(2)}, u32[]{:S(2)}) collective-permute-start(bf16[512,768]{1,0:T(8,128)(2,1)S(1)} %get-tuple-element.53.refs_4_.refs_5_), channel_id=1, source_target_pairs={{1,0},{3,2},{5,4},{7,6},{9,8},{11,10},{13,12},{15,14},{17,16},{19,... | collective-permute-start | bytes 2359304 | tf_op jit(solution)/shard_map/cond/branch_1_fun/ppermute | solution.py:44
  28.1 2.9 %collective-permute-done.refs_0_.refs_1_ = bf16[512,768]{1,0:T(8,128)(2,1)S(1)} collective-permute-done((bf16[512,768]{1,0:T(8,128)(2,1)S(1)}, bf16[512,768]{1,0:T(8,128)(2,1)S(1)}, u32[]{:S(2)}, u32[]{:S(2)}) %collective-permute-start) | collective-permute-done | bytes 786464 | tf_op jit(solution)/shard_map/cond/branch_1_fun/ppermute | solution.py:44
  30.9 8.6 %attend.3 = (bf16[256,4096]{1,0:T(8,128)(2,1)S(1)}, bf16[512,768]{1,0:T(8,128)(2,1)S(1)}, bf16[512,768]{1,0:T(8,128)(2,1)S(1)}, bf16[512,768]{1,0:T(8,128)(2,1)S(1)}) custom-call(s32[8]{0:T(128)S(1)} %get-tuple-element.48.starts_ref, bf16[256,4096]{1,0:T(8,128)(2,1)S(1)} %get-tuple-element.49.q_ref, bf16[256,4096]{1,0:T(8,128)(2,1)S(1)} %get-tuple-element.50.g_ref, ...), custom_call_target="tpu_custom_call" | custom-call | flops 1 | bytes 1 | tf_op jit(solution)/shard_map/cond/branch_1_fun/attend/pallas_call | solution.py:234
  39.5 0.2 collective-permute-start.1
  39.7 2.3 %collective-permute-done.1.back_ref = bf16[512,768]{1,0:T(8,128)(2,1)} collective-permute-done((bf16[512,768]{1,0:T(8,128)(2,1)S(1)}, bf16[512,768]{1,0:T(8,128)(2,1)}, u32[]{:S(2)}, u32[]{:S(2)}) %collective-permute-start.1) | collective-permute-done | bytes 786464 | tf_op jit(solution)/shard_map/cond/branch_1_fun/ppermute | solution.py:36
  42.0 2.1 %merge.2 = bf16[512,768]{1,0:T(8,128)(2,1)} custom-call(bf16[512,768]{1,0:T(8,128)(2,1)S(1)} %get-tuple-element.56.far_ref, bf16[512,768]{1,0:T(8,128)(2,1)} %collective-permute-done.1.back_ref), custom_call_target="tpu_custom_call" | custom-call | flops 1 | bytes 1 | tf_op jit(solution)/shard_map/cond/branch_1_fun/merge/pallas_call | solution.py:305
  44.1 3.3 %collective-permute-start.14 = (bf16[512,768]{1,0:T(8,128)(2,1)}, bf16[512,768]{1,0:T(8,128)(2,1)}, u32[]{:S(2)}, u32[]{:S(2)}) collective-permute-start(bf16[512,768]{1,0:T(8,128)(2,1)} %get-tuple-element.114), channel_id=1, source_target_pairs={{2,0},{3,1},{4,2},{5,3},{6,4},{7,5},{8,6},{9,7},{10,8},{11,9},{12,... | collective-permute-start | bytes 2359304 | tf_op jit(solution)/shard_map/ppermute | solution.py:32
  47.4 0.0 collective-permute-done.8
  47.4 0.0 collective-permute-done.9
  47.4 17.8 %conditional.4 = (bf16[256,4096]{1,0:T(8,128)(2,1)S(1)}, bf16[512,768]{1,0:T(8,128)(2,1)}, bf16[512,768]{1,0:T(8,128)(2,1)S(1)}, bf16[512,768]{1,0:T(8,128)(2,1)}) conditional(s32[]{:T(128)} %bitcast, bf16[256,4096]{1,0:T(8,128)(2,1)S(1)} %get-tuple-element.105, (bf16[512,768]{1,0:T(8,128)(2,1)S(1)}, s32[8]{0:T(128)S(1)}, ...), branch_computations={%region_2.0_spmd, %region_3.0_spmd} | conditional | flops 2 | bytes 6291570 | solution.py:429
  47.4 1.3 %collective-permute-start.2 = (bf16[512,768]{1,0:T(8,128)(2,1)S(1)}, bf16[512,768]{1,0:T(8,128)(2,1)S(1)}, u32[]{:S(2)}, u32[]{:S(2)}) collective-permute-start(bf16[512,768]{1,0:T(8,128)(2,1)S(1)} %get-tuple-element.64.refs_4_.refs_5_), channel_id=1, source_target_pairs={{1,0},{3,2},{5,4},{7,6},{9,8},{11,10},{13,12},{15,14},{17,16},{19,... | collective-permute-start | bytes 2359304 | tf_op jit(solution)/shard_map/cond/branch_1_fun/ppermute | solution.py:44
  48.7 2.9 %collective-permute-done.2.refs_0_.refs_1_ = bf16[512,768]{1,0:T(8,128)(2,1)S(1)} collective-permute-done((bf16[512,768]{1,0:T(8,128)(2,1)S(1)}, bf16[512,768]{1,0:T(8,128)(2,1)S(1)}, u32[]{:S(2)}, u32[]{:S(2)}) %collective-permute-start.2) | collective-permute-done | bytes 786464 | tf_op jit(solution)/shard_map/cond/branch_1_fun/ppermute | solution.py:44
  51.6 9.0 %attend.4 = (bf16[256,4096]{1,0:T(8,128)(2,1)S(1)}, bf16[512,768]{1,0:T(8,128)(2,1)S(1)}, bf16[512,768]{1,0:T(8,128)(2,1)S(1)}, bf16[512,768]{1,0:T(8,128)(2,1)S(1)}) custom-call(s32[8]{0:T(128)S(1)} %get-tuple-element.59.starts_ref, bf16[256,4096]{1,0:T(8,128)(2,1)} %get-tuple-element.60.q_ref, ...), custom_call_target="tpu_custom_call", output_to_operand_aliasing={{0}: (11, {})} | custom-call | flops 1 | bytes 1 | tf_op jit(solution)/shard_map/cond/branch_1_fun/attend/pallas_call | solution.py:234
  60.6 0.2 collective-permute-start.3
  60.8 2.3 %collective-permute-done.3.back_ref = bf16[512,768]{1,0:T(8,128)(2,1)} collective-permute-done((bf16[512,768]{1,0:T(8,128)(2,1)S(1)}, bf16[512,768]{1,0:T(8,128)(2,1)}, u32[]{:S(2)}, u32[]{:S(2)}) %collective-permute-start.3) | collective-permute-done | bytes 786464 | tf_op jit(solution)/shard_map/cond/branch_1_fun/ppermute | solution.py:36
  63.1 2.1 %merge.3 = bf16[512,768]{1,0:T(8,128)(2,1)} custom-call(bf16[512,768]{1,0:T(8,128)(2,1)S(1)} %get-tuple-element.68.far_ref, bf16[512,768]{1,0:T(8,128)(2,1)} %collective-permute-done.3.back_ref), custom_call_target="tpu_custom_call" | custom-call | flops 1 | bytes 1 | tf_op jit(solution)/shard_map/cond/branch_1_fun/merge/pallas_call | solution.py:305
  65.2 2.5 %collective-permute-start.13 = (bf16[512,768]{1,0:T(8,128)(2,1)}, bf16[512,768]{1,0:T(8,128)(2,1)S(1)}, u32[]{:S(2)}, u32[]{:S(2)}) collective-permute-start(bf16[512,768]{1,0:T(8,128)(2,1)} %get-tuple-element.111), channel_id=1, source_target_pairs={{2,0},{3,1},{4,2},{5,3},{6,4},{7,5},{8,6},{9,7},{10,8},{11,9},{12,... | collective-permute-start | bytes 2359304 | tf_op jit(solution)/shard_map/ppermute | solution.py:32
  67.7 0.8 collective-permute-done.10
  68.5 0.0 collective-permute-done.11
  68.5 12.7 %conditional.5 = (bf16[256,4096]{1,0:T(8,128)(2,1)S(1)}, bf16[512,512]{1,0:T(8,128)(2,1)S(1)}, bf16[512,512]{1,0:T(8,128)(2,1)S(1)}) conditional(s32[]{:T(128)} %bitcast, bf16[256,4096]{1,0:T(8,128)(2,1)S(1)} %get-tuple-element.106, (bf16[512,512]{1,0:T(8,128)(2,1)}, s32[8]{0:T(128)S(1)}, bf16[256,4096]{1,0:T(8,128)(2,1)}, ...), branch_computations={%region_4.0_spmd, %region_5.0_spmd} | conditional | flops 2 | bytes 4194410 | solution.py:429
  68.5 1.3 %collective-permute-start.4 = (bf16[512,512]{1,0:T(8,128)(2,1)}, bf16[512,512]{1,0:T(8,128)(2,1)S(1)}, u32[]{:S(2)}, u32[]{:S(2)}) collective-permute-start(bf16[512,512]{1,0:T(8,128)(2,1)} %get-tuple-element.76.refs_4_.refs_5_), channel_id=1, source_target_pairs={{1,0},{3,2},{5,4},{7,6},{9,8},{11,10},{13,12},{15,14},{17,16},{19,... | collective-permute-start | bytes 1572872 | tf_op jit(solution)/shard_map/cond/branch_1_fun/ppermute | solution.py:44
  69.8 2.7 %collective-permute-done.4.refs_0_.refs_1_ = bf16[512,512]{1,0:T(8,128)(2,1)S(1)} collective-permute-done((bf16[512,512]{1,0:T(8,128)(2,1)}, bf16[512,512]{1,0:T(8,128)(2,1)S(1)}, u32[]{:S(2)}, u32[]{:S(2)}) %collective-permute-start.4) | collective-permute-done | bytes 524320 | tf_op jit(solution)/shard_map/cond/branch_1_fun/ppermute | solution.py:44
  72.5 6.5 %attend.5 = (bf16[256,4096]{1,0:T(8,128)(2,1)S(1)}, bf16[512,512]{1,0:T(8,128)(2,1)S(1)}, bf16[512,512]{1,0:T(8,128)(2,1)S(1)}, bf16[512,512]{1,0:T(8,128)(2,1)S(1)}) custom-call(s32[8]{0:T(128)S(1)} %get-tuple-element.71.starts_ref, bf16[256,4096]{1,0:T(8,128)(2,1)} %get-tuple-element.72.q_ref, ...), custom_call_target="tpu_custom_call", output_to_operand_aliasing={{0}: (11, {})} | custom-call | flops 1 | bytes 1 | tf_op jit(solution)/shard_map/cond/branch_1_fun/attend/pallas_call | solution.py:234
  79.0 0.2 collective-permute-start.5
  79.2 1.8 %collective-permute-done.5.back_ref = bf16[512,512]{1,0:T(8,128)(2,1)S(1)} collective-permute-done((bf16[512,512]{1,0:T(8,128)(2,1)S(1)}, bf16[512,512]{1,0:T(8,128)(2,1)S(1)}, u32[]{:S(2)}, u32[]{:S(2)}) %collective-permute-start.5) | collective-permute-done | bytes 524320 | tf_op jit(solution)/shard_map/cond/branch_1_fun/ppermute | solution.py:36
  81.0 0.2 merge_kept.1
  81.1 0.0 copy-start.2
  81.1 3.5 %collective-permute-start.12 = (bf16[512,512]{1,0:T(8,128)(2,1)S(1)}, bf16[512,512]{1,0:T(8,128)(2,1)S(1)}, u32[]{:S(2)}, u32[]{:S(2)}) collective-permute-start(bf16[512,512]{1,0:T(8,128)(2,1)S(1)} %get-tuple-element.109), channel_id=1, source_target_pairs={{2,0},{3,1},{4,2},{5,3},{6,4},{7,5},{8,6},{9,7},{10,8},{11,9},{12,... | collective-permute-start | bytes 1572872 | tf_op jit(solution)/shard_map/ppermute | solution.py:32
  84.6 0.0 collective-permute-done.14.home_ref
  84.6 2.5 %finish.3 = (bf16[256,2048]{1,0:T(8,128)(2,1)}, bf16[256,2048]{1,0:T(8,128)(2,1)}) custom-call(bf16[512,768]{1,0:T(8,128)(2,1)S(1)} %get-tuple-element.113.own_ref, bf16[512,768]{1,0:T(8,128)(2,1)} %collective-permute-done.14.home_ref, bf16[512,768]{1,0:T(8,128)(2,1)} %get-tuple-element.115.refs_0_), custom_call_target="tpu_custom_call" | custom-call | flops 1 | bytes 1 | tf_op jit(solution)/shard_map/finish/pallas_call | solution.py:374
  87.1 2.3 %collective-permute-done.13.home_ref = bf16[512,768]{1,0:T(8,128)(2,1)S(1)} collective-permute-done((bf16[512,768]{1,0:T(8,128)(2,1)}, bf16[512,768]{1,0:T(8,128)(2,1)S(1)}, u32[]{:S(2)}, u32[]{:S(2)}) %collective-permute-start.13) | collective-permute-done | bytes 786464 | tf_op jit(solution)/shard_map/ppermute | solution.py:32
  89.4 2.2 %finish.4 = (bf16[256,2048]{1,0:T(8,128)(2,1)}, bf16[256,2048]{1,0:T(8,128)(2,1)}) custom-call(bf16[512,768]{1,0:T(8,128)(2,1)S(1)} %get-tuple-element.110.own_ref, bf16[512,768]{1,0:T(8,128)(2,1)S(1)} %collective-permute-done.13.home_ref, bf16[512,768]{1,0:T(8,128)(2,1)} %get-tuple-element.112.refs_0_, ...), custom_call_target="tpu_custom_call", output_to_operand_aliasing={{0}: (3, {}), {1}: (4, {})} | custom-call | flops 1 | bytes 1 | tf_op jit(solution)/shard_map/finish/pallas_call | solution.py:374
  91.7 0.0 copy-done.2
  91.7 8.3 %collective-permute-done.12.home_ref = bf16[512,512]{1,0:T(8,128)(2,1)S(1)} collective-permute-done((bf16[512,512]{1,0:T(8,128)(2,1)S(1)}, bf16[512,512]{1,0:T(8,128)(2,1)S(1)}, u32[]{:S(2)}, u32[]{:S(2)}) %collective-permute-start.12) | collective-permute-done | bytes 524320 | tf_op jit(solution)/shard_map/ppermute | solution.py:32
  100.0 0.9 finish.5
Async XLA Ops:
  0.6 26.1 %copy-start.4 = (bf16[256,4096]{1,0:T(8,128)(2,1)S(1)}, bf16[256,4096]{1,0:T(8,128)(2,1)}, u32[]{:S(2)}) copy-start(bf16[256,4096]{1,0:T(8,128)(2,1)} %param.14) | copy-start | bytes 6291460
  1.9 24.7 %copy-start.5 = (s32[8]{0:T(128)S(1)}, s32[8]{0:T(128)}, u32[]{:S(2)}) copy-start(s32[8]{0:T(128)} %param.15) | copy-start | bytes 100
  1.9 24.8 %copy-start = (bf16[256,2048]{1,0:T(8,128)(2,1)S(1)}, bf16[256,2048]{1,0:T(8,128)(2,1)}, u32[]{:S(2)}) copy-start(bf16[256,2048]{1,0:T(8,128)(2,1)} %k_ref.5) | copy-start | bytes 3145732
  2.0 24.8 %copy-start.1 = (bf16[256,2048]{1,0:T(8,128)(2,1)S(1)}, bf16[256,2048]{1,0:T(8,128)(2,1)}, u32[]{:S(2)}) copy-start(bf16[256,2048]{1,0:T(8,128)(2,1)} %v_ref.5) | copy-start | bytes 3145732
  2.0 24.8 %copy-start.3 = (bf16[256,4096]{1,0:T(8,128)(2,1)S(1)}, bf16[256,4096]{1,0:T(8,128)(2,1)}, u32[]{:S(2)}) copy-start(bf16[256,4096]{1,0:T(8,128)(2,1)} %param.11) | copy-start | bytes 6291460
  2.0 22.6 %collective-permute-start.6 = (bf16[512,768]{1,0:T(8,128)(2,1)S(1)}, bf16[512,768]{1,0:T(8,128)(2,1)S(1)}, u32[]{:S(2)}, u32[]{:S(2)}) collective-permute-start(bf16[512,768]{1,0:T(8,128)(2,1)S(1)} %pack.3), channel_id=1, source_target_pairs={{0,2},{1,3},{2,4},{3,5},{4,6},{5,7},{6,8},{7,9},{8,10},{9,11},{10,... | collective-permute-start | bytes 2359304 | tf_op jit(solution)/shard_map/ppermute | solution.py:32
  5.7 21.0 %collective-permute-start.7 = (bf16[512,768]{1,0:T(8,128)(2,1)S(1)}, bf16[512,768]{1,0:T(8,128)(2,1)S(1)}, u32[]{:S(2)}, u32[]{:S(2)}) collective-permute-start(bf16[512,768]{1,0:T(8,128)(2,1)S(1)} %pack.3), channel_id=1, source_target_pairs={{0,1},{2,3},{4,5},{6,7},{8,9},{10,11},{12,13},{14,15},{16,17},{18,... | collective-permute-start | bytes 2359304 | tf_op jit(solution)/shard_map/ppermute | solution.py:40
  9.2 38.2 %collective-permute-start.8 = (bf16[512,768]{1,0:T(8,128)(2,1)}, bf16[512,768]{1,0:T(8,128)(2,1)S(1)}, u32[]{:S(2)}, u32[]{:S(2)}) collective-permute-start(bf16[512,768]{1,0:T(8,128)(2,1)} %pack.4), channel_id=1, source_target_pairs={{0,2},{1,3},{2,4},{3,5},{4,6},{5,7},{6,8},{7,9},{8,10},{9,11},{10,... | collective-permute-start | bytes 2359304 | tf_op jit(solution)/shard_map/ppermute | solution.py:32
  12.6 34.8 %collective-permute-start.9 = (bf16[512,768]{1,0:T(8,128)(2,1)}, bf16[512,768]{1,0:T(8,128)(2,1)S(1)}, u32[]{:S(2)}, u32[]{:S(2)}) collective-permute-start(bf16[512,768]{1,0:T(8,128)(2,1)} %pack.4), channel_id=1, source_target_pairs={{0,1},{2,3},{4,5},{6,7},{8,9},{10,11},{12,13},{14,15},{16,17},{18,... | collective-permute-start | bytes 2359304 | tf_op jit(solution)/shard_map/ppermute | solution.py:40
  15.8 52.6 %collective-permute-start.10 = (bf16[512,512]{1,0:T(8,128)(2,1)}, bf16[512,512]{1,0:T(8,128)(2,1)}, u32[]{:S(2)}, u32[]{:S(2)}) collective-permute-start(bf16[512,512]{1,0:T(8,128)(2,1)} %pack.5), channel_id=1, source_target_pairs={{0,2},{1,3},{2,4},{3,5},{4,6},{5,7},{6,8},{7,9},{8,10},{9,11},{10,... | collective-permute-start | bytes 1572872 | tf_op jit(solution)/shard_map/ppermute | solution.py:32
  24.6 43.9 %collective-permute-start.11 = (bf16[512,512]{1,0:T(8,128)(2,1)}, bf16[512,512]{1,0:T(8,128)(2,1)}, u32[]{:S(2)}, u32[]{:S(2)}) collective-permute-start(bf16[512,512]{1,0:T(8,128)(2,1)} %pack.5), channel_id=1, source_target_pairs={{0,1},{2,3},{4,5},{6,7},{8,9},{10,11},{12,13},{14,15},{16,17},{18,... | collective-permute-start | bytes 1572872 | tf_op jit(solution)/shard_map/ppermute | solution.py:40
  26.8 4.2 %collective-permute-start = (bf16[512,768]{1,0:T(8,128)(2,1)S(1)}, bf16[512,768]{1,0:T(8,128)(2,1)S(1)}, u32[]{:S(2)}, u32[]{:S(2)}) collective-permute-start(bf16[512,768]{1,0:T(8,128)(2,1)S(1)} %get-tuple-element.53.refs_4_.refs_5_), channel_id=1, source_target_pairs={{1,0},{3,2},{5,4},{7,6},{9,8},{11,10},{13,12},{15,14},{17,16},{19,... | collective-permute-start | bytes 2359304 | tf_op jit(solution)/shard_map/cond/branch_1_fun/ppermute | solution.py:44
  39.5 2.5 %collective-permute-start.1 = (bf16[512,768]{1,0:T(8,128)(2,1)S(1)}, bf16[512,768]{1,0:T(8,128)(2,1)}, u32[]{:S(2)}, u32[]{:S(2)}) collective-permute-start(bf16[512,768]{1,0:T(8,128)(2,1)S(1)} %get-tuple-element.57), channel_id=1, source_target_pairs={{0,1},{1,0},{2,3},{3,2},{4,5},{5,4},{6,7},{7,6},{8,9},{9,8},{10,11... | collective-permute-start | bytes 2359304 | tf_op jit(solution)/shard_map/cond/branch_1_fun/ppermute | solution.py:36
  44.1 40.5 %collective-permute-start.14 = (bf16[512,768]{1,0:T(8,128)(2,1)}, bf16[512,768]{1,0:T(8,128)(2,1)}, u32[]{:S(2)}, u32[]{:S(2)}) collective-permute-start(bf16[512,768]{1,0:T(8,128)(2,1)} %get-tuple-element.114), channel_id=1, source_target_pairs={{2,0},{3,1},{4,2},{5,3},{6,4},{7,5},{8,6},{9,7},{10,8},{11,9},{12,... | collective-permute-start | bytes 2359304 | tf_op jit(solution)/shard_map/ppermute | solution.py:32
  47.4 4.2 %collective-permute-start.2 = (bf16[512,768]{1,0:T(8,128)(2,1)S(1)}, bf16[512,768]{1,0:T(8,128)(2,1)S(1)}, u32[]{:S(2)}, u32[]{:S(2)}) collective-permute-start(bf16[512,768]{1,0:T(8,128)(2,1)S(1)} %get-tuple-element.64.refs_4_.refs_5_), channel_id=1, source_target_pairs={{1,0},{3,2},{5,4},{7,6},{9,8},{11,10},{13,12},{15,14},{17,16},{19,... | collective-permute-start | bytes 2359304 | tf_op jit(solution)/shard_map/cond/branch_1_fun/ppermute | solution.py:44
  60.6 2.5 %collective-permute-start.3 = (bf16[512,768]{1,0:T(8,128)(2,1)S(1)}, bf16[512,768]{1,0:T(8,128)(2,1)}, u32[]{:S(2)}, u32[]{:S(2)}) collective-permute-start(bf16[512,768]{1,0:T(8,128)(2,1)S(1)} %get-tuple-element.69), channel_id=1, source_target_pairs={{0,1},{1,0},{2,3},{3,2},{4,5},{5,4},{6,7},{7,6},{8,9},{9,8},{10,11... | collective-permute-start | bytes 2359304 | tf_op jit(solution)/shard_map/cond/branch_1_fun/ppermute | solution.py:36
  65.2 24.3 %collective-permute-start.13 = (bf16[512,768]{1,0:T(8,128)(2,1)}, bf16[512,768]{1,0:T(8,128)(2,1)S(1)}, u32[]{:S(2)}, u32[]{:S(2)}) collective-permute-start(bf16[512,768]{1,0:T(8,128)(2,1)} %get-tuple-element.111), channel_id=1, source_target_pairs={{2,0},{3,1},{4,2},{5,3},{6,4},{7,5},{8,6},{9,7},{10,8},{11,9},{12,... | collective-permute-start | bytes 2359304 | tf_op jit(solution)/shard_map/ppermute | solution.py:32
  68.5 4.0 %collective-permute-start.4 = (bf16[512,512]{1,0:T(8,128)(2,1)}, bf16[512,512]{1,0:T(8,128)(2,1)S(1)}, u32[]{:S(2)}, u32[]{:S(2)}) collective-permute-start(bf16[512,512]{1,0:T(8,128)(2,1)} %get-tuple-element.76.refs_4_.refs_5_), channel_id=1, source_target_pairs={{1,0},{3,2},{5,4},{7,6},{9,8},{11,10},{13,12},{15,14},{17,16},{19,... | collective-permute-start | bytes 1572872 | tf_op jit(solution)/shard_map/cond/branch_1_fun/ppermute | solution.py:44
  79.0 2.0 %collective-permute-start.5 = (bf16[512,512]{1,0:T(8,128)(2,1)S(1)}, bf16[512,512]{1,0:T(8,128)(2,1)S(1)}, u32[]{:S(2)}, u32[]{:S(2)}) collective-permute-start(bf16[512,512]{1,0:T(8,128)(2,1)S(1)} %get-tuple-element.82), channel_id=1, source_target_pairs={{0,1},{1,0},{2,3},{3,2},{4,5},{5,4},{6,7},{7,6},{8,9},{9,8},{10,11... | collective-permute-start | bytes 1572872 | tf_op jit(solution)/shard_map/cond/branch_1_fun/ppermute | solution.py:36
  81.1 10.6 %copy-start.2 = (bf16[256,4096]{1,0:T(8,128)(2,1)}, bf16[256,4096]{1,0:T(8,128)(2,1)S(1)}, u32[]{:S(2)}) copy-start(bf16[256,4096]{1,0:T(8,128)(2,1)S(1)} %get-tuple-element.102) | copy-start | bytes 6291460
  81.1 18.9 %collective-permute-start.12 = (bf16[512,512]{1,0:T(8,128)(2,1)S(1)}, bf16[512,512]{1,0:T(8,128)(2,1)S(1)}, u32[]{:S(2)}, u32[]{:S(2)}) collective-permute-start(bf16[512,512]{1,0:T(8,128)(2,1)S(1)} %get-tuple-element.109), channel_id=1, source_target_pairs={{2,0},{3,1},{4,2},{5,3},{6,4},{7,5},{8,6},{9,7},{10,8},{11,9},{12,... | collective-permute-start | bytes 1572872 | tf_op jit(solution)/shard_map/ppermute | solution.py:32

commit v7 on v6

--- a/solution.py
+++ b/solution.py
@@ -13,6 +13,7 @@
 AXES = ("seq", "head")
 GROUPS = (6, 6, 4)
 STEP = 2
+LAST_STEP = 4
 UNIT = 128
 STRIP = 32
 VMEM_LIMIT = 16 * 1024 * 1024
@@ -207,11 +208,12 @@
     rows, width = keys.shape
     back = 1 + len(others)
     group = queries.shape[1] // width
-    step = STEP * HEAD_SIZE
+    each = LAST_STEP if heads == LAST_STEP else STEP
+    step = each * HEAD_SIZE
     unit = min(UNIT, rows)
 
     def part(height, wide, offset, row=0):
-        return pl.BlockSpec((height, wide), lambda i: (row, offset // STEP + i))
+        return pl.BlockSpec((height, wide), lambda i: (row, offset // each + i))
 
     wide = part(rows, group * step, first)
     narrow = part(rows, step, first)
@@ -233,7 +235,7 @@
     outs = [queries.shape] + outs
     return pl.pallas_call(
         functools.partial(kernel, rows, back, group, len(near) == 2, pieces),
-        grid=(heads // STEP,),
+        grid=(heads // each,),
         in_specs=in_specs,
         out_specs=[wide] + [part(shape[0], step, 0) for shape in outs[1:]],
         out_shape=[jax.ShapeDtypeStruct(outs[0], jnp.bfloat16)]
@@ -414,7 +416,7 @@
             start, heads, dquery, 1,
         )
         returned = swapped(to_near, devices)
-        if start == starts[-1]:
+        if start > 0:
             return dquery, *merge_kept(to_far, own, returned)
         return dquery, merge(to_far, returned), own, returned
 
@@ -423,7 +425,7 @@
     for start, heads, received, own_near in zip(starts, GROUPS, far, early):
         def skip(received, own_near, dquery):
             zeros = jnp.zeros_like(received)
-            parts = [zeros] * (2 if start == starts[-1] else 3)
+            parts = [zeros] * (2 if start > 0 else 3)
             return jnp.zeros_like(queries) if dquery is None else dquery, *parts
 
         dquery, send, own, *returned = lax.cond(

time: 101 us -> 100 us (0.990)
  Pallas kernels: 39.1 us -> 36.6 us
  waiting for transfers between devices: 31.7 us -> 33.7 us
    ppermute x6, waiting for transfers between devices: 16.9 us -> 19.2 us  [shifted(): return lax.ppermute(x, AXES, pairs)]
    pallas_call x2 -> x1, Pallas kernels: 4.18 us -> 2.06 us  [merge(): pl.pallas_call(merge_kernel, in_specs=[whole] * 2, out_specs=whole, out_s...]
    pallas_call x3, Pallas kernels: 5.56 us -> 4.32 us  [finish(): pl.pallas_call(functools.partial(finish_kernel, first, terms), in_specs=i...]
    ppermute x6, starting transfers between devices: 19.7 us -> 18.6 us  [shifted(): return lax.ppermute(x, AXES, pairs)]
    pallas_call x1 -> x2, Pallas kernels: 0.15 us -> 1.29 us  [merge_kept(): pl.pallas_call(merge_kept_kernel, in_specs=[whole] * 3, out_specs=[whole]...]
  transfers between devices with their start and end apart: 15 -> 15, of which waited for: 10 -> 10; matrix products, arithmetic and copies ran while one was open for 0% -> 0% of each run, Pallas kernels for 37% -> 35%
where the time goes in v7:
time: 100 us; the launch traced here: 99.8 us
  Pallas kernels  36.6 us (37%)
  waiting for transfers between devices  33.7 us (34%)
  starting transfers between devices  28.1 us (28%)
  between operations  1.09 us (1%)
    pallas_call x3, Pallas kernels, attend(): pl.pallas_call(functools.partial(kernel, rows, back, group, len(near) ==...  23.8 us
    ppermute x6, waiting for transfers between devices, shifted(): return lax.ppermute(x, AXES, pairs)  19.2 us
    ppermute x6, starting transfers between devices, shifted(): return lax.ppermute(x, AXES, pairs)  18.6 us
    ppermute x3, waiting for transfers between devices, to_even(): return lax.ppermute(x, AXES, [(i + 1, i) for i in range(0, devices, 2)])  8.29 us
    ppermute x3, waiting for transfers between devices, swapped(): return lax.ppermute(x, AXES, [(i, i ^ 1) for i in range(devices)])  6.2 us
    pallas_call x3, Pallas kernels, pack(): pl.pallas_call(functools.partial(pack_kernel, first), in_specs=[pl.BlockS...  5.14 us
    ppermute x3, starting transfers between devices, to_odd(): return lax.ppermute(x, AXES, [(i, i + 1) for i in range(0, devices, 2)])  4.93 us
    pallas_call x3, Pallas kernels, finish(): pl.pallas_call(functools.partial(finish_kernel, first, terms), in_specs=i...  4.32 us
  transfers between devices with their start and end apart: 15, of which 10 were waited for; matrix products, arithmetic and copies ran while one was open for 0% of the time, Pallas kernels for 35%

profile of v7, /device:TPU:14, one launch (start us, length us, event | category | flops | bytes accessed | tf_op | source)
XLA Modules:
  0.0 99.8 jit_solution(9774879522999744895)
XLA Ops:
  0.6 0.0 copy-start.4
  0.6 1.3 %pack.3 = bf16[512,768]{1,0:T(8,128)(2,1)S(1)} custom-call(bf16[256,2048]{1,0:T(8,128)(2,1)} %k_ref.5, bf16[256,2048]{1,0:T(8,128)(2,1)} %v_ref.5), custom_call_target="tpu_custom_call" | custom-call | tf_op jit(solution)/shard_map/pack/pallas_call | solution.py:272
  1.9 0.0 copy-start.5
  1.9 0.0 copy-start
  2.0 0.0 copy-start.1
  2.0 0.0 copy-start.3
  2.0 3.7 %collective-permute-start.6 = (bf16[512,768]{1,0:T(8,128)(2,1)S(1)}, bf16[512,768]{1,0:T(8,128)(2,1)S(1)}, u32[]{:S(2)}, u32[]{:S(2)}) collective-permute-start(bf16[512,768]{1,0:T(8,128)(2,1)S(1)} %pack.3), channel_id=1, source_target_pairs={{0,2},{1,3},{2,4},{3,5},{4,6},{5,7},{6,8},{7,9},{8,10},{9,11},{10,... | collective-permute-start | bytes 2359304 | tf_op jit(solution)/shard_map/ppermute | solution.py:33
  5.7 1.5 %collective-permute-start.7 = (bf16[512,768]{1,0:T(8,128)(2,1)S(1)}, bf16[512,768]{1,0:T(8,128)(2,1)S(1)}, u32[]{:S(2)}, u32[]{:S(2)}) collective-permute-start(bf16[512,768]{1,0:T(8,128)(2,1)S(1)} %pack.3), channel_id=1, source_target_pairs={{0,1},{2,3},{4,5},{6,7},{8,9},{10,11},{12,13},{14,15},{16,17},{18,... | collective-permute-start | bytes 2359304 | tf_op jit(solution)/shard_map/ppermute | solution.py:41
  7.2 2.0 %pack.4 = bf16[512,768]{1,0:T(8,128)(2,1)} custom-call(bf16[256,2048]{1,0:T(8,128)(2,1)} %k_ref.5, bf16[256,2048]{1,0:T(8,128)(2,1)} %v_ref.5), custom_call_target="tpu_custom_call" | custom-call | tf_op jit(solution)/shard_map/pack/pallas_call | solution.py:272
  9.2 3.4 %collective-permute-start.8 = (bf16[512,768]{1,0:T(8,128)(2,1)}, bf16[512,768]{1,0:T(8,128)(2,1)S(1)}, u32[]{:S(2)}, u32[]{:S(2)}) collective-permute-start(bf16[512,768]{1,0:T(8,128)(2,1)} %pack.4), channel_id=1, source_target_pairs={{0,2},{1,3},{2,4},{3,5},{4,6},{5,7},{6,8},{7,9},{8,10},{9,11},{10,... | collective-permute-start | bytes 2359304 | tf_op jit(solution)/shard_map/ppermute | solution.py:33
  12.6 1.3 %collective-permute-start.9 = (bf16[512,768]{1,0:T(8,128)(2,1)}, bf16[512,768]{1,0:T(8,128)(2,1)S(1)}, u32[]{:S(2)}, u32[]{:S(2)}) collective-permute-start(bf16[512,768]{1,0:T(8,128)(2,1)} %pack.4), channel_id=1, source_target_pairs={{0,1},{2,3},{4,5},{6,7},{8,9},{10,11},{12,13},{14,15},{16,17},{18,... | collective-permute-start | bytes 2359304 | tf_op jit(solution)/shard_map/ppermute | solution.py:41
  14.0 1.8 %pack.5 = bf16[512,512]{1,0:T(8,128)(2,1)} custom-call(bf16[256,2048]{1,0:T(8,128)(2,1)} %k_ref.5, bf16[256,2048]{1,0:T(8,128)(2,1)} %v_ref.5), custom_call_target="tpu_custom_call" | custom-call | tf_op jit(solution)/shard_map/pack/pallas_call | solution.py:272
  15.8 3.3 %collective-permute-start.10 = (bf16[512,512]{1,0:T(8,128)(2,1)}, bf16[512,512]{1,0:T(8,128)(2,1)}, u32[]{:S(2)}, u32[]{:S(2)}) collective-permute-start(bf16[512,512]{1,0:T(8,128)(2,1)} %pack.5), channel_id=1, source_target_pairs={{0,2},{1,3},{2,4},{3,5},{4,6},{5,7},{6,8},{7,9},{8,10},{9,11},{10,... | collective-permute-start | bytes 1572872 | tf_op jit(solution)/shard_map/ppermute | solution.py:33
  19.2 5.4 %collective-permute-done.6 = bf16[512,768]{1,0:T(8,128)(2,1)S(1)} collective-permute-done((bf16[512,768]{1,0:T(8,128)(2,1)S(1)}, bf16[512,768]{1,0:T(8,128)(2,1)S(1)}, u32[]{:S(2)}, u32[]{:S(2)}) %collective-permute-start.6) | collective-permute-done | bytes 786464 | tf_op jit(solution)/shard_map/ppermute | solution.py:33
  24.6 2.1 %collective-permute-start.11 = (bf16[512,512]{1,0:T(8,128)(2,1)}, bf16[512,512]{1,0:T(8,128)(2,1)}, u32[]{:S(2)}, u32[]{:S(2)}) collective-permute-start(bf16[512,512]{1,0:T(8,128)(2,1)} %pack.5), channel_id=1, source_target_pairs={{0,1},{2,3},{4,5},{6,7},{8,9},{10,11},{12,13},{14,15},{16,17},{18,... | collective-permute-start | bytes 1572872 | tf_op jit(solution)/shard_map/ppermute | solution.py:41
  26.7 0.0 copy-done.5
  26.7 0.0 collective-permute-done.7
  26.7 0.0 copy-done.4
  26.7 0.0 copy-done
  26.7 0.0 copy-done.1
  26.7 0.0 copy-done.3
  26.7 17.3 %conditional.3 = (bf16[256,4096]{1,0:T(8,128)(2,1)S(1)}, bf16[512,768]{1,0:T(8,128)(2,1)}, bf16[512,768]{1,0:T(8,128)(2,1)S(1)}, bf16[512,768]{1,0:T(8,128)(2,1)}) conditional(s32[]{:T(128)} %bitcast, () %tuple.32, (bf16[512,768]{1,0:T(8,128)(2,1)S(1)}, s32[8]{0:T(128)S(1)}, bf16[256,4096]{1,0:T(8,128)(2,1)S(1)}, bf16[256,4096]{1,0:T(8,128)(2,1)S(1)}, ...), branch_computations={%region_0.0_spmd, %region_1.0_spmd} | conditional | flops 2 | bytes 6291570 | solution.py:431
  26.8 1.3 %collective-permute-start = (bf16[512,768]{1,0:T(8,128)(2,1)S(1)}, bf16[512,768]{1,0:T(8,128)(2,1)S(1)}, u32[]{:S(2)}, u32[]{:S(2)}) collective-permute-start(bf16[512,768]{1,0:T(8,128)(2,1)S(1)} %get-tuple-element.53.refs_4_.refs_5_), channel_id=1, source_target_pairs={{1,0},{3,2},{5,4},{7,6},{9,8},{11,10},{13,12},{15,14},{17,16},{19,... | collective-permute-start | bytes 2359304 | tf_op jit(solution)/shard_map/cond/branch_1_fun/ppermute | solution.py:45
  28.1 2.9 %collective-permute-done.refs_0_.refs_1_ = bf16[512,768]{1,0:T(8,128)(2,1)S(1)} collective-permute-done((bf16[512,768]{1,0:T(8,128)(2,1)S(1)}, bf16[512,768]{1,0:T(8,128)(2,1)S(1)}, u32[]{:S(2)}, u32[]{:S(2)}) %collective-permute-start) | collective-permute-done | bytes 786464 | tf_op jit(solution)/shard_map/cond/branch_1_fun/ppermute | solution.py:45
  30.9 8.6 %attend.3 = (bf16[256,4096]{1,0:T(8,128)(2,1)S(1)}, bf16[512,768]{1,0:T(8,128)(2,1)S(1)}, bf16[512,768]{1,0:T(8,128)(2,1)S(1)}, bf16[512,768]{1,0:T(8,128)(2,1)S(1)}) custom-call(s32[8]{0:T(128)S(1)} %get-tuple-element.48.starts_ref, bf16[256,4096]{1,0:T(8,128)(2,1)S(1)} %get-tuple-element.49.q_ref, bf16[256,4096]{1,0:T(8,128)(2,1)S(1)} %get-tuple-element.50.g_ref, ...), custom_call_target="tpu_custom_call" | custom-call | flops 1 | bytes 1 | tf_op jit(solution)/shard_map/cond/branch_1_fun/attend/pallas_call | solution.py:236
  39.5 0.2 collective-permute-start.1
  39.7 2.3 %collective-permute-done.1.back_ref = bf16[512,768]{1,0:T(8,128)(2,1)} collective-permute-done((bf16[512,768]{1,0:T(8,128)(2,1)S(1)}, bf16[512,768]{1,0:T(8,128)(2,1)}, u32[]{:S(2)}, u32[]{:S(2)}) %collective-permute-start.1) | collective-permute-done | bytes 786464 | tf_op jit(solution)/shard_map/cond/branch_1_fun/ppermute | solution.py:37
  42.0 2.1 %merge.1 = bf16[512,768]{1,0:T(8,128)(2,1)} custom-call(bf16[512,768]{1,0:T(8,128)(2,1)S(1)} %get-tuple-element.56.far_ref, bf16[512,768]{1,0:T(8,128)(2,1)} %collective-permute-done.1.back_ref), custom_call_target="tpu_custom_call" | custom-call | flops 1 | bytes 1 | tf_op jit(solution)/shard_map/cond/branch_1_fun/merge/pallas_call | solution.py:307
  44.1 3.3 %collective-permute-start.14 = (bf16[512,768]{1,0:T(8,128)(2,1)}, bf16[512,768]{1,0:T(8,128)(2,1)}, u32[]{:S(2)}, u32[]{:S(2)}) collective-permute-start(bf16[512,768]{1,0:T(8,128)(2,1)} %get-tuple-element.114), channel_id=1, source_target_pairs={{2,0},{3,1},{4,2},{5,3},{6,4},{7,5},{8,6},{9,7},{10,8},{11,9},{12,... | collective-permute-start | bytes 2359304 | tf_op jit(solution)/shard_map/ppermute | solution.py:33
  47.4 0.0 collective-permute-done.8
  47.4 0.0 collective-permute-done.9
  47.4 16.6 %conditional.4 = (bf16[256,4096]{1,0:T(8,128)(2,1)S(1)}, bf16[512,768]{1,0:T(8,128)(2,1)}, bf16[512,768]{1,0:T(8,128)(2,1)S(1)}) conditional(s32[]{:T(128)} %bitcast, bf16[256,4096]{1,0:T(8,128)(2,1)S(1)} %get-tuple-element.106, (bf16[512,768]{1,0:T(8,128)(2,1)S(1)}, s32[8]{0:T(128)S(1)}, bf16[256,4096]{1,0:T(8,128)(2,1)}, ...), branch_computations={%region_2.0_spmd, %region_3.0_spmd} | conditional | flops 2 | bytes 6291562 | solution.py:431
  47.4 1.3 %collective-permute-start.2 = (bf16[512,768]{1,0:T(8,128)(2,1)S(1)}, bf16[512,768]{1,0:T(8,128)(2,1)S(1)}, u32[]{:S(2)}, u32[]{:S(2)}) collective-permute-start(bf16[512,768]{1,0:T(8,128)(2,1)S(1)} %get-tuple-element.64.refs_4_.refs_5_), channel_id=1, source_target_pairs={{1,0},{3,2},{5,4},{7,6},{9,8},{11,10},{13,12},{15,14},{17,16},{19,... | collective-permute-start | bytes 2359304 | tf_op jit(solution)/shard_map/cond/branch_1_fun/ppermute | solution.py:45
  48.7 2.9 %collective-permute-done.2.refs_0_.refs_1_ = bf16[512,768]{1,0:T(8,128)(2,1)S(1)} collective-permute-done((bf16[512,768]{1,0:T(8,128)(2,1)S(1)}, bf16[512,768]{1,0:T(8,128)(2,1)S(1)}, u32[]{:S(2)}, u32[]{:S(2)}) %collective-permute-start.2) | collective-permute-done | bytes 786464 | tf_op jit(solution)/shard_map/cond/branch_1_fun/ppermute | solution.py:45
  51.6 8.9 %attend.4 = (bf16[256,4096]{1,0:T(8,128)(2,1)S(1)}, bf16[512,768]{1,0:T(8,128)(2,1)S(1)}, bf16[512,768]{1,0:T(8,128)(2,1)S(1)}, bf16[512,768]{1,0:T(8,128)(2,1)S(1)}) custom-call(s32[8]{0:T(128)S(1)} %get-tuple-element.59.starts_ref, bf16[256,4096]{1,0:T(8,128)(2,1)} %get-tuple-element.60.q_ref, ...), custom_call_target="tpu_custom_call", output_to_operand_aliasing={{0}: (11, {})} | custom-call | flops 1 | bytes 1 | tf_op jit(solution)/shard_map/cond/branch_1_fun/attend/pallas_call | solution.py:236
  60.5 0.2 collective-permute-start.3
  60.7 2.1 %collective-permute-done.3.back_ref = bf16[512,768]{1,0:T(8,128)(2,1)S(1)} collective-permute-done((bf16[512,768]{1,0:T(8,128)(2,1)S(1)}, bf16[512,768]{1,0:T(8,128)(2,1)S(1)}, u32[]{:S(2)}, u32[]{:S(2)}) %collective-permute-start.3) | collective-permute-done | bytes 786464 | tf_op jit(solution)/shard_map/cond/branch_1_fun/ppermute | solution.py:37
  62.9 1.1 %merge_kept.2 = (bf16[512,768]{1,0:T(8,128)(2,1)}, bf16[512,768]{1,0:T(8,128)(2,1)S(1)}) custom-call(bf16[512,768]{1,0:T(8,128)(2,1)S(1)} %get-tuple-element.68.far_ref, bf16[512,768]{1,0:T(8,128)(2,1)S(1)} %get-tuple-element.69.own_ref, bf16[512,768]{1,0:T(8,128)(2,1)S(1)} %collective-permute-done.3.back_ref), custom_call_target="tpu_custom_call" | custom-call | flops 1 | bytes 1 | tf_op jit(solution)/shard_map/cond/branch_1_fun/merge_kept/pallas_call | solution.py:336
  64.0 2.5 %collective-permute-start.13 = (bf16[512,768]{1,0:T(8,128)(2,1)}, bf16[512,768]{1,0:T(8,128)(2,1)S(1)}, u32[]{:S(2)}, u32[]{:S(2)}) collective-permute-start(bf16[512,768]{1,0:T(8,128)(2,1)} %get-tuple-element.112), channel_id=1, source_target_pairs={{2,0},{3,1},{4,2},{5,3},{6,4},{7,5},{8,6},{9,7},{10,8},{11,9},{12,... | collective-permute-start | bytes 2359304 | tf_op jit(solution)/shard_map/ppermute | solution.py:33
  66.5 1.9 %collective-permute-done.10 = bf16[512,512]{1,0:T(8,128)(2,1)} collective-permute-done((bf16[512,512]{1,0:T(8,128)(2,1)}, bf16[512,512]{1,0:T(8,128)(2,1)}, u32[]{:S(2)}, u32[]{:S(2)}) %collective-permute-start.10) | collective-permute-done | bytes 524320 | tf_op jit(solution)/shard_map/ppermute | solution.py:33
  68.5 0.0 collective-permute-done.11
  68.5 12.6 %conditional.5 = (bf16[256,4096]{1,0:T(8,128)(2,1)S(1)}, bf16[512,512]{1,0:T(8,128)(2,1)S(1)}, bf16[512,512]{1,0:T(8,128)(2,1)S(1)}) conditional(s32[]{:T(128)} %bitcast, bf16[256,4096]{1,0:T(8,128)(2,1)S(1)} %get-tuple-element.107, (bf16[512,512]{1,0:T(8,128)(2,1)}, s32[8]{0:T(128)S(1)}, bf16[256,4096]{1,0:T(8,128)(2,1)}, ...), branch_computations={%region_4.0_spmd, %region_5.0_spmd} | conditional | flops 2 | bytes 4194410 | solution.py:431
  68.5 1.5 %collective-permute-start.4 = (bf16[512,512]{1,0:T(8,128)(2,1)}, bf16[512,512]{1,0:T(8,128)(2,1)S(1)}, u32[]{:S(2)}, u32[]{:S(2)}) collective-permute-start(bf16[512,512]{1,0:T(8,128)(2,1)} %get-tuple-element.78.refs_4_.refs_5_), channel_id=1, source_target_pairs={{1,0},{3,2},{5,4},{7,6},{9,8},{11,10},{13,12},{15,14},{17,16},{19,... | collective-permute-start | bytes 1572872 | tf_op jit(solution)/shard_map/cond/branch_1_fun/ppermute | solution.py:45
  69.9 2.5 %collective-permute-done.4.refs_0_.refs_1_ = bf16[512,512]{1,0:T(8,128)(2,1)S(1)} collective-permute-done((bf16[512,512]{1,0:T(8,128)(2,1)}, bf16[512,512]{1,0:T(8,128)(2,1)S(1)}, u32[]{:S(2)}, u32[]{:S(2)}) %collective-permute-start.4) | collective-permute-done | bytes 524320 | tf_op jit(solution)/shard_map/cond/branch_1_fun/ppermute | solution.py:45
  72.5 6.3 %attend.5 = (bf16[256,4096]{1,0:T(8,128)(2,1)S(1)}, bf16[512,512]{1,0:T(8,128)(2,1)S(1)}, bf16[512,512]{1,0:T(8,128)(2,1)S(1)}, bf16[512,512]{1,0:T(8,128)(2,1)S(1)}) custom-call(s32[8]{0:T(128)S(1)} %get-tuple-element.73.starts_ref, bf16[256,4096]{1,0:T(8,128)(2,1)} %get-tuple-element.74.q_ref, ...), custom_call_target="tpu_custom_call", output_to_operand_aliasing={{0}: (11, {})} | custom-call | flops 1 | bytes 1 | tf_op jit(solution)/shard_map/cond/branch_1_fun/attend/pallas_call | solution.py:236
  78.8 0.2 collective-permute-start.5
  79.0 1.8 %collective-permute-done.5.back_ref = bf16[512,512]{1,0:T(8,128)(2,1)S(1)} collective-permute-done((bf16[512,512]{1,0:T(8,128)(2,1)S(1)}, bf16[512,512]{1,0:T(8,128)(2,1)S(1)}, u32[]{:S(2)}, u32[]{:S(2)}) %collective-permute-start.5) | collective-permute-done | bytes 524320 | tf_op jit(solution)/shard_map/cond/branch_1_fun/ppermute | solution.py:37
  80.7 0.2 merge_kept.3
  81.1 0.0 copy-start.2
  81.1 2.3 %collective-permute-start.12 = (bf16[512,512]{1,0:T(8,128)(2,1)S(1)}, bf16[512,512]{1,0:T(8,128)(2,1)S(1)}, u32[]{:S(2)}, u32[]{:S(2)}) collective-permute-start(bf16[512,512]{1,0:T(8,128)(2,1)S(1)} %get-tuple-element.110), channel_id=1, source_target_pairs={{2,0},{3,1},{4,2},{5,3},{6,4},{7,5},{8,6},{9,7},{10,8},{11,9},{12,... | collective-permute-start | bytes 1572872 | tf_op jit(solution)/shard_map/ppermute | solution.py:33
  83.5 0.0 collective-permute-done.14.home_ref
  83.5 2.5 %finish.3 = (bf16[256,2048]{1,0:T(8,128)(2,1)}, bf16[256,2048]{1,0:T(8,128)(2,1)}) custom-call(bf16[512,768]{1,0:T(8,128)(2,1)S(1)} %get-tuple-element.113.own_ref, bf16[512,768]{1,0:T(8,128)(2,1)} %collective-permute-done.14.home_ref, bf16[512,768]{1,0:T(8,128)(2,1)} %get-tuple-element.115.refs_0_), custom_call_target="tpu_custom_call" | custom-call | flops 1 | bytes 1 | tf_op jit(solution)/shard_map/finish/pallas_call | solution.py:376
  86.0 1.5 %collective-permute-done.13.home_ref = bf16[512,768]{1,0:T(8,128)(2,1)S(1)} collective-permute-done((bf16[512,768]{1,0:T(8,128)(2,1)}, bf16[512,768]{1,0:T(8,128)(2,1)S(1)}, u32[]{:S(2)}, u32[]{:S(2)}) %collective-permute-start.13) | collective-permute-done | bytes 786464 | tf_op jit(solution)/shard_map/ppermute | solution.py:33
  87.5 1.0 finish.4
  88.5 0.0 copy-done.2
  88.5 10.3 %collective-permute-done.12.home_ref = bf16[512,512]{1,0:T(8,128)(2,1)S(1)} collective-permute-done((bf16[512,512]{1,0:T(8,128)(2,1)S(1)}, bf16[512,512]{1,0:T(8,128)(2,1)S(1)}, u32[]{:S(2)}, u32[]{:S(2)}) %collective-permute-start.12) | collective-permute-done | bytes 524320 | tf_op jit(solution)/shard_map/ppermute | solution.py:33
  98.8 0.9 finish.5
Async XLA Ops:
  0.6 26.1 %copy-start.4 = (bf16[256,4096]{1,0:T(8,128)(2,1)S(1)}, bf16[256,4096]{1,0:T(8,128)(2,1)}, u32[]{:S(2)}) copy-start(bf16[256,4096]{1,0:T(8,128)(2,1)} %param.14) | copy-start | bytes 6291460
  1.9 24.7 %copy-start.5 = (s32[8]{0:T(128)S(1)}, s32[8]{0:T(128)}, u32[]{:S(2)}) copy-start(s32[8]{0:T(128)} %param.15) | copy-start | bytes 100
  1.9 24.8 %copy-start = (bf16[256,2048]{1,0:T(8,128)(2,1)S(1)}, bf16[256,2048]{1,0:T(8,128)(2,1)}, u32[]{:S(2)}) copy-start(bf16[256,2048]{1,0:T(8,128)(2,1)} %k_ref.5) | copy-start | bytes 3145732
  2.0 24.8 %copy-start.1 = (bf16[256,2048]{1,0:T(8,128)(2,1)S(1)}, bf16[256,2048]{1,0:T(8,128)(2,1)}, u32[]{:S(2)}) copy-start(bf16[256,2048]{1,0:T(8,128)(2,1)} %v_ref.5) | copy-start | bytes 3145732
  2.0 24.8 %copy-start.3 = (bf16[256,4096]{1,0:T(8,128)(2,1)S(1)}, bf16[256,4096]{1,0:T(8,128)(2,1)}, u32[]{:S(2)}) copy-start(bf16[256,4096]{1,0:T(8,128)(2,1)} %param.11) | copy-start | bytes 6291460
  2.0 22.6 %collective-permute-start.6 = (bf16[512,768]{1,0:T(8,128)(2,1)S(1)}, bf16[512,768]{1,0:T(8,128)(2,1)S(1)}, u32[]{:S(2)}, u32[]{:S(2)}) collective-permute-start(bf16[512,768]{1,0:T(8,128)(2,1)S(1)} %pack.3), channel_id=1, source_target_pairs={{0,2},{1,3},{2,4},{3,5},{4,6},{5,7},{6,8},{7,9},{8,10},{9,11},{10,... | collective-permute-start | bytes 2359304 | tf_op jit(solution)/shard_map/ppermute | solution.py:33
  5.7 21.0 %collective-permute-start.7 = (bf16[512,768]{1,0:T(8,128)(2,1)S(1)}, bf16[512,768]{1,0:T(8,128)(2,1)S(1)}, u32[]{:S(2)}, u32[]{:S(2)}) collective-permute-start(bf16[512,768]{1,0:T(8,128)(2,1)S(1)} %pack.3), channel_id=1, source_target_pairs={{0,1},{2,3},{4,5},{6,7},{8,9},{10,11},{12,13},{14,15},{16,17},{18,... | collective-permute-start | bytes 2359304 | tf_op jit(solution)/shard_map/ppermute | solution.py:41
  9.2 38.2 %collective-permute-start.8 = (bf16[512,768]{1,0:T(8,128)(2,1)}, bf16[512,768]{1,0:T(8,128)(2,1)S(1)}, u32[]{:S(2)}, u32[]{:S(2)}) collective-permute-start(bf16[512,768]{1,0:T(8,128)(2,1)} %pack.4), channel_id=1, source_target_pairs={{0,2},{1,3},{2,4},{3,5},{4,6},{5,7},{6,8},{7,9},{8,10},{9,11},{10,... | collective-permute-start | bytes 2359304 | tf_op jit(solution)/shard_map/ppermute | solution.py:33
  12.6 34.8 %collective-permute-start.9 = (bf16[512,768]{1,0:T(8,128)(2,1)}, bf16[512,768]{1,0:T(8,128)(2,1)S(1)}, u32[]{:S(2)}, u32[]{:S(2)}) collective-permute-start(bf16[512,768]{1,0:T(8,128)(2,1)} %pack.4), channel_id=1, source_target_pairs={{0,1},{2,3},{4,5},{6,7},{8,9},{10,11},{12,13},{14,15},{16,17},{18,... | collective-permute-start | bytes 2359304 | tf_op jit(solution)/shard_map/ppermute | solution.py:41
  15.8 52.6 %collective-permute-start.10 = (bf16[512,512]{1,0:T(8,128)(2,1)}, bf16[512,512]{1,0:T(8,128)(2,1)}, u32[]{:S(2)}, u32[]{:S(2)}) collective-permute-start(bf16[512,512]{1,0:T(8,128)(2,1)} %pack.5), channel_id=1, source_target_pairs={{0,2},{1,3},{2,4},{3,5},{4,6},{5,7},{6,8},{7,9},{8,10},{9,11},{10,... | collective-permute-start | bytes 1572872 | tf_op jit(solution)/shard_map/ppermute | solution.py:33
  24.6 43.9 %collective-permute-start.11 = (bf16[512,512]{1,0:T(8,128)(2,1)}, bf16[512,512]{1,0:T(8,128)(2,1)}, u32[]{:S(2)}, u32[]{:S(2)}) collective-permute-start(bf16[512,512]{1,0:T(8,128)(2,1)} %pack.5), channel_id=1, source_target_pairs={{0,1},{2,3},{4,5},{6,7},{8,9},{10,11},{12,13},{14,15},{16,17},{18,... | collective-permute-start | bytes 1572872 | tf_op jit(solution)/shard_map/ppermute | solution.py:41
  26.8 4.2 %collective-permute-start = (bf16[512,768]{1,0:T(8,128)(2,1)S(1)}, bf16[512,768]{1,0:T(8,128)(2,1)S(1)}, u32[]{:S(2)}, u32[]{:S(2)}) collective-permute-start(bf16[512,768]{1,0:T(8,128)(2,1)S(1)} %get-tuple-element.53.refs_4_.refs_5_), channel_id=1, source_target_pairs={{1,0},{3,2},{5,4},{7,6},{9,8},{11,10},{13,12},{15,14},{17,16},{19,... | collective-permute-start | bytes 2359304 | tf_op jit(solution)/shard_map/cond/branch_1_fun/ppermute | solution.py:45
  39.5 2.5 %collective-permute-start.1 = (bf16[512,768]{1,0:T(8,128)(2,1)S(1)}, bf16[512,768]{1,0:T(8,128)(2,1)}, u32[]{:S(2)}, u32[]{:S(2)}) collective-permute-start(bf16[512,768]{1,0:T(8,128)(2,1)S(1)} %get-tuple-element.57), channel_id=1, source_target_pairs={{0,1},{1,0},{2,3},{3,2},{4,5},{5,4},{6,7},{7,6},{8,9},{9,8},{10,11... | collective-permute-start | bytes 2359304 | tf_op jit(solution)/shard_map/cond/branch_1_fun/ppermute | solution.py:37
  44.1 39.4 %collective-permute-start.14 = (bf16[512,768]{1,0:T(8,128)(2,1)}, bf16[512,768]{1,0:T(8,128)(2,1)}, u32[]{:S(2)}, u32[]{:S(2)}) collective-permute-start(bf16[512,768]{1,0:T(8,128)(2,1)} %get-tuple-element.114), channel_id=1, source_target_pairs={{2,0},{3,1},{4,2},{5,3},{6,4},{7,5},{8,6},{9,7},{10,8},{11,9},{12,... | collective-permute-start | bytes 2359304 | tf_op jit(solution)/shard_map/ppermute | solution.py:33
  47.4 4.2 %collective-permute-start.2 = (bf16[512,768]{1,0:T(8,128)(2,1)S(1)}, bf16[512,768]{1,0:T(8,128)(2,1)S(1)}, u32[]{:S(2)}, u32[]{:S(2)}) collective-permute-start(bf16[512,768]{1,0:T(8,128)(2,1)S(1)} %get-tuple-element.64.refs_4_.refs_5_), channel_id=1, source_target_pairs={{1,0},{3,2},{5,4},{7,6},{9,8},{11,10},{13,12},{15,14},{17,16},{19,... | collective-permute-start | bytes 2359304 | tf_op jit(solution)/shard_map/cond/branch_1_fun/ppermute | solution.py:45
  60.5 2.4 %collective-permute-start.3 = (bf16[512,768]{1,0:T(8,128)(2,1)S(1)}, bf16[512,768]{1,0:T(8,128)(2,1)S(1)}, u32[]{:S(2)}, u32[]{:S(2)}) collective-permute-start(bf16[512,768]{1,0:T(8,128)(2,1)S(1)} %get-tuple-element.70), channel_id=1, source_target_pairs={{0,1},{1,0},{2,3},{3,2},{4,5},{5,4},{6,7},{7,6},{8,9},{9,8},{10,11... | collective-permute-start | bytes 2359304 | tf_op jit(solution)/shard_map/cond/branch_1_fun/ppermute | solution.py:37
  64.0 23.4 %collective-permute-start.13 = (bf16[512,768]{1,0:T(8,128)(2,1)}, bf16[512,768]{1,0:T(8,128)(2,1)S(1)}, u32[]{:S(2)}, u32[]{:S(2)}) collective-permute-start(bf16[512,768]{1,0:T(8,128)(2,1)} %get-tuple-element.112), channel_id=1, source_target_pairs={{2,0},{3,1},{4,2},{5,3},{6,4},{7,5},{8,6},{9,7},{10,8},{11,9},{12,... | collective-permute-start | bytes 2359304 | tf_op jit(solution)/shard_map/ppermute | solution.py:33
  68.5 4.0 %collective-permute-start.4 = (bf16[512,512]{1,0:T(8,128)(2,1)}, bf16[512,512]{1,0:T(8,128)(2,1)S(1)}, u32[]{:S(2)}, u32[]{:S(2)}) collective-permute-start(bf16[512,512]{1,0:T(8,128)(2,1)} %get-tuple-element.78.refs_4_.refs_5_), channel_id=1, source_target_pairs={{1,0},{3,2},{5,4},{7,6},{9,8},{11,10},{13,12},{15,14},{17,16},{19,... | collective-permute-start | bytes 1572872 | tf_op jit(solution)/shard_map/cond/branch_1_fun/ppermute | solution.py:45
  78.8 2.0 %collective-permute-start.5 = (bf16[512,512]{1,0:T(8,128)(2,1)S(1)}, bf16[512,512]{1,0:T(8,128)(2,1)S(1)}, u32[]{:S(2)}, u32[]{:S(2)}) collective-permute-start(bf16[512,512]{1,0:T(8,128)(2,1)S(1)} %get-tuple-element.84), channel_id=1, source_target_pairs={{0,1},{1,0},{2,3},{3,2},{4,5},{5,4},{6,7},{7,6},{8,9},{9,8},{10,11... | collective-permute-start | bytes 1572872 | tf_op jit(solution)/shard_map/cond/branch_1_fun/ppermute | solution.py:37
  81.1 7.3 %copy-start.2 = (bf16[256,4096]{1,0:T(8,128)(2,1)}, bf16[256,4096]{1,0:T(8,128)(2,1)S(1)}, u32[]{:S(2)}) copy-start(bf16[256,4096]{1,0:T(8,128)(2,1)S(1)} %get-tuple-element.103) | copy-start | bytes 6291460
  81.1 17.6 %collective-permute-start.12 = (bf16[512,512]{1,0:T(8,128)(2,1)S(1)}, bf16[512,512]{1,0:T(8,128)(2,1)S(1)}, u32[]{:S(2)}, u32[]{:S(2)}) collective-permute-start(bf16[512,512]{1,0:T(8,128)(2,1)S(1)} %get-tuple-element.110), channel_id=1, source_target_pairs={{2,0},{3,1},{4,2},{5,3},{6,4},{7,5},{8,6},{9,7},{10,8},{11,9},{12,... | collective-permute-start | bytes 1572872 | tf_op jit(solution)/shard_map/ppermute | solution.py:33
